TPU v7x, 32 devices: a whole 2x2x4 slice. The times are simulated.
32 devices in a mesh: wide: 8 (over z, y), narrow: 4 (over x, core).
Axes of the slice: x: 2, y: 2, z: 4, core: 2. Of those that a mesh axis runs over, the one named last changes fastest.
Arguments:
- captions: bfloat16 [64, 64, 768], P(('wide', 'narrow')), may hold values from -6 to 6
- images: bfloat16 [64, 576, 768], P('wide', 'narrow'), may hold values from -6 to 6
- lengths: int32 [64], P(('wide', 'narrow')), may hold values from 5 to 64, as said below
- out_grad: bfloat16 [64, 64, 768], P(('wide', 'narrow')), may hold values from -6 to 6
- self_proj: bfloat16 [768, 2304], P(('wide', 'narrow')), may hold values from -0.21875 to 0.21875
- self_output: bfloat16 [768, 768], P(('wide', 'narrow')), may hold values from -0.875 to 0.875
- cross_query: bfloat16 [768, 768], P(('wide', 'narrow')), may hold values from -0.21875 to 0.21875
- cross_memory: bfloat16 [768, 1536], P(('wide', 'narrow')), may hold values from -0.21875 to 0.21875
- cross_output: bfloat16 [768, 768], P(('wide', 'narrow')), may hold values from -3 to 3
- hidden_up: bfloat16 [768, 3072], P(('wide', 'narrow')), may hold values from -0.21875 to 0.21875
- hidden_down: bfloat16 [3072, 768], P(('wide', 'narrow')), may hold values from -0.109375 to 0.109375
- first_gain: bfloat16 [768], P(('wide', 'narrow')), may hold values from 0.099609375 to 1.8984375
- first_shift: bfloat16 [768], P(('wide', 'narrow')), may hold values from -3 to 3
- second_gain: bfloat16 [768], P(('wide', 'narrow')), may hold values from 0.099609375 to 1.8984375
- second_shift: bfloat16 [768], P(('wide', 'narrow')), may hold values from -3 to 3
- third_gain: bfloat16 [768], P(('wide', 'narrow')), may hold values from 0.099609375 to 1.8984375
- third_shift: bfloat16 [768], P(('wide', 'narrow')), may hold values from -3 to 3
Outputs:
- layer_out: bfloat16 [64, 64, 768], P(('wide', 'narrow'))
- input_grad: bfloat16 [64, 64, 768], P(('wide', 'narrow'))
- image_grad: bfloat16 [64, 576, 768], P('wide', 'narrow')
- self_proj_grad: float32 [768, 2304], P(('wide', 'narrow'))
- self_output_grad: float32 [768, 768], P(('wide', 'narrow'))
- cross_query_grad: float32 [768, 768], P(('wide', 'narrow'))
- cross_memory_grad: float32 [768, 1536], P(('wide', 'narrow'))
- cross_output_grad: float32 [768, 768], P(('wide', 'narrow'))
- hidden_up_grad: float32 [768, 3072], P(('wide', 'narrow'))
- hidden_down_grad: float32 [3072, 768], P(('wide', 'narrow'))
- first_gain_grad: float32 [768], P(('wide', 'narrow'))
- first_shift_grad: float32 [768], P(('wide', 'narrow'))
- second_gain_grad: float32 [768], P(('wide', 'narrow'))
- second_shift_grad: float32 [768], P(('wide', 'narrow'))
- third_gain_grad: float32 [768], P(('wide', 'narrow'))
- third_shift_grad: float32 [768], P(('wide', 'narrow'))
Inputs may be any that keep to these rules, and one draw needn't show every extreme that they name: Tokens at positions of lengths or later are padding; some caption has 64 real tokens.
All inputs are finite; a program needn't handle non-finite values.
Results may differ from a plain program's by a relative error of at most 0.025.
Values may be sent and summed in bfloat16 or wider, within the bound.
A program may use at most 128 MiB of HBM per device.

v0:
```python
import jax
import jax.numpy as jnp
from jax import lax
from jax.sharding import PartitionSpec as P

HEADS = 12


def layer_norm(value, gain, shift):
    center = jnp.mean(value, axis=-1, keepdims=True)
    centred = value - center
    spread = jnp.mean(centred * centred, axis=-1, keepdims=True)
    return centred * lax.rsqrt(spread + 1e-05) * gain + shift


def matmul(left, right):
    return jnp.dot(left, right, preferred_element_type=jnp.float32)


def backmul(left, right):
    return lax.dot_general(
        left, right, (((1,), (1,)), ((), ())), preferred_element_type=jnp.float32
    )


def weightmul(left, right):
    return lax.dot_general(
        left, right, (((0,), (0,)), ((), ())), preferred_element_type=jnp.float32
    )


def owned_columns(left, wide_count, narrow_count, narrow_place):
    rows, columns = left.shape
    share = columns // (wide_count * narrow_count)
    parts = left.reshape(rows, wide_count, narrow_count, share)
    picked = lax.dynamic_slice_in_dim(parts, narrow_place, 1, 2)
    return picked.reshape(rows, wide_count * share)


def per_device(
    captions,
    images,
    lengths,
    out_grad,
    self_proj,
    self_output,
    cross_query,
    cross_memory,
    cross_output,
    hidden_up,
    hidden_down,
    first_gain,
    first_shift,
    second_gain,
    second_shift,
    third_gain,
    third_shift,
):
    shards = (
        self_proj,
        self_output,
        cross_query,
        cross_memory,
        cross_output,
        hidden_up,
        hidden_down,
        first_gain,
        first_shift,
        second_gain,
        second_shift,
        third_gain,
        third_shift,
    )
    gathered = (
        lax.all_gather(shards[0], ("wide", "narrow"), axis=0, tiled=True),
        lax.all_gather(shards[1], ("wide", "narrow"), axis=0, tiled=True),
        lax.all_gather(shards[2], ("wide", "narrow"), axis=0, tiled=True),
        lax.all_gather(shards[3], ("wide", "narrow"), axis=0, tiled=True),
        lax.all_gather(shards[4], ("wide", "narrow"), axis=0, tiled=True),
        lax.all_gather(shards[5], ("wide", "narrow"), axis=0, tiled=True),
        lax.all_gather(shards[6], ("wide", "narrow"), axis=0, tiled=True),
        lax.all_gather(shards[7], ("wide", "narrow"), axis=0, tiled=True),
        lax.all_gather(shards[8], ("wide", "narrow"), axis=0, tiled=True),
        lax.all_gather(shards[9], ("wide", "narrow"), axis=0, tiled=True),
        lax.all_gather(shards[10], ("wide", "narrow"), axis=0, tiled=True),
        lax.all_gather(shards[11], ("wide", "narrow"), axis=0, tiled=True),
        lax.all_gather(shards[12], ("wide", "narrow"), axis=0, tiled=True),
    )
    weight_joint, weight_self, weight_query, weight_memory, weight_cross, weight_up, weight_down = (
        gathered[:7]
    )
    gain_one, shift_one, gain_two, shift_two, gain_three, shift_three = [
        item.astype(jnp.float32) for item in gathered[7:]
    ]
    count, seq_len, width = captions.shape
    head_size = width // HEADS
    scale = head_size ** (-0.5)
    tokens = count * seq_len
    inputs = captions.astype(jnp.float32).reshape(tokens, width)
    normed_one, pull_one = jax.vjp(layer_norm, inputs, gain_one, shift_one)
    low_one = normed_one.astype(jnp.bfloat16)
    joint = matmul(low_one, weight_joint).astype(jnp.bfloat16)
    queries = joint[:, :width].reshape(count, seq_len, HEADS, head_size)
    keys_self = joint[:, width : 2 * width].reshape(count, seq_len, HEADS, head_size)
    values_self = joint[:, 2 * width :].reshape(count, seq_len, HEADS, head_size)
    scores = (
        jnp.einsum("cqhe,ckhe->chqk", queries, keys_self, preferred_element_type=jnp.float32)
        * scale
    )
    places = jnp.arange(seq_len)
    allowed = (places[None, :] <= places[:, None])[None, None] & (
        places[None, None, None, :] < lengths[:, None, None, None]
    )
    scores = jnp.where(allowed, scores, -1000000000.0)
    probs = jax.nn.softmax(scores, axis=-1)
    probs_low = probs.astype(jnp.bfloat16)
    mixed = (
        jnp.einsum("chqk,ckhe->cqhe", probs_low, values_self, preferred_element_type=jnp.float32)
        .astype(jnp.bfloat16)
        .reshape(tokens, width)
    )
    first_res = inputs + matmul(mixed, weight_self)
    normed_two, pull_two = jax.vjp(layer_norm, first_res, gain_two, shift_two)
    low_two = normed_two.astype(jnp.bfloat16)
    cross_q = matmul(low_two, weight_query).astype(jnp.bfloat16).reshape(count, seq_len, width)
    all_queries = lax.all_gather(cross_q, "narrow", axis=0, tiled=True)
    groups = all_queries.shape[0]
    image_count = images.shape[1]
    image_rows = images.reshape(groups * image_count, width)
    memory = matmul(image_rows, weight_memory).astype(jnp.bfloat16)
    cross_k = memory[:, :width].reshape(groups, image_count, HEADS, head_size)
    cross_v = memory[:, width:].reshape(groups, image_count, HEADS, head_size)
    query_heads = all_queries.reshape(groups, seq_len, HEADS, head_size)
    cross_s = (
        jnp.einsum("cqhe,ckhe->chqk", query_heads, cross_k, preferred_element_type=jnp.float32)
        * scale
    )
    local_top = jnp.max(cross_s, axis=-1)
    global_top = lax.pmax(local_top, "narrow")
    expo = jnp.exp(cross_s - global_top[..., None])
    expo_low = expo.astype(jnp.bfloat16)
    numer_part = jnp.einsum(
        "chqk,ckhe->cqhe", expo_low, cross_v, preferred_element_type=jnp.float32
    ).reshape(groups, seq_len, width)
    total_part = jnp.sum(expo, axis=-1)
    numer, totals = (
        lax.psum_scatter(
            numer_part.astype(jnp.bfloat16), "narrow", scatter_dimension=0, tiled=True
        ).astype(jnp.float32),
        lax.psum_scatter(
            total_part.astype(jnp.bfloat16), "narrow", scatter_dimension=0, tiled=True
        ).astype(jnp.float32),
    )
    per_row = jnp.transpose(totals, (0, 2, 1))[..., None]
    attended_full = numer.reshape(count, seq_len, HEADS, head_size) / per_row
    attended = attended_full.astype(jnp.bfloat16).reshape(tokens, width)
    second_res = first_res + matmul(attended, weight_cross)
    normed_three, pull_three = jax.vjp(layer_norm, second_res, gain_three, shift_three)
    low_three = normed_three.astype(jnp.bfloat16)
    hidden = matmul(low_three, weight_up)
    activated_full, pull_gelu = jax.vjp(jax.nn.gelu, hidden)
    activated = activated_full.astype(jnp.bfloat16)
    layer_out = (
        (second_res + matmul(activated, weight_down))
        .astype(jnp.bfloat16)
        .reshape(count, seq_len, width)
    )
    grad_low = out_grad.reshape(tokens, width)
    grad_full = grad_low.astype(jnp.float32)
    hidden_grad = pull_gelu(backmul(grad_low, weight_down))[0].astype(jnp.bfloat16)
    res_three, gain_three_grad, shift_three_grad = pull_three(backmul(hidden_grad, weight_up))
    second_grad = grad_full + res_three
    cross_low = second_grad.astype(jnp.bfloat16)
    attended_grad = backmul(cross_low, weight_cross).reshape(count, seq_len, HEADS, head_size)
    numer_grad = (attended_grad / per_row).astype(jnp.bfloat16)
    total_grad = -jnp.sum(attended_grad * attended_full, axis=-1) / per_row[..., 0]
    all_numer, all_total = (
        lax.all_gather(
            numer_grad.astype(jnp.float32).reshape(count, seq_len, width).astype(jnp.bfloat16),
            "narrow",
            axis=0,
            tiled=True,
        ).astype(jnp.float32),
        lax.all_gather(total_grad.astype(jnp.bfloat16), "narrow", axis=0, tiled=True).astype(
            total_grad.dtype
        ),
    )
    numer_heads = all_numer.astype(jnp.bfloat16).reshape(groups, seq_len, HEADS, head_size)
    prob_cross = jnp.einsum(
        "cqhe,ckhe->chqk", numer_heads, cross_v, preferred_element_type=jnp.float32
    )
    score_grad = (expo * (prob_cross + jnp.transpose(all_total, (0, 2, 1))[..., None])).astype(
        jnp.bfloat16
    )
    query_part = (
        jnp.einsum("chqk,ckhe->cqhe", score_grad, cross_k, preferred_element_type=jnp.float32)
        * scale
    ).reshape(groups, seq_len, width)
    key_grad = (
        jnp.einsum("chqk,cqhe->ckhe", score_grad, query_heads, preferred_element_type=jnp.float32)
        * scale
    ).astype(jnp.bfloat16)
    value_grad = jnp.einsum(
        "chqk,cqhe->ckhe", expo_low, numer_heads, preferred_element_type=jnp.float32
    ).astype(jnp.bfloat16)
    query_grad = lax.psum_scatter(
        query_part.astype(jnp.bfloat16), "narrow", scatter_dimension=0, tiled=True
    ).reshape(tokens, width)
    memory_grad = jnp.concatenate(
        [
            key_grad.reshape(groups * image_count, width),
            value_grad.reshape(groups * image_count, width),
        ],
        axis=1,
    )
    image_grad = backmul(memory_grad, weight_memory).astype(jnp.bfloat16).reshape(images.shape)
    memory_wgrad = weightmul(image_rows, memory_grad)
    res_two, gain_two_grad, shift_two_grad = pull_two(backmul(query_grad, weight_query))
    first_grad = second_grad + res_two
    self_low = first_grad.astype(jnp.bfloat16)
    mixed_grad = (
        backmul(self_low, weight_self)
        .astype(jnp.bfloat16)
        .reshape(count, seq_len, HEADS, head_size)
    )
    prob_self = jnp.einsum(
        "cqhe,ckhe->chqk", mixed_grad, values_self, preferred_element_type=jnp.float32
    )
    self_score = (probs * (prob_self - jnp.sum(probs * prob_self, axis=-1, keepdims=True))).astype(
        jnp.bfloat16
    )
    query_self = (
        jnp.einsum("chqk,ckhe->cqhe", self_score, keys_self, preferred_element_type=jnp.float32)
        * scale
    )
    key_self = (
        jnp.einsum("chqk,cqhe->ckhe", self_score, queries, preferred_element_type=jnp.float32)
        * scale
    )
    value_self = jnp.einsum(
        "chqk,cqhe->ckhe", probs_low, mixed_grad, preferred_element_type=jnp.float32
    )
    joint_grad = jnp.concatenate(
        [
            query_self.reshape(tokens, width),
            key_self.reshape(tokens, width),
            value_self.reshape(tokens, width),
        ],
        axis=1,
    ).astype(jnp.bfloat16)
    res_one, gain_one_grad, shift_one_grad = pull_one(backmul(joint_grad, weight_joint))
    input_grad = (first_grad + res_one).astype(jnp.bfloat16).reshape(count, seq_len, width)
    group_rows = (
        lax.all_gather(low_one, "narrow", axis=0, tiled=True),
        lax.all_gather(joint_grad, "narrow", axis=0, tiled=True),
        lax.all_gather(mixed, "narrow", axis=0, tiled=True),
        lax.all_gather(self_low, "narrow", axis=0, tiled=True),
        lax.all_gather(low_two, "narrow", axis=0, tiled=True),
        lax.all_gather(query_grad, "narrow", axis=0, tiled=True),
        lax.all_gather(attended, "narrow", axis=0, tiled=True),
        lax.all_gather(cross_low, "narrow", axis=0, tiled=True),
        lax.all_gather(low_three, "narrow", axis=0, tiled=True),
        lax.all_gather(hidden_grad, "narrow", axis=0, tiled=True),
        lax.all_gather(activated, "narrow", axis=0, tiled=True),
        lax.all_gather(grad_low, "narrow", axis=0, tiled=True),
    )
    wide_count = lax.axis_size("wide")
    narrow_count = lax.axis_size("narrow")
    narrow_place = lax.axis_index("narrow")
    text_terms = tuple(
        (
            weightmul(
                owned_columns(group_rows[2 * item], wide_count, narrow_count, narrow_place),
                group_rows[2 * item + 1],
            )
            for item in range(6)
        )
    )
    text_summed = lax.psum_scatter(text_terms, "wide", scatter_dimension=0, tiled=True)
    terms = (
        memory_wgrad,
        gain_one_grad,
        shift_one_grad,
        gain_two_grad,
        shift_two_grad,
        gain_three_grad,
        shift_three_grad,
    )
    summed = (
        lax.psum_scatter(terms[0], ("wide", "narrow"), scatter_dimension=0, tiled=True),
        lax.psum_scatter(terms[1], ("wide", "narrow"), scatter_dimension=0, tiled=True),
        lax.psum_scatter(terms[2], ("wide", "narrow"), scatter_dimension=0, tiled=True),
        lax.psum_scatter(terms[3], ("wide", "narrow"), scatter_dimension=0, tiled=True),
        lax.psum_scatter(terms[4], ("wide", "narrow"), scatter_dimension=0, tiled=True),
        lax.psum_scatter(terms[5], ("wide", "narrow"), scatter_dimension=0, tiled=True),
        lax.psum_scatter(terms[6], ("wide", "narrow"), scatter_dimension=0, tiled=True),
    )
    return (
        layer_out,
        input_grad,
        image_grad,
        text_summed[0],
        text_summed[1],
        text_summed[2],
        summed[0],
        text_summed[3],
        text_summed[4],
        text_summed[5],
        summed[1],
        summed[2],
        summed[3],
        summed[4],
        summed[5],
        summed[6],
    )


def solution(mesh):
    in_specs = (
        P(("wide", "narrow"), None, None),
        P("wide", "narrow", None),
        P(("wide", "narrow")),
        P(("wide", "narrow"), None, None),
        P(("wide", "narrow"), None),
        P(("wide", "narrow"), None),
        P(("wide", "narrow"), None),
        P(("wide", "narrow"), None),
        P(("wide", "narrow"), None),
        P(("wide", "narrow"), None),
        P(("wide", "narrow"), None),
        P(("wide", "narrow")),
        P(("wide", "narrow")),
        P(("wide", "narrow")),
        P(("wide", "narrow")),
        P(("wide", "narrow")),
        P(("wide", "narrow")),
    )
    out_specs = (
        P(("wide", "narrow"), None, None),
        P(("wide", "narrow"), None, None),
        P("wide", "narrow", None),
        P(("wide", "narrow"), None),
        P(("wide", "narrow"), None),
        P(("wide", "narrow"), None),
        P(("wide", "narrow"), None),
        P(("wide", "narrow"), None),
        P(("wide", "narrow"), None),
        P(("wide", "narrow"), None),
        P(("wide", "narrow")),
        P(("wide", "narrow")),
        P(("wide", "narrow")),
        P(("wide", "narrow")),
        P(("wide", "narrow")),
        P(("wide", "narrow")),
    )
    return jax.shard_map(
        per_device, mesh=mesh, in_specs=in_specs, out_specs=out_specs, check_vma=False
    )
```

profile of v0, /device:TPU:1, one launch (start us, length us, event | category | flops | bytes accessed | tf_op | source)
XLA Modules:
  0.0 1218.4 jit_solution(9722246109001476237)
XLA Ops:
  17.4 41.7 %all-reduce.14 = (bf16[768]{0:T(1024)(128)(2,1)S(1)}, bf16[768]{0:T(1024)(128)(2,1)S(1)}, bf16[768]{0:T(1024)(128)(2,1)S(1)}, bf16[768]{0:T(1024)(128)(2,1)S(1)}...) all-reduce(bf16[768]{0:T(1024)(128)(2,1)S(1)} %dynamic-update-slice, ...), channel_id=1, replica_groups=mesh['wide'=8,'narrow'=4] {'wide','narrow'}, use_global_device_ids=true, to_apply=%add.1 | all-reduce | flops 4608 | bytes 18432
  103.2 29.4 %all-gather.11.cloned.1.call-done = bf16[768,2304]{1,0:T(8,128)(2,1)} async-done(((bf16[24,2304]{1,0:T(8,128)(2,1)}), bf16[768,2304]{1,0:T(8,128)(2,1)}) %all-gather.11.cloned.1.call-update) | async-done | bytes 3538960 | tf_op jit(solution)/shard_map/all_gather | solution.py:75
  146.4 42.1 %all-gather.13.cloned.1.call-done = bf16[768,768]{1,0:T(8,128)(2,1)} async-done(((bf16[24,768]{1,0:T(8,128)(2,1)}), bf16[768,768]{1,0:T(8,128)(2,1)}) %all-gather.13.cloned.1.call-update) | async-done | bytes 1179664 | tf_op jit(solution)/shard_map/all_gather | solution.py:76
  191.0 53.1 %all-gather.17.cloned.1.call-done = bf16[768,768]{1,0:T(8,128)(2,1)} async-done(((bf16[24,768]{1,0:T(8,128)(2,1)}), bf16[768,768]{1,0:T(8,128)(2,1)}) %all-gather.17.cloned.1.call-update) | async-done | bytes 1179664 | tf_op jit(solution)/shard_map/all_gather | solution.py:77
  245.8 9.2 all_gather.92
  262.6 10.6 pmax.7
  290.7 11.5 all-reduce.6
  309.3 53.8 %all-gather.19.cloned.1.call-done = bf16[768,768]{1,0:T(8,128)(2,1)} async-done(((bf16[24,768]{1,0:T(8,128)(2,1)}), bf16[768,768]{1,0:T(8,128)(2,1)}) %all-gather.19.cloned.1.call-update) | async-done | bytes 1179664 | tf_op jit(solution)/shard_map/all_gather | solution.py:79
  365.2 63.8 %all-gather.23.cloned.1.call-done = bf16[3072,768]{1,0:T(8,128)(2,1)} async-done(((bf16[96,768]{1,0:T(8,128)(2,1)}), bf16[3072,768]{1,0:T(8,128)(2,1)}) %all-gather.23.cloned.1.call-update) | async-done | bytes 4718608 | tf_op jit(solution)/shard_map/all_gather | solution.py:81
  434.3 60.6 %all-gather.21.cloned.1.call-done = bf16[768,3072]{1,0:T(8,128)(2,1)} async-done(((bf16[24,3072]{1,0:T(8,128)(2,1)}), bf16[768,3072]{1,0:T(8,128)(2,1)}) %all-gather.21.cloned.1.call-update) | async-done | bytes 4718608 | tf_op jit(solution)/shard_map/all_gather | solution.py:80
  512.5 9.3 all_gather.98
  544.8 21.7 %reduce-scatter.15.cloned.1.call-done = bf16[2,64,768]{2,1,0:T(8,128)(2,1)} async-done(((bf16[8,64,768]{2,1,0:T(8,128)(2,1)}), bf16[2,64,768]{2,1,0:T(8,128)(2,1)}) %reduce-scatter.15.cloned.1.call-update) | async-done | bytes 196624 | tf_op jit(solution)/shard_map/reduce_scatter | solution.py:206
  594.2 9.3 all_gather.106
  606.8 13.7 %all_gather.107 = bf16[512,768]{1,0:T(8,128)(2,1)S(1)} all-gather(bf16[128,768]{1,0:T(8,128)(2,1)} %copy-done.23), channel_id=1, replica_groups=mesh['wide'=8,'narrow'=4] {'narrow'}, dimensions={0}, use_global_device_ids=true | all-gather | bytes 983040 | tf_op jit(solution)/shard_map/all_gather | solution.py:261
  621.7 9.2 all_gather.104
  634.3 13.3 %all_gather.102 = bf16[512,768]{0,1:T(8,128)(2,1)S(1)} all-gather(bf16[128,768]{0,1:T(8,128)(2,1)S(1)} %copy-done.20), channel_id=1, replica_groups=mesh['wide'=8,'narrow'=4] {'narrow'}, dimensions={0}, use_global_device_ids=true | all-gather | bytes 983040 | tf_op jit(solution)/shard_map/all_gather | solution.py:256
  647.6 12.4 %all_gather.105 = bf16[512,768]{1,0:T(8,128)(2,1)S(1)} all-gather(bf16[128,768]{1,0:T(8,128)(2,1)} %bitcast.187), channel_id=1, replica_groups=mesh['wide'=8,'narrow'=4] {'narrow'}, dimensions={0}, use_global_device_ids=true | all-gather | bytes 983040 | tf_op jit(solution)/shard_map/all_gather | solution.py:259
  714.6 9.4 all_gather.100
  777.8 39.0 %all-reduce.13 = (f32[768]{0:T(1024)S(1)}, f32[768]{0:T(1024)S(1)}, f32[768]{0:T(1024)S(1)}, f32[768]{0:T(1024)S(1)}, f32[768]{0:T(1024)S(1)}, /*index=5*/f32[768]{0:T(1024)S(1)}) all-reduce(f32[768]{0:T(1024)S(1)} %get-tuple-element.116, ...), channel_id=12, replica_groups=mesh['wide'=8,'narrow'=4] {'wide','narrow'}, use_global_device_ids=true, to_apply=%region_30.31.clone | all-reduce | flops 4608 | bytes 36864
  821.3 62.5 %reduce-scatter.19.cloned.1.call-done = f32[24,768]{1,0:T(8,128)} async-done(((f32[192,768]{1,0:T(8,128)}), f32[24,768]{1,0:T(8,128)}) %reduce-scatter.19.cloned.1.call-update) | async-done | bytes 73744 | tf_op jit(solution)/shard_map/reduce_scatter | solution.py:279
  883.8 113.0 %reduce-scatter.29.cloned.1.call-done = f32[24,1536]{1,0:T(8,128)} async-done(((f32[768,1536]{1,0:T(8,128)}), f32[24,1536]{1,0:T(8,128)}) %reduce-scatter.29.cloned.1.call-update) | async-done | bytes 147472
  996.9 69.4 %reduce-scatter.17.cloned.1.call-done = f32[24,2304]{1,0:T(8,128)} async-done(((f32[192,2304]{1,0:T(8,128)}), f32[24,2304]{1,0:T(8,128)}) %reduce-scatter.17.cloned.1.call-update) | async-done | bytes 221200 | tf_op jit(solution)/shard_map/reduce_scatter | solution.py:279
  1066.3 72.5 %reduce-scatter.25.cloned.1.call-done = f32[24,3072]{1,0:T(8,128)} async-done(((f32[192,3072]{1,0:T(8,128)}), f32[24,3072]{1,0:T(8,128)}) %reduce-scatter.25.cloned.1.call-update) | async-done | bytes 294928 | tf_op jit(solution)/shard_map/reduce_scatter | solution.py:279
  1138.8 72.6 %reduce-scatter.27.cloned.1.call-done = f32[96,768]{1,0:T(8,128)} async-done(((f32[768,768]{1,0:T(8,128)}), f32[96,768]{1,0:T(8,128)}) %reduce-scatter.27.cloned.1.call-update) | async-done | bytes 294928 | tf_op jit(solution)/shard_map/reduce_scatter | solution.py:279
  (322 shorter events, 299.3 us)
Async XLA Ops:
  7.2 63.2 %all-gather.15.cloned.1.call-start = ((), (), s32[]{:S(2)}) async-start(), calls=%async_computation.11 | async-start | bytes 2433024 | tf_op jit(solution)/shard_map/all_gather | solution.py:78
  7.9 124.7 %all-gather.11.cloned.1.call-start = ((), (), s32[]{:S(2)}) async-start(), calls=%async_computation.9 | async-start | bytes 3649536 | tf_op jit(solution)/shard_map/all_gather | solution.py:75
  8.7 179.7 %all-gather.13.cloned.1.call-start = ((), (), s32[]{:S(2)}) async-start(), calls=%async_computation.10 | async-start | bytes 1216512 | tf_op jit(solution)/shard_map/all_gather | solution.py:76
  9.4 234.8 %all-gather.17.cloned.1.call-start = ((), (), s32[]{:S(2)}) async-start(), calls=%async_computation.12 | async-start | bytes 1216512 | tf_op jit(solution)/shard_map/all_gather | solution.py:77
  10.0 296.3 %reduce-scatter.13.cloned.1.call-start = ((), (), s32[]{:S(2)}) async-start(), calls=%async_computation.13 | async-start | bytes 983040 | tf_op jit(solution)/shard_map/reduce_scatter | solution.py:147
  60.4 130.4 %copy-start.34 = (f32[768]{0:T(1024)}, f32[768]{0:T(1024)S(1)}, u32[]{:S(2)}) copy-start(f32[768]{0:T(1024)S(1)} %convert_element_type.148) | copy-start | bytes 9220
  146.4 110.1 %copy-start.19 = (bf16[128,768]{0,1:T(8,128)(2,1)}, bf16[128,768]{0,1:T(8,128)(2,1)S(1)}, u32[]{:S(2)}) copy-start(bf16[128,768]{0,1:T(8,128)(2,1)S(1)} %reshape.321) | copy-start | bytes 589828
  282.1 81.0 %all-gather.19.cloned.1.call-start = ((), (), s32[]{:S(2)}) async-start(), calls=%async_computation.14 | async-start | bytes 1216512 | tf_op jit(solution)/shard_map/all_gather | solution.py:79
  282.7 146.3 %all-gather.23.cloned.1.call-start = ((), (), s32[]{:S(2)}) async-start(), calls=%async_computation.16 | async-start | bytes 4866048 | tf_op jit(solution)/shard_map/all_gather | solution.py:81
  283.4 211.4 %all-gather.21.cloned.1.call-start = ((), (), s32[]{:S(2)}) async-start(), calls=%async_computation.15 | async-start | bytes 4866048 | tf_op jit(solution)/shard_map/all_gather | solution.py:80
  284.2 282.3 %reduce-scatter.15.cloned.1.call-start = ((), (), s32[]{:S(2)}) async-start(), calls=%async_computation.17 | async-start | bytes 983040 | tf_op jit(solution)/shard_map/reduce_scatter | solution.py:206
  364.8 135.9 %copy-start.44 = (f32[128]{0:T(128)}, f32[128]{0:T(128)S(1)}, u32[]{:S(2)}) copy-start(f32[128]{0:T(128)S(1)} %broadcast_multiply_fusion.1) | copy-start | bytes 1540
  365.0 135.7 %copy-start.48 = (f32[128]{0:T(128)}, f32[128]{0:T(128)S(1)}, u32[]{:S(2)}) copy-start(f32[128]{0:T(128)S(1)} %fusion.33) | copy-start | bytes 1540
  365.2 129.6 %copy-start.30 = (bf16[128,768]{1,0:T(8,128)(2,1)}, bf16[128,768]{1,0:T(8,128)(2,1)S(1)}, u32[]{:S(2)}) copy-start(bf16[128,768]{1,0:T(8,128)(2,1)S(1)} %add_convert_fusion.1) | copy-start | bytes 589828
  544.7 182.6 %all-gather.25.cloned.1.call-start = ((), (), s32[]{:S(2)}) async-start(), calls=%async_computation.18 | async-start | bytes 2949120 | tf_op jit(solution)/shard_map/all_gather | solution.py:255
  592.9 150.9 %all-gather.27.cloned.1.call-start = ((), (), s32[]{:S(2)}) async-start(), calls=%async_computation.23 | async-start | bytes 3932160 | tf_op jit(solution)/shard_map/all_gather | solution.py:263
  593.6 163.5 %all-gather.29.cloned.1.call-start = ((), (), s32[]{:S(2)}) async-start(), calls=%async_computation.25 | async-start | bytes 3932160 | tf_op jit(solution)/shard_map/all_gather | solution.py:264
  594.2 227.1 %reduce-scatter.23.cloned.1.call-start = ((), (), s32[]{:S(2)}) async-start(), calls=%async_computation.22 | async-start | bytes 663552 | tf_op jit(solution)/shard_map/reduce_scatter | solution.py:279
  621.7 199.6 %reduce-scatter.21.cloned.1.call-start = ((), (), s32[]{:S(2)}) async-start(), calls=%async_computation.21 | async-start | bytes 663552 | tf_op jit(solution)/shard_map/reduce_scatter | solution.py:279
  661.1 222.7 %reduce-scatter.19.cloned.1.call-start = ((), (), s32[]{:S(2)}) async-start(), calls=%async_computation.20 | async-start | bytes 663552 | tf_op jit(solution)/shard_map/reduce_scatter | solution.py:279
  698.7 298.2 %reduce-scatter.29.cloned.1.call-start = ((), (), s32[]{:S(2)}) async-start(), calls=%async_computation.27 | async-start | bytes 4866048
  713.7 352.6 %reduce-scatter.17.cloned.1.call-start = ((), (), s32[]{:S(2)}) async-start(), calls=%async_computation.19 | async-start | bytes 1990656 | tf_op jit(solution)/shard_map/reduce_scatter | solution.py:279
  731.2 407.6 %reduce-scatter.25.cloned.1.call-start = ((), (), s32[]{:S(2)}) async-start(), calls=%async_computation.24 | async-start | bytes 2654208 | tf_op jit(solution)/shard_map/reduce_scatter | solution.py:279
  747.8 463.6 %reduce-scatter.27.cloned.1.call-start = ((), (), s32[]{:S(2)}) async-start(), calls=%async_computation.26 | async-start | bytes 2654208 | tf_op jit(solution)/shard_map/reduce_scatter | solution.py:279
  (55 other events, 932.8 us)
Sparse Core Ops, SparseCore 0:
  10.9 59.4 all-gather.14
  73.3 59.2 all-gather.10
  135.6 52.8 all-gather.12
  191.2 52.9 all-gather.16
  282.2 23.1 reduce-scatter.12
  308.6 54.4 all-gather.18
  366.4 62.5 all-gather.22
  432.3 62.4 all-gather.20
  544.9 21.5 reduce-scatter.14
  593.0 28.9 all-gather.24
  623.6 36.2 all-gather.26
  661.3 28.5 all-gather.28
  693.7 60.0 reduce-scatter.22
  757.9 61.0 reduce-scatter.20
  822.7 61.0 reduce-scatter.18
  890.6 106.1 reduce-scatter.28
  1000.7 65.4 reduce-scatter.16
  1070.6 68.1 reduce-scatter.24
  1143.3 68.1 reduce-scatter.26
where the time goes:
time: 1230 us; the launch traced here: 1220 us
  waiting for transfers between devices  727 us (59%)
  blocking collectives  221 us (18%)
  local copies, waits for them, and re-layouts  129 us (10%)
  matrix products  101 us (8%)
  other arithmetic  23.2 us (2%)
  between operations  16 us (1%)
    reduce_scatter x6, waiting for transfers between devices, per_device(): lax.psum_scatter(text_terms, 'wide', scatter_dimension=0, tiled=True)  277 us
    unnamed x20, waiting for transfers between devices  119 us
    unnamed x3, blocking collectives  92.1 us
    all_gather x1, waiting for transfers between devices, per_device(): lax.all_gather(shards[6], ('wide', 'narrow'), axis=0, tiled=True)  63.8 us
    all_gather x1, waiting for transfers between devices, per_device(): lax.all_gather(shards[5], ('wide', 'narrow'), axis=0, tiled=True)  60.6 us
    all_gather x1, waiting for transfers between devices, per_device(): lax.all_gather(shards[4], ('wide', 'narrow'), axis=0, tiled=True)  53.8 us
    all_gather x1, waiting for transfers between devices, per_device(): lax.all_gather(shards[2], ('wide', 'narrow'), axis=0, tiled=True)  53.1 us
    all_gather x1, waiting for transfers between devices, per_device(): lax.all_gather(shards[1], ('wide', 'narrow'), axis=0, tiled=True)  42.1 us
  transfers between devices with their start and end apart: 19, of which 13 were waited for; matrix products, arithmetic and copies ran while one was open for 14% of the time, Pallas kernels for 0%

commit v1 on v0

v1 whole, which is shorter than its diff:
```python
import functools

import jax
import jax.numpy as jnp
from jax import lax
from jax.experimental import pallas as pl
from jax.experimental.pallas import tpu as pltpu
from jax.sharding import PartitionSpec as P

HEADS = 12
NODES = 32
UNITS = 8
MESH = pl.DeviceIdType.MESH
F32 = jnp.float32
LOW = jnp.bfloat16
EPSILON = 1e-05
GELU_A = 0.7978845608028654
GELU_B = 0.044715

QS, KS, VS, SO, CK, CV, CQ, CO, UP = 0, 1, 2, 3, 4, 5, 6, 7, 8


def mm(left, right):
    return jnp.dot(left, right, preferred_element_type=F32)


def mm_bt(left, right):
    return lax.dot_general(left, right, (((1,), (1,)), ((), ())), preferred_element_type=F32)


def mm_at(left, right):
    return lax.dot_general(left, right, (((0,), (0,)), ((), ())), preferred_element_type=F32)


def norm(value, gain, shift):
    centred = value - jnp.mean(value, axis=-1, keepdims=True)
    rstd = lax.rsqrt(jnp.mean(centred * centred, axis=-1, keepdims=True) + EPSILON)
    hat = centred * rstd
    return hat, rstd, hat * gain + shift


def norm_pull(grad, hat, rstd, gain):
    scaled = grad * gain
    inner = jnp.mean(scaled * hat, axis=-1, keepdims=True)
    back = rstd * (scaled - jnp.mean(scaled, axis=-1, keepdims=True) - hat * inner)
    gain_grad = jnp.sum(grad * hat, axis=0, keepdims=True)
    shift_grad = jnp.sum(grad, axis=0, keepdims=True)
    return back, gain_grad, shift_grad


class Layer:
    def __init__(self, refs, lanes, narrow):
        self.__dict__.update(refs)
        self.N = narrow
        self.lanes = lanes
        wide, nar = lax.axis_index("wide"), lax.axis_index("narrow")
        flat = wide * narrow + nar
        self.wide, self.nar = wide, nar
        self.node = lax.div(flat, lanes)
        self.lane = lax.rem(flat, lanes)
        node = self.node
        self.c = lax.rem(node, 2)
        self.x = lax.rem(lax.div(node, 2), 2)
        self.y = lax.rem(lax.div(node, 4), 2)
        self.z = lax.div(node, 8)
        self.started = []
        self.count, self.seq = self.captions.shape[0] // 64, 64
        self.tokens, self.width = self.captions.shape
        self.groups = self.QA.shape[0]
        self.image_rows = self.images.shape[0] // self.groups
        self.pairs = self.width // 128
        lane = lax.broadcasted_iota(jnp.int32, (1, 128), 1)
        self.first = (lane < 64).astype(F32).astype(LOW)
        self.second = (lane >= 64).astype(F32).astype(LOW)
        self.is_first = lane < 64

    def device(self, z, y, x, c):
        flat = (z * 8 + y * 4 + x * 2 + c) * self.lanes + self.lane
        return (lax.div(flat, self.N), lax.rem(flat, self.N))

    def sibling(self):
        return self.device(self.z, self.y, self.x, 1 - self.c)

    def x_peer(self):
        return self.device(self.z, self.y, 1 - self.x, self.c)

    def y_peer(self):
        return self.device(self.z, 1 - self.y, self.x, self.c)

    def z_index(self, k):
        return lax.rem(self.z + k, 4)

    def z_peer(self, k):
        return self.device(self.z_index(k), self.y, self.x, self.c)

    def n_index(self, k):
        return lax.rem(self.nar + k, self.N)

    def n_peer(self, k):
        return (self.wide, self.n_index(k))

    def enter(self):
        barrier = pltpu.get_barrier_semaphore()
        peers = [self.sibling(), self.x_peer(), self.y_peer()]
        peers += [self.z_peer(k) for k in (1, 2, 3)]
        peers += [self.n_peer(k) for k in range(1, self.N)]
        for peer in peers:
            pl.semaphore_signal(barrier, inc=1, device_id=peer, device_id_type=MESH)
        pl.semaphore_wait(barrier, len(peers))

    def copy(self, src, dst, sems, where, peer):
        send, recv = sems
        return pltpu.make_async_remote_copy(
            src_ref=src,
            dst_ref=dst,
            send_sem=send.at[where],
            recv_sem=recv.at[where],
            device_id=peer,
            device_id_type=MESH,
        )

    def start(self, copies):
        for item in copies:
            item.start()
        self.started += copies

    def finish_sends(self):
        for item in self.started:
            item.wait_send()
        self.started = []

    def part(self, unit, half, z, y, x):
        if unit < 6:
            if half is None:
                return self.W.at[2 * unit + self.c, z, y, x]
            return self.W.at[2 * unit + self.c, z, y, x, :, pl.ds(384 * half, 384)]
        first = 96 * (unit - 6)
        if half is None:
            return self.HD.at[self.c, z, y, x, pl.ds(first, 96)]
        return self.HD.at[self.c, z, y, x, pl.ds(first + 48 * half, 48)]

    def pair_copies(self):
        c = self.c
        other = pl.ds(pl.multiple_of(384 * (1 - c), 128), 384)
        rows = pl.ds(pl.multiple_of(96 * c, 32), 96)
        return [
            self.copy(self.pack.at[1 - c], self.PAIR, self.s_pair, 0, self.sibling()),
            self.copy(
                self.down.at[:, other],
                self.HD.at[1 - c, self.z, self.y, self.x, rows],
                self.s_pair,
                1,
                self.sibling(),
            ),
        ]

    def pair_merge(self):
        c = self.c
        copies = self.pair_copies()
        own = pl.ds(pl.multiple_of(384 * c, 128), 384)
        rows = pl.ds(pl.multiple_of(96 * c, 32), 96)
        self.HD[c, self.z, self.y, self.x, rows] = self.down[:, own]
        copies[0].wait_recv()
        mine = self.pack[c].astype(F32)
        theirs = self.PAIR[...].astype(F32)
        even = c == 0
        low = jnp.where(even, mine, theirs)
        high = jnp.where(even, theirs, mine)
        for unit in range(6):
            rows = slice(24 * unit, 24 * unit + 24)
            both = jnp.concatenate([low[rows], high[rows]], axis=0).astype(LOW)
            self.W[2 * unit + c, self.z, self.y, self.x] = both
        copies[1].wait_recv()

    def z_copies(self, unit):
        here = self.part(unit, None, self.z, self.y, self.x)
        return [
            self.copy(here, here, self.s_z, (unit, k - 1), self.z_peer(k)) for k in (1, 2, 3)
        ]

    def two_copies(self, unit):
        every = slice(None)
        a = self.part(unit, 0, every, self.y, self.x)
        b = self.part(unit, 1, every, self.y, self.x)
        return [
            self.copy(a, a, self.s_two, (unit, 0), self.x_peer()),
            self.copy(b, b, self.s_two, (unit, 1), self.y_peer()),
        ]

    def three_copies(self, unit):
        every = slice(None)
        a = self.part(unit, 0, every, self.y, every)
        b = self.part(unit, 1, every, every, self.x)
        return [
            self.copy(a, a, self.s_three, (unit, 0), self.y_peer()),
            self.copy(b, b, self.s_three, (unit, 1), self.x_peer()),
        ]

    def hand_copies(self, unit):
        every = slice(None)
        whole = self.part(unit, None, every, every, every)
        return [self.copy(whole, whole, self.s_hand, unit, self.sibling())]

    def arrived(self, copies):
        for item in copies:
            item.wait_recv()

    def gather_tick(self, tick):
        if 0 <= tick < UNITS:
            self.arrived(self.z_copies(tick))
            self.start(self.two_copies(tick))
        if 0 <= tick - 1 < UNITS:
            self.arrived(self.two_copies(tick - 1))
            self.start(self.three_copies(tick - 1))
        if 0 <= tick - 2 < UNITS:
            self.arrived(self.three_copies(tick - 2))
            self.start(self.hand_copies(tick - 2))
        if 0 <= tick - 3 < UNITS:
            self.arrived(self.hand_copies(tick - 3))

    def rs_one_copies(self, unit):
        every = slice(None)
        a = self.part(unit, 0, every, 1 - self.y, every)
        b = self.part(unit, 1, every, every, 1 - self.x)
        return [
            self.copy(a, self.R1.at[unit, 0], self.s_rs1, (unit, 0), self.y_peer()),
            self.copy(b, self.R1.at[unit, 1], self.s_rs1, (unit, 1), self.x_peer()),
        ]

    def rs_two_copies(self, unit):
        every = slice(None)
        a = self.part(unit, 0, every, self.y, 1 - self.x)
        b = self.part(unit, 1, every, 1 - self.y, self.x)
        return [
            self.copy(a, self.R2.at[unit, 0], self.s_rs2, (unit, 0), self.x_peer()),
            self.copy(b, self.R2.at[unit, 1], self.s_rs2, (unit, 1), self.y_peer()),
        ]

    def rs_three_copies(self, unit):
        out = []
        for k in (1, 2, 3):
            here = self.part(unit, None, self.z_index(k), self.y, self.x)
            there = self.R3.at[unit, k - 1] if unit < 6 else self.R3H.at[unit - 6, k - 1]
            out.append(self.copy(here, there, self.s_rs3, (unit, k - 1), self.z_peer(k)))
        return out

    def rs_four_copies(self, unit):
        if unit < 6:
            block = 2 * unit + self.c
            return [
                self.copy(self.SF.at[unit], self.block_grad.at[block], self.s_rs4, unit, self.sibling())
            ]
        half = pl.ds(pl.multiple_of(384 * self.c, 128), 384)
        return [
            self.copy(self.SFH, self.down_out.at[:, half], self.s_rs4, unit, self.sibling())
        ]

    def add_into(self, ref, term):
        ref[...] = (ref[...].astype(F32) + term.astype(F32)).astype(LOW)

    def rs_one(self, unit):
        self.start(self.rs_one_copies(unit))

    def rs_two(self, unit):
        self.arrived(self.rs_one_copies(unit))

        @pl.loop(0, 4)
        def _(z):
            self.add_into(self.part(unit, 0, z, self.y, slice(None)), self.R1[unit, 0, z])
            self.add_into(self.part(unit, 1, z, slice(None), self.x), self.R1[unit, 1, z])

        self.start(self.rs_two_copies(unit))

    def rs_three(self, unit):
        self.arrived(self.rs_two_copies(unit))

        @pl.loop(0, 4)
        def _(z):
            self.add_into(self.part(unit, 0, z, self.y, self.x), self.R2[unit, 0, z])
            self.add_into(self.part(unit, 1, z, self.y, self.x), self.R2[unit, 1, z])

        self.start(self.rs_three_copies(unit))

    def rs_total(self, unit):
        self.arrived(self.rs_three_copies(unit))
        total = self.part(unit, None, self.z, self.y, self.x)[...].astype(F32)
        for k in range(3):
            more = self.R3[unit, k] if unit < 6 else self.R3H[unit - 6, k]
            total = total + more.astype(F32)
        return total

    def rs_four(self, unit):
        even = self.c == 0
        if unit < 6:
            total = self.rs_total(unit)
            low, high = total[:24], total[24:]
            self.block_grad[2 * unit + self.c] = jnp.where(even, low, high)
            self.SF[unit] = jnp.where(even, high, low)
            self.start(self.rs_four_copies(unit))
        if unit == 7:
            low, high = self.rs_total(6), self.rs_total(7)
            half = pl.ds(pl.multiple_of(384 * self.c, 128), 384)
            self.down_out[:, half] = jnp.where(even, low, high)
            self.SFH[...] = jnp.where(even, high, low)
            self.start(self.rs_four_copies(7))

    def rs_done(self, unit):
        if unit != 6:
            self.arrived(self.rs_four_copies(unit))

    def scatter_tick(self, order, tick):
        def at(back):
            place = tick - back
            return order[place] if 0 <= place < len(order) else None

        if at(0) is not None:
            self.rs_one(at(0))
        if at(1) is not None:
            self.rs_two(at(1))
        if at(2) is not None:
            self.rs_three(at(2))
        if at(3) is not None:
            self.rs_four(at(3))

    def sum_all(self, which, value):
        def copies(stage):
            peers = [[self.sibling()], [self.x_peer()], [self.y_peer()]]
            peers += [[self.z_peer(k) for k in (1, 2, 3)]]
            return [
                self.copy(
                    self.V.at[which, stage],
                    self.VR.at[which, stage + i],
                    self.s_vec,
                    (which, stage + i),
                    peer,
                )
                for i, peer in enumerate(peers[stage])
            ]

        for stage in range(4):
            self.V[which, stage] = value
            now = copies(stage)
            self.start(now)
            self.arrived(now)
            for i in range(len(now)):
                value = value + self.VR[which, stage + i]
        return value

    def keep_left(self, place, value):
        self.LHS[place, self.c] = value
        here = self.LHS.at[place, self.c]
        self.start([self.copy(here, here, self.s_left, place, self.sibling())])

    def keep_right(self, place, value):
        self.RHS[place, self.c] = value
        here = self.RHS.at[place, self.c]
        self.start([self.copy(here, here, self.s_right, place, self.sibling())])

    def left_arrived(self, place):
        here = self.LHS.at[place, self.c]
        self.copy(here, here, self.s_left, place, self.sibling()).wait_recv()

    def right_arrived(self, place):
        here = self.RHS.at[place, self.c]
        self.copy(here, here, self.s_right, place, self.sibling()).wait_recv()

    def weight(self, block):
        return self.W[block].reshape(self.width, self.width)

    def weight_grad(self, unit, left, right):
        c = self.c
        li = jnp.where(c == 0, left[0], left[1])
        ri = jnp.where(c == 0, right[0], right[1])
        right_all = self.RHS[ri].reshape(2 * self.tokens, self.width)
        for t in range(2):
            left_all = self.LHS[li, :, :, pl.ds(384 * t, 384)].reshape(2 * self.tokens, 384)
            part = mm_at(left_all, right_all).astype(LOW)
            self.W[2 * unit + c, pl.ds(2 * t, 2)] = part.reshape(2, 2, 2, 48, self.width)

    def down_grad(self):
        c = self.c
        half = pl.ds(pl.multiple_of(384 * c, 128), 384)
        right_all = self.RHS[10, :, :, half].reshape(2 * self.tokens, 384)
        for j in range(4):
            for t in range(2):
                left_all = self.LHS[5 + j, :, :, pl.ds(384 * t, 384)].reshape(2 * self.tokens, 384)
                part = mm_at(left_all, right_all).astype(LOW)
                self.HD[c, j, t] = part.reshape(2, 192, 384)

    def memory_copy(self):
        return self.copy(self.W.at[CV - self.c], self.CM, self.s_memory, 0, self.sibling())

    def memory_grad_other(self):
        c = self.c

        @pl.loop(0, 2)
        def _(t):
            left = self.images[:, pl.ds(pl.multiple_of(384 * t, 128), 384)]
            part = mm_at(left, self.KV[1 - c]).astype(LOW)
            self.W[CV - c, pl.ds(2 * t, 2)] = part.reshape(2, 2, 2, 48, self.width)

        self.start([self.memory_copy()])

    def memory_grad_own(self):
        c = self.c
        self.memory_copy().wait_recv()

        @pl.loop(0, 2)
        def _(t):
            left = self.images[:, pl.ds(pl.multiple_of(384 * t, 128), 384)]
            part = mm_at(left, self.KV[c]).reshape(2, 2, 2, 48, self.width)
            part = part + self.CM[pl.ds(2 * t, 2)].astype(F32)
            self.W[CK + c, pl.ds(2 * t, 2)] = part.astype(LOW)

    def masked(self, value):
        return value * self.first, value * self.second

    def self_attention(self):
        rows = lax.broadcasted_iota(jnp.int32, (128, 128), 0)
        cols = lax.broadcasted_iota(jnp.int32, (128, 128), 1)
        length = jnp.where(cols < 64, self.lengths[0], self.lengths[1])
        allowed = (lax.div(rows, 64) == lax.div(cols, 64)) & (cols <= rows)
        allowed = allowed & (lax.rem(cols, 64) < length)
        parts = []
        for p in range(self.pairs):
            at = slice(128 * p, 128 * p + 128)
            q, k, v = self.QKV[0, :, at], self.QKV[1, :, at], self.QKV[2, :, at]
            total = None
            for h, (qm, vm) in enumerate(zip(self.masked(q), self.masked(v))):
                s = mm_bt(qm, k) * 0.125
                s = jnp.where(allowed, s, -1000000000.0)
                e = jnp.exp(s - jnp.max(s, axis=-1, keepdims=True))
                prob = e / jnp.sum(e, axis=-1, keepdims=True)
                self.PS[2 * p + h] = prob
                out = mm(prob.astype(LOW), vm)
                total = out if total is None else total + out
            parts.append(total.astype(LOW))
        return jnp.concatenate(parts, axis=1)

    def self_attention_back(self, grad):
        parts = ([], [], [])
        for p in range(self.pairs):
            at = slice(128 * p, 128 * p + 128)
            q, k, v = self.QKV[0, :, at], self.QKV[1, :, at], self.QKV[2, :, at]
            g = grad[:, at]
            dq = dk = dv = 0.0
            for h, (qm, km, gm) in enumerate(
                zip(self.masked(q), self.masked(k), self.masked(g))
            ):
                prob = self.PS[2 * p + h]
                dp = mm_bt(gm, v)
                ds = prob * (dp - jnp.sum(prob * dp, axis=-1, keepdims=True))
                ds = ds.astype(LOW)
                dq = dq + mm(ds, km)
                dk = dk + mm_at(ds, qm)
                dv = dv + mm_at(prob.astype(LOW), gm)
            for out, item in zip(parts, (dq * 0.125, dk * 0.125, dv)):
                out.append(item.astype(LOW))
        return [jnp.concatenate(item, axis=1) for item in parts]

    def stacked(self, value):
        a, b = self.masked(value)
        return jnp.concatenate([a, b], axis=0)

    def diagonal(self, value):
        return jnp.where(self.is_first, value[:64], value[64:])

    def memory_forward(self, which):
        w = self.weight(CK + which)

        @pl.loop(0, 3)
        def _(t):
            size = self.images.shape[0] // 3
            rows = pl.ds(pl.multiple_of(size * t, 16), size)
            self.KV[which, rows] = mm(self.images[rows], w).astype(LOW)

    def cross_forward(self, place):
        rows = pl.ds(pl.multiple_of(place * self.image_rows, 16), self.image_rows)
        for p in range(self.pairs):
            at = slice(128 * p, 128 * p + 128)
            k, v = self.KV[0, rows, at], self.KV[1, rows, at]
            q = self.stacked(self.QA[place, :, at])
            s = mm_bt(k, q) * 0.125
            top = jnp.max(s, axis=0, keepdims=True)
            e = jnp.exp(s - top)
            self.E[place, p] = e
            self.ST[place, p : p + 1] = jnp.sum(e, axis=0, keepdims=True)
            self.ST[place, 8 + p : 9 + p] = top
            num = mm_at(e.astype(LOW), v)
            self.NUM[place, :, at] = self.diagonal(num).astype(LOW)
        self.ST[place, 6:8] = jnp.ones((2, 128), F32)
        self.ST[place, 14:16] = jnp.zeros((2, 128), F32)

    def cross_backward(self, place):
        rows = pl.ds(pl.multiple_of(place * self.image_rows, 16), self.image_rows)
        for p in range(self.pairs):
            at = slice(128 * p, 128 * p + 128)
            k, v = self.KV[0, rows, at], self.KV[1, rows, at]
            q = self.stacked(self.QA[place, :, at])
            g = self.stacked(self.GA[place, :, at])
            e = self.E[place, p]
            ds = e * (mm_bt(v, g) + self.DL[place, p : p + 1])
            ds = ds.astype(LOW)
            dq = mm_at(ds, k)
            self.NUM[place, :, at] = (self.diagonal(dq) * 0.125).astype(LOW)
            self.KV[0, rows, at] = (mm(ds, q) * 0.125).astype(LOW)
            self.KV[1, rows, at] = mm(e.astype(LOW), g).astype(LOW)

    def own(self, k=0):
        return pl.ds(self.n_index(k) * self.count, self.count)

    def query_copies(self):
        here = self.QA.at[self.own()]
        return [self.copy(here, here, self.s_query, k - 1, self.n_peer(k)) for k in range(1, self.N)]

    def number_copies(self, k):
        return [
            self.copy(
                self.NUM.at[self.own(k)], self.NUMR.at[self.N - k], self.s_num, k - 1, self.n_peer(k)
            ),
            self.copy(
                self.ST.at[self.own(k)], self.STR.at[self.N - k], self.s_st, k - 1, self.n_peer(k)
            ),
        ]

    def grad_copies(self, k):
        return [
            self.copy(
                self.GS.at[k], self.GA.at[self.own()], self.s_g, k - 1, self.n_peer(k)
            ),
            self.copy(
                self.DS.at[k], self.DL.at[self.own()], self.s_dl, k - 1, self.n_peer(k)
            ),
        ]

    def back_copies(self, k):
        return [
            self.copy(self.NUM.at[self.own(k)], self.NUMR.at[k], self.s_dq, k - 1, self.n_peer(k))
        ]

    def column(self, turned, p):
        return jnp.where(self.is_first, turned[:64, p : p + 1], turned[64:, p : p + 1])

    def combine(self):
        self.NUMR[0] = self.NUM[self.own()]
        self.STR[0] = self.ST[self.own()]
        done = []
        for j in range(self.count):
            totals = [self.STR[k, j, :8] for k in range(self.N)]
            tops = [self.STR[k, j, 8:] for k in range(self.N)]
            top = functools.reduce(jnp.maximum, tops)
            shares = [jnp.exp(item - top) for item in tops]
            total = sum(a * b for a, b in zip(shares, totals))
            turned = []
            for k in range(self.N):
                scale = shares[k] / total
                self.SCR[k, j] = scale
                wide = jnp.concatenate([scale, jnp.zeros((120, 128), F32)], axis=0)
                turned.append(wide.T)
                self.SCT[k, j] = turned[k]
            parts = []
            for p in range(self.pairs):
                at = slice(128 * p, 128 * p + 128)
                parts.append(
                    sum(
                        self.NUMR[k, j, :, at].astype(F32) * self.column(turned[k], p)
                        for k in range(self.N)
                    )
                )
            done.append(jnp.concatenate(parts, axis=1))
        return jnp.concatenate(done, axis=0)

    def spread_grad(self, doc):
        lane = lax.broadcasted_iota(jnp.int32, (128, 128), 1)
        for j in range(self.count):
            rows = slice(64 * j, 64 * j + 64)
            inner = jnp.zeros((128, 128), F32)
            for p in range(self.pairs):
                at = slice(128 * p, 128 * p + 128)
                part = doc[rows, at]
                prod = part * self.OCF[rows, at]
                a = jnp.sum(jnp.where(self.is_first, prod, 0.0), axis=1, keepdims=True)
                b = jnp.sum(jnp.where(self.is_first, 0.0, prod), axis=1, keepdims=True)
                inner = jnp.where(lane == p, jnp.concatenate([a, b], axis=0), inner)
                for k in range(self.N):
                    scale = self.column(self.SCT[k, j], p)
                    self.GS[k, j, :, at] = (part * scale).astype(LOW)
            inner = inner.T[:8]
            for k in range(self.N):
                self.DS[k, j] = -inner * self.SCR[k, j]

    def run(self):
        c = self.c
        tokens, width, count = self.tokens, self.width, self.count
        self.enter()
        self.start(self.pair_copies())
        self.keep_right(10, self.out_grad[...])
        vectors = self.sum_all(0, self.vec[...])
        gain1, shift1 = vectors[0:1], vectors[1:2]
        gain2, shift2 = vectors[2:3], vectors[3:4]
        gain3, shift3 = vectors[4:5], vectors[5:6]
        self.pair_merge()
        for unit in range(UNITS):
            self.start(self.z_copies(unit))
        for tick in range(UNITS + 3):
            self.gather_tick(tick)
        self.finish_sends()

        inputs = self.captions[...].astype(F32)
        hat1, rstd1, a1 = norm(inputs, gain1, shift1)
        self.HAT[0] = hat1
        a1 = a1.astype(LOW)
        self.keep_left(0, a1)
        for j in range(3):
            self.QKV[j] = mm(a1, self.weight(j)).astype(LOW)
        mixed = self.self_attention()
        self.keep_left(1, mixed)
        r1 = inputs + mm(mixed, self.weight(SO))
        hat2, rstd2, a2 = norm(r1, gain2, shift2)
        self.HAT[1] = hat2
        a2 = a2.astype(LOW)
        self.keep_left(2, a2)
        self.QA[self.own()] = mm(a2, self.weight(CQ)).astype(LOW).reshape(count, 64, width)
        queries = self.query_copies()
        self.start(queries)
        self.memory_forward(0)
        self.memory_forward(1)
        self.arrived(queries)
        pl.loop(0, self.groups)(self.cross_forward)
        for k in range(1, self.N):
            self.start(self.number_copies(k))
        for k in range(1, self.N):
            self.arrived(self.number_copies(k))
        full = self.combine()
        self.OCF[...] = full
        oc = full.astype(LOW)
        self.keep_left(3, oc)
        r2 = r1 + mm(oc, self.weight(CO))
        hat3, rstd3, a3 = norm(r2, gain3, shift3)
        self.HAT[2] = hat3
        a3 = a3.astype(LOW)
        self.keep_left(4, a3)
        out = [r2[:, :384], r2[:, 384:]]
        grad = self.out_grad[...]
        e3 = 0.0
        for j in range(4):
            hidden = mm(a3, self.weight(UP + j))
            square = hidden * hidden
            tanh = jnp.tanh(GELU_A * hidden * (1.0 + GELU_B * square))
            act = (0.5 * hidden * (1.0 + tanh)).astype(LOW)
            slope = 0.5 * (1.0 + tanh) + 0.5 * hidden * (1.0 - tanh * tanh) * (
                GELU_A * (1.0 + 3.0 * GELU_B * square)
            )
            self.keep_left(5 + j, act)
            down = [self.HD[i, j].reshape(width, 384) for i in range(2)]
            for i in range(2):
                out[i] = out[i] + mm(act, down[i])
            back = mm_bt(grad[:, :384], down[0]) + mm_bt(grad[:, 384:], down[1])
            dhp = (back * slope).astype(LOW)
            self.keep_right(6 + j, dhp)
            e3 = e3 + mm_bt(dhp, self.weight(UP + j))
        self.layer_out[...] = jnp.concatenate(out, axis=1).astype(LOW)

        order = [6, 7, 4, 5, 3, 2, 1, 0]
        back3, gain3_grad, shift3_grad = norm_pull(e3, self.HAT[2], rstd3, gain3)
        dr2 = grad.astype(F32) + back3
        dcat = dr2.astype(LOW)
        self.keep_right(5, dcat)
        self.spread_grad(mm_bt(dcat, self.weight(CO)))
        for k in range(1, self.N):
            self.start(self.grad_copies(k))
        self.GA[self.own()] = self.GS[0]
        self.DL[self.own()] = self.DS[0]
        for k in range(1, self.N):
            self.arrived(self.grad_copies(k))
        self.finish_sends()
        pl.loop(0, self.groups)(self.cross_backward)
        for k in range(1, self.N):
            self.start(self.back_copies(k))
        self.NUMR[0] = self.NUM[self.own()]
        for k in range(1, self.N):
            self.arrived(self.back_copies(k))
        dqc = sum(self.NUMR[k].astype(F32) for k in range(self.N))
        dqc = dqc.astype(LOW).reshape(tokens, width)
        self.keep_right(4, dqc)
        back2, gain2_grad, shift2_grad = norm_pull(
            mm_bt(dqc, self.weight(CQ)), self.HAT[1], rstd2, gain2
        )
        dr1 = dr2 + back2
        dattn = dr1.astype(LOW)
        self.keep_right(3, dattn)
        dos = mm_bt(dattn, self.weight(SO)).astype(LOW)
        e1 = 0.0
        for j, item in enumerate(self.self_attention_back(dos)):
            self.keep_right(j, item)
            e1 = e1 + mm_bt(item, self.weight(j))
        back1, gain1_grad, shift1_grad = norm_pull(e1, self.HAT[0], rstd1, gain1)
        self.input_grad[...] = (dr1 + back1).astype(LOW)

        @pl.loop(0, 3)
        def _(t):
            size = self.images.shape[0] // 3
            rows = pl.ds(pl.multiple_of(size * t, 16), size)
            part = mm_bt(self.KV[0, rows], self.weight(CK))
            part = part + mm_bt(self.KV[1, rows], self.weight(CV))
            self.image_grad[rows] = part.astype(LOW)

        grads = [gain1_grad, shift1_grad, gain2_grad, shift2_grad, gain3_grad, shift3_grad]
        grads = jnp.concatenate(grads + [jnp.zeros((2, width), F32)], axis=0)

        for place in range(9):
            self.left_arrived(place)
        for place in range(11):
            self.right_arrived(place)
        self.finish_sends()
        self.down_grad()
        self.weight_grad(4, (4, 4), (6, 7))
        self.weight_grad(5, (4, 4), (8, 9))
        self.weight_grad(3, (2, 3), (4, 5))
        self.memory_grad_other()
        self.memory_grad_own()
        self.weight_grad(1, (0, 1), (2, 3))
        self.weight_grad(0, (0, 0), (0, 1))
        for tick in range(UNITS + 3):
            self.scatter_tick(order, tick)
        self.vec_grad[...] = self.sum_all(1, grads)
        for unit in range(UNITS):
            self.rs_done(unit)
        self.finish_sends()


def layer_call(lanes, narrow, captions, images, lengths, out_grad, pack, down, vec):
    tokens, width = captions.shape
    count = tokens // 64
    groups = narrow * count
    image_rows = images.shape[0]
    pairs = width // 128
    ins = ["captions", "images", "lengths", "out_grad", "pack", "down", "vec"]
    outs = {
        "layer_out": ((tokens, width), LOW),
        "input_grad": ((tokens, width), LOW),
        "image_grad": ((image_rows, width), LOW),
        "block_grad": ((12, 24, width), F32),
        "down_out": ((96, width), F32),
        "vec_grad": ((8, width), F32),
    }
    memory = {
        "W": ((12, 4, 2, 2, 48, width), LOW),
        "HD": ((2, 4, 2, 2, 192, 384), LOW),
        "PAIR": ((144, width), LOW),
        "KV": ((2, image_rows, width), LOW),
        "E": ((groups, pairs, image_rows // groups, 128), F32),
        "LHS": ((9, 2, tokens, width), LOW),
        "RHS": ((11, 2, tokens, width), LOW),
        "R1": ((UNITS, 2, 4, 2, 48, 384), LOW),
        "R2": ((UNITS, 2, 4, 48, 384), LOW),
        "R3": ((6, 3, 48, width), LOW),
        "R3H": ((2, 3, 96, 384), LOW),
        "CM": ((4, 2, 2, 48, width), LOW),
        "SF": ((6, 24, width), F32),
        "SFH": ((96, 384), F32),
        "V": ((2, 4, 8, width), F32),
        "VR": ((2, 6, 8, width), F32),
        "QKV": ((3, tokens, width), LOW),
        "PS": ((HEADS, 128, 128), F32),
        "HAT": ((3, tokens, width), F32),
        "OCF": ((tokens, width), F32),
        "QA": ((groups, 64, width), LOW),
        "NUM": ((groups, 64, width), LOW),
        "ST": ((groups, 16, 128), F32),
        "NUMR": ((narrow, count, 64, width), LOW),
        "STR": ((narrow, count, 16, 128), F32),
        "SCR": ((narrow, count, 8, 128), F32),
        "SCT": ((narrow, count, 128, 128), F32),
        "GS": ((narrow, count, 64, width), LOW),
        "DS": ((narrow, count, 8, 128), F32),
        "GA": ((groups, 64, width), LOW),
        "DL": ((groups, 8, 128), F32),
    }
    signals = {
        "s_pair": (2,),
        "s_z": (UNITS, 3),
        "s_two": (UNITS, 2),
        "s_three": (UNITS, 2),
        "s_hand": (UNITS,),
        "s_rs1": (UNITS, 2),
        "s_rs2": (UNITS, 2),
        "s_rs3": (UNITS, 3),
        "s_rs4": (UNITS,),
        "s_vec": (2, 6),
        "s_left": (9,),
        "s_right": (11,),
        "s_memory": (1,),
        "s_query": (narrow - 1,),
        "s_num": (narrow - 1,),
        "s_st": (narrow - 1,),
        "s_g": (narrow - 1,),
        "s_dl": (narrow - 1,),
        "s_dq": (narrow - 1,),
    }
    scratch = [pltpu.VMEM(shape, kind) for shape, kind in memory.values()]
    for shape in signals.values():
        scratch += [pltpu.SemaphoreType.DMA(shape)] * 2

    def body(*refs):
        named = dict(zip(ins + list(outs) + list(memory), refs))
        rest = refs[len(named) :]
        for i, name in enumerate(signals):
            named[name] = (rest[2 * i], rest[2 * i + 1])
        Layer(named, lanes, narrow).run()

    vmem = pl.BlockSpec(memory_space=pltpu.VMEM)
    in_specs = [vmem] * len(ins)
    in_specs[2] = pl.BlockSpec(memory_space=pltpu.SMEM)
    return pl.pallas_call(
        body,
        out_shape=[jax.ShapeDtypeStruct(shape, kind) for shape, kind in outs.values()],
        in_specs=in_specs,
        out_specs=[vmem] * len(outs),
        scratch_shapes=scratch,
        compiler_params=pltpu.CompilerParams(
            collective_id=0, has_side_effects=True, vmem_limit_bytes=64 * 1024 * 1024 - 65536
        ),
        cost_estimate=pl.CostEstimate(
            flops=17 * 10**9, bytes_accessed=8 * 10**6, transcendentals=2 * 10**6
        ),
        name="layer",
    )(captions, images, lengths, out_grad, pack, down, vec)


def lane_gather(value, lanes, narrow, axis):
    if lanes == 1:
        return value
    assert lanes % narrow == 0
    value = lax.all_gather(value, "narrow", axis=axis, tiled=True)
    step = 1
    wide_count = lax.axis_size("wide")
    while step * narrow < lanes:
        swap = [(i, i ^ step) for i in range(wide_count)]
        other = lax.ppermute(value, "wide", swap)
        low = (lax.axis_index("wide") // step) % 2 == 0
        first = jnp.where(low, value, other)
        second = jnp.where(low, other, value)
        value = jnp.concatenate([first, second], axis=axis)
        step *= 2
    return value


def lane_scatter(value, lanes, narrow, axis):
    if lanes == 1:
        return value
    wide_count = lax.axis_size("wide")
    step = lanes // narrow
    while step > 1:
        step //= 2
        swap = [(i, i ^ step) for i in range(wide_count)]
        first, second = jnp.split(value, 2, axis=axis)
        low = (lax.axis_index("wide") // step) % 2 == 0
        other = lax.ppermute(jnp.where(low, second, first), "wide", swap)
        value = jnp.where(low, first, second) + other
    return lax.psum_scatter(value, "narrow", scatter_dimension=axis, tiled=True)


def per_device(captions, images, lengths, out_grad, *params):
    narrow = lax.axis_size("narrow")
    devices = lax.axis_size("wide") * narrow
    lanes = devices // NODES
    count, seq_len, width = captions.shape
    tokens = count * seq_len
    flat = lax.axis_index("wide") * narrow + lax.axis_index("narrow")
    params = [lane_gather(item, lanes, narrow, 0) for item in params]
    joint, self_out, query, memory, cross, up, down = params[:7]
    blocks = [joint[:, width * j : width * (j + 1)] for j in range(3)] + [self_out]
    blocks += [memory[:, :width], memory[:, width:], query, cross]
    blocks += [up[:, width * j : width * (j + 1)] for j in range(4)]
    pack = jnp.stack([jnp.concatenate(blocks[i::2], axis=0) for i in range(2)])
    own = width // NODES
    start = lax.div(flat, lanes) * own
    vec = jnp.zeros((8, width), F32)
    vec = lax.dynamic_update_slice(vec, jnp.stack(params[7:]).astype(F32), (0, start))
    out, input_grad, image_grad, block_grad, down_grad, vec_grad = layer_call(
        lanes,
        narrow,
        captions.reshape(tokens, width),
        images.reshape(-1, width),
        lengths,
        out_grad.reshape(tokens, width),
        pack,
        down,
        vec,
    )
    vec_own = lax.dynamic_slice(vec_grad, (0, start), (6, own))
    block_grad = lane_scatter(block_grad, lanes, narrow, 1)
    down_grad = lane_scatter(down_grad, lanes, narrow, 0)
    vec_own = lane_scatter(vec_own, lanes, narrow, 1)

    def columns(*places):
        return jnp.concatenate([block_grad[i] for i in places], axis=1)

    return (
        out.reshape(captions.shape),
        input_grad.reshape(captions.shape),
        image_grad.reshape(images.shape),
        columns(QS, KS, VS),
        block_grad[SO],
        block_grad[CQ],
        columns(CK, CV),
        block_grad[CO],
        columns(UP, UP + 1, UP + 2, UP + 3),
        down_grad,
        *[vec_own[i] for i in range(6)],
    )


def solution(mesh):
    both = ("wide", "narrow")
    rows = P(both, None)
    text = P(both, None, None)
    vector = P(both)
    image = P("wide", "narrow", None)
    in_specs = (text, image, vector, text) + (rows,) * 7 + (vector,) * 6
    out_specs = (text, text, image) + (rows,) * 7 + (vector,) * 6
    return jax.shard_map(
        per_device, mesh=mesh, in_specs=in_specs, out_specs=out_specs, check_vma=False
    )
```

time: 1230 us -> 315 us (0.26)
  waiting for transfers between devices: 727 us -> 0 us
  Pallas kernels: 0 us -> 295 us
  blocking collectives: 221 us -> 0 us
  local copies, waits for them, and re-layouts: 129 us -> 13.6 us
  matrix products: 101 us -> 0 us
  other arithmetic: 23.2 us -> 2.91 us
  between operations: 16 us -> 0.71 us
    all_gather x10 -> x0, waiting for transfers between devices: 310 us -> none  [the longest x1 63.8 us: per_device(): lax.all_gather(shards[6], ('wide', 'narrow'), axis=0, tiled=True)]
    reduce_scatter x8 -> x0, waiting for transfers between devices: 299 us -> none  [the longest x6 277 us: per_device(): lax.psum_scatter(text_terms, 'wide', scatter_dimension=0, tiled=True)]
    pallas_call x0 -> x1, Pallas kernels: none -> 295 us  [layer_call(): pl.pallas_call(body, out_shape=[jax.ShapeDtypeStruct(shape, kind) for sha...]
    unnamed x20 -> x0, waiting for transfers between devices: 119 us -> none
    all_gather x12 -> x0, blocking collectives: 118 us -> none  [the longest x1 13.7 us: per_device(): lax.all_gather(cross_low, 'narrow', axis=0, tiled=True)]
    dot_general x33 -> x0, matrix products: 101 us -> none  [the longest x7 22.5 us: matmul(): return jnp.dot(left, right, preferred_element_type=jnp.float32)]
    unnamed x3 -> x0, blocking collectives: 92.1 us -> none
    reshape x21 -> x0, local copies, waits for them, and re-layouts: 56.5 us -> none  [the longest x2 14.2 us: per_device(): cross_k = memory[:, :width].reshape(groups, image_count, HEADS, head_size)]
  transfers between devices with their start and end apart: 19 -> 0, of which waited for: 13 -> 0; matrix products, arithmetic and copies ran while one was open for 14% -> 0% of each run, Pallas kernels for 0% -> 0%
where the time goes in v1:
time: 315 us; the launch traced here: 313 us
  Pallas kernels  295 us (94%)
  local copies, waits for them, and re-layouts  13.6 us (4%)
    pallas_call x1, Pallas kernels, layer_call(): pl.pallas_call(body, out_shape=[jax.ShapeDtypeStruct(shape, kind) for sha...  295 us
    unnamed x20, local copies, waits for them, and re-layouts  8.01 us

profile of v1, /device:TPU:1, one launch (start us, length us, event | category | flops | bytes accessed | tf_op | source)
XLA Modules:
  0.0 312.5 jit_solution(17765589114368473264)
XLA Ops:
  0.7 0.8 stack.39
  1.4 0.6 dynamic_update_slice.3.refs_6_
  2.0 0.8 slice_dynamic-update-slice_fusion.8
  2.8 0.8 slice_dynamic-update-slice_fusion.7
  3.6 0.8 constant_dynamic-update-slice_fusion.2
  4.4 0.8 slice_dynamic-update-slice_fusion.6
  5.2 0.8 constant_dynamic-update-slice_fusion
  6.0 0.8 slice_dynamic-update-slice_fusion.5
  6.8 0.8 slice_dynamic-update-slice_fusion.4
  7.5 0.0 copy-done.4
  7.5 0.8 pad_maximum_fusion.refs_4_
  8.4 295.3 %layer.1 = (bf16[128,768]{1,0:T(8,128)(2,1)}, bf16[128,768]{1,0:T(8,128)(2,1)}, bf16[1152,768]{1,0:T(8,128)(2,1)}, f32[12,24,768]{2,1,0:T(8,128)}, f32[96,768]{1,0:T(8,128)}, /*index=5*/f32[8,768]{1,0:T(8,128)}) custom-call(bf16[128,768]{1,0:T(8,128)(2,1)} %bitcast.62, bf16[1152,768]{1,0:T(8,128)(2,1)} %bitcast.61, s32[2]{0:T(128)} %refs_2_.1, ...), custom_call_target="tpu_custom_call" | custom-call | flops 16999999488 | bytes 8000000 | tf_op jit(solution)/shard_map/layer/pallas_call | solution.py:815
  303.6 0.0 copy-start.3
  303.7 0.8 constant_dynamic-slice_fusion
  304.5 0.5 slice_bitcast_fusion.12
  305.0 2.1 slice_bitcast_fusion.3
  307.1 0.7 pad_maximum_fusion.1
  307.9 0.7 pad_maximum_fusion.3
  308.5 0.7 pad_maximum_fusion.2
  309.2 0.7 copy.48
  309.9 0.7 copy.49
  310.6 1.2 copy.50
  311.8 0.0 copy-done.1
  311.8 0.7 copy.51
  (9 shorter events, 0.0 us)
Async XLA Ops:
  2.0 5.5 %copy-start.4 = (f32[8,768]{1,0:T(8,128)}, f32[8,768]{1,0:T(8,128)S(1)}, u32[]{:S(2)}) copy-start(f32[8,768]{1,0:T(8,128)S(1)} %dynamic_update_slice.3.refs_6_) | copy-start | bytes 73732
  303.6 5.6 %copy-start.3 = (bf16[128,768]{1,0:T(8,128)(2,1)S(1)}, bf16[128,768]{1,0:T(8,128)(2,1)}, u32[]{:S(2)}) copy-start(bf16[128,768]{1,0:T(8,128)(2,1)} %get-tuple-element.22) | copy-start | bytes 589828
  303.6 6.3 %copy-start.2 = (bf16[128,768]{1,0:T(8,128)(2,1)S(1)}, bf16[128,768]{1,0:T(8,128)(2,1)}, u32[]{:S(2)}) copy-start(bf16[128,768]{1,0:T(8,128)(2,1)} %get-tuple-element.23) | copy-start | bytes 589828
  305.0 5.6 %copy-start = (bf16[1152,768]{1,0:T(8,128)(2,1)S(1)}, bf16[1152,768]{1,0:T(8,128)(2,1)}, u32[]{:S(2)}) copy-start(bf16[1152,768]{1,0:T(8,128)(2,1)} %get-tuple-element.24) | copy-start | bytes 5308420
  310.6 1.2 copy-start.1

commit v2 on v1

v2 whole, which is shorter than its diff:
```python
import functools

import jax
import jax.numpy as jnp
from jax import lax
from jax.experimental import pallas as pl
from jax.experimental.pallas import tpu as pltpu
from jax.sharding import PartitionSpec as P

HEADS = 12
NODES = 32
UNITS = 11
MESH = pl.DeviceIdType.MESH
F32 = jnp.float32
LOW = jnp.bfloat16
EPSILON = 1e-05
GELU_A = 0.7978845608028654
GELU_B = 0.044715

QS, KS, VS, SO, CK, CV, CQ, CO, UP = 0, 1, 2, 3, 4, 5, 6, 7, 8
DOWN = UP + 1
GATHER = (256,) * 8
SCATTER = (256, 128, 256, 128, 256, 128, 256, 128)


def mm(left, right):
    return jnp.dot(left, right, preferred_element_type=F32)


def mm_bt(left, right):
    return lax.dot_general(left, right, (((1,), (1,)), ((), ())), preferred_element_type=F32)


def mm_at(left, right):
    return lax.dot_general(left, right, (((0,), (0,)), ((), ())), preferred_element_type=F32)


def norm(value, gain, shift):
    centred = value - jnp.mean(value, axis=-1, keepdims=True)
    rstd = lax.rsqrt(jnp.mean(centred * centred, axis=-1, keepdims=True) + EPSILON)
    hat = centred * rstd
    return hat, rstd, hat * gain + shift


def norm_pull(grad, hat, rstd, gain):
    scaled = grad * gain
    inner = jnp.mean(scaled * hat, axis=-1, keepdims=True)
    back = rstd * (scaled - jnp.mean(scaled, axis=-1, keepdims=True) - hat * inner)
    gain_grad = jnp.sum(grad * hat, axis=0, keepdims=True)
    shift_grad = jnp.sum(grad, axis=0, keepdims=True)
    return back, gain_grad, shift_grad


class Layer:
    def __init__(self, refs, lanes, narrow):
        self.__dict__.update(refs)
        self.N = narrow
        self.lanes = lanes
        wide, nar = lax.axis_index("wide"), lax.axis_index("narrow")
        flat = wide * narrow + nar
        self.wide, self.nar = wide, nar
        self.node = lax.div(flat, lanes)
        self.lane = lax.rem(flat, lanes)
        node = self.node
        self.c = lax.rem(node, 2)
        self.x = lax.rem(lax.div(node, 2), 2)
        self.y = lax.rem(lax.div(node, 4), 2)
        self.z = lax.div(node, 8)
        self.started = []
        self.count, self.seq = self.captions.shape[0] // 64, 64
        self.tokens, self.width = self.captions.shape
        self.groups = self.QA.shape[0]
        self.image_rows = self.images.shape[0] // self.groups
        self.pairs = self.width // 128
        lane = lax.broadcasted_iota(jnp.int32, (1, 128), 1)
        self.low_lanes = (lane < 64).astype(F32).astype(LOW)
        self.high_lanes = (lane >= 64).astype(F32).astype(LOW)
        self.is_first = lane < 64

    def device(self, z, y, x, c):
        flat = (z * 8 + y * 4 + x * 2 + c) * self.lanes + self.lane
        return (lax.div(flat, self.N), lax.rem(flat, self.N))

    def sibling(self):
        return self.device(self.z, self.y, self.x, 1 - self.c)

    def x_peer(self):
        return self.device(self.z, self.y, 1 - self.x, self.c)

    def y_peer(self):
        return self.device(self.z, 1 - self.y, self.x, self.c)

    def z_index(self, k):
        return lax.rem(self.z + k, 4)

    def z_peer(self, k):
        return self.device(self.z_index(k), self.y, self.x, self.c)

    def n_index(self, k):
        return lax.rem(self.nar + k, self.N)

    def n_peer(self, k):
        return (self.wide, self.n_index(k))

    def enter(self):
        barrier = pltpu.get_barrier_semaphore()
        peers = [self.sibling(), self.x_peer(), self.y_peer()]
        peers += [self.z_peer(k) for k in (1, 2, 3)]
        peers += [self.n_peer(k) for k in range(1, self.N)]
        for peer in peers:
            pl.semaphore_signal(barrier, inc=1, device_id=peer, device_id_type=MESH)
        pl.semaphore_wait(barrier, len(peers))

    def copy(self, src, dst, sems, where, peer):
        send, recv = sems
        return pltpu.make_async_remote_copy(
            src_ref=src,
            dst_ref=dst,
            send_sem=send.at[where],
            recv_sem=recv.at[where],
            device_id=peer,
            device_id_type=MESH,
        )

    def start(self, copies):
        for item in copies:
            item.start()
        self.started += copies

    def finish_sends(self):
        for item in self.started:
            item.wait_send()
        self.started = []

    def finish_early(self):
        for item in self.started[: self.gathered]:
            item.wait_send()
        self.started = self.started[self.gathered :]

    def part(self, unit, half, z, y, x, grad=False):
        every = slice(None)
        if unit < UP:
            first = (SCATTER if grad else GATHER)[unit]
            low, size = ((0, 384), (0, first), (first, 384 - first))[0 if half is None else half + 1]
            if grad and unit in (CK, CV):
                return self.CP.at[unit - CK, z, y, x, every, pl.ds(low, size)]
            columns = pl.ds(pl.multiple_of(384 * self.c + low, 128), size)
            return self.W.at[unit, z, y, x, every, columns]
        if unit == UP:
            return self.W.at[UP + self.c, z, y, x]
        ref = self.HG if grad else self.HD.at[self.c]
        return ref.at[z, x, pl.ds(96 * (unit - DOWN), 96)]

    def half_columns(self, c):
        return pl.ds(pl.multiple_of(384 * c, 128), 384)

    def shards(self):
        found = [(self.self_proj, self.width * j) for j in range(3)] + [(self.self_output, 0)]
        found += [(self.cross_memory, self.width * j) for j in range(2)]
        return found + [(self.cross_query, 0), (self.cross_output, 0)]

    def half_block(self, block, c):
        ref, start = self.shards()[block]
        return ref[:, pl.ds(pl.multiple_of(start + 384 * c, 128), 384)].astype(F32)

    def up_block(self, y, c):
        runs = []
        for j in range(2):
            start = self.width * (2 * c + j) + 384 * y
            runs.append(self.hidden_up[:, pl.ds(pl.multiple_of(start, 128), 384)].astype(F32))
        return jnp.concatenate(runs, axis=1)

    def pair_copies(self):
        c = self.c
        rows = pl.ds(pl.multiple_of(96 * c, 32), 96)
        there = self.HD.at[1 - c, self.z, self.x, rows]
        down = self.hidden_down.at[:, self.half_columns(1 - c)]
        return [
            self.copy(self.PA.at[0], self.PA.at[1], self.s_pair, 0, self.sibling()),
            self.copy(self.PB.at[0], self.PB.at[1], self.s_pair, 1, self.sibling()),
            self.copy(down, there, self.s_pair, 2, self.sibling()),
        ]

    def pair_pack(self):
        c = 1 - self.c
        blocks = [self.half_block(block, c) for block in range(UP)]
        self.PA[0] = jnp.concatenate(blocks, axis=0).astype(LOW)
        both = [self.up_block(y, c) for y in range(2)]
        self.PB[0] = jnp.concatenate(both, axis=0).astype(LOW)

    def in_order(self, mine, theirs):
        even = self.c == 0
        low, high = jnp.where(even, mine, theirs), jnp.where(even, theirs, mine)
        return jnp.concatenate([low, high], axis=0)

    def pair_merge(self):
        c = self.c
        copies = self.pair_copies()
        rows = pl.ds(pl.multiple_of(96 * c, 32), 96)
        self.HD[c, self.z, self.x, rows] = self.hidden_down[:, self.half_columns(c)]
        columns = pl.ds(pl.multiple_of(384 * c, 128), 384)
        copies[0].wait_recv()
        theirs = self.PA[1].astype(F32)
        for block in range(UP):
            both = self.in_order(self.half_block(block, c), theirs[24 * block : 24 * block + 24])
            self.W[block, self.z, self.y, self.x, :, columns] = both.astype(LOW)
        copies[1].wait_recv()
        theirs = self.PB[1].astype(F32)
        both = [self.in_order(self.up_block(y, c), theirs[24 * y : 24 * y + 24]) for y in range(2)]
        south = self.y == 0
        self.W[UP + c, self.z, self.y, self.x] = jnp.where(south, both[0], both[1]).astype(LOW)
        self.UPS[...] = jnp.where(south, both[1], both[0]).astype(LOW)
        copies[2].wait_recv()

    def up_copies(self):
        there = self.W.at[UP + self.c, self.z, self.y, self.x]
        return [self.copy(self.UPS, there, self.s_up, 0, self.y_peer())]

    def z_copies(self, unit):
        y = slice(None) if unit == UP else self.y
        here = self.part(unit, None, self.z, y, self.x)
        return [
            self.copy(here, here, self.s_z, (unit, k - 1), self.z_peer(k)) for k in (1, 2, 3)
        ]

    def two_copies(self, unit):
        every = slice(None)
        a = self.part(unit, 0, every, self.y, self.x)
        b = self.part(unit, 1, every, self.y, self.x)
        return [
            self.copy(a, a, self.s_two, (unit, 0), self.x_peer()),
            self.copy(b, b, self.s_two, (unit, 1), self.y_peer()),
        ]

    def three_copies(self, unit):
        every = slice(None)
        if unit >= UP:
            here = self.part(unit, None, every, every, self.x)
            return [self.copy(here, here, self.s_three, (unit, 0), self.x_peer())]
        a = self.part(unit, 0, every, self.y, every)
        b = self.part(unit, 1, every, every, self.x)
        return [
            self.copy(a, a, self.s_three, (unit, 0), self.y_peer()),
            self.copy(b, b, self.s_three, (unit, 1), self.x_peer()),
        ]

    def hand_copies(self, unit):
        every = slice(None)
        whole = self.part(unit, None, every, every, every)
        return [self.copy(whole, whole, self.s_hand, unit, self.sibling())]

    def arrived(self, copies):
        for item in copies:
            item.wait_recv()

    def first(self, unit):
        self.start(self.z_copies(unit))

    def second(self, unit):
        self.arrived(self.z_copies(unit))
        if unit < UP:
            self.start(self.two_copies(unit))

    def third(self, unit):
        if unit < UP:
            self.arrived(self.two_copies(unit))
        self.start(self.three_copies(unit))

    def hand(self, unit):
        self.arrived(self.three_copies(unit))
        self.start(self.hand_copies(unit))

    def done(self, unit):
        self.arrived(self.hand_copies(unit))

    def term(self, unit, half, z=slice(None)):
        first = SCATTER[unit]
        return (unit, z, ..., pl.ds(*((0, first), (first, 384 - first))[half]))

    def rs_one_copies(self, unit):
        every = slice(None)
        if unit >= UP:
            here = self.part(unit, None, every, every, 1 - self.x, grad=True)
            there = self.RU1 if unit == UP else self.RH1.at[unit - DOWN]
            return [self.copy(here, there, self.s_rs1, (unit, 0), self.x_peer())]
        a = self.part(unit, 0, every, 1 - self.y, every, grad=True)
        b = self.part(unit, 1, every, every, 1 - self.x, grad=True)
        return [
            self.copy(a, self.R1.at[self.term(unit, 0)], self.s_rs1, (unit, 0), self.y_peer()),
            self.copy(b, self.R1.at[self.term(unit, 1)], self.s_rs1, (unit, 1), self.x_peer()),
        ]

    def rs_two_copies(self, unit):
        every = slice(None)
        a = self.part(unit, 0, every, self.y, 1 - self.x, grad=True)
        b = self.part(unit, 1, every, 1 - self.y, self.x, grad=True)
        return [
            self.copy(a, self.R2.at[self.term(unit, 0)], self.s_rs2, (unit, 0), self.x_peer()),
            self.copy(b, self.R2.at[self.term(unit, 1)], self.s_rs2, (unit, 1), self.y_peer()),
        ]

    def rs_three_copies(self, unit):
        out = []
        y = slice(None) if unit == UP else self.y
        for k in (1, 2, 3):
            here = self.part(unit, None, self.z_index(k), y, self.x, grad=True)
            if unit < UP:
                there = self.R3.at[unit, k - 1]
            elif unit == UP:
                there = self.RU3.at[k - 1]
            else:
                there = self.RH3.at[unit - DOWN, k - 1]
            out.append(self.copy(here, there, self.s_rs3, (unit, k - 1), self.z_peer(k)))
        return out

    def up_back_copies(self):
        return [self.copy(self.UPS, self.UPR, self.s_up, 1, self.y_peer())]

    def grad_columns(self, block):
        return pl.ds(pl.multiple_of(self.width * block + 384 * self.c, 128), 384)

    def rs_four_copies(self, unit):
        c = self.c
        if unit < UP:
            there = self.block_grad.at[:, self.grad_columns(unit)]
            return [self.copy(self.SF.at[unit], there, self.s_rs4, unit, self.sibling())]
        if unit == UP:
            out = []
            for i in range(2):
                for h in range(2):
                    there = self.block_grad.at[:, self.up_columns(i, h)]
                    here = self.SFU.at[i, :, pl.ds(384 * h, 384)]
                    out.append(self.copy(here, there, self.s_rs5, (i, h), self.sibling()))
            return out
        there = self.down_out.at[:, self.half_columns(c)]
        return [self.copy(self.SFH, there, self.s_rs4, unit, self.sibling())]

    def up_columns(self, i, h):
        y = self.y if i == 0 else 1 - self.y
        start = self.width * (UP + 2 * self.c + h) + 384 * y
        return pl.ds(pl.multiple_of(start, 128), 384)

    def add_into(self, ref, term):
        ref[...] = (ref[...].astype(F32) + term.astype(F32)).astype(LOW)

    def rs_one(self, unit):
        self.start(self.rs_one_copies(unit))

    def rs_two(self, unit):
        self.arrived(self.rs_one_copies(unit))
        every = slice(None)

        @pl.loop(0, 4)
        def _(z):
            if unit < UP:
                a, b = self.R1[self.term(unit, 0, z)], self.R1[self.term(unit, 1, z)]
                self.add_into(self.part(unit, 0, z, self.y, every, grad=True), a)
                self.add_into(self.part(unit, 1, z, every, self.x, grad=True), b)
            else:
                more = self.RU1[z] if unit == UP else self.RH1[unit - DOWN, z]
                self.add_into(self.part(unit, None, z, every, self.x, grad=True), more)

        if unit < UP:
            self.start(self.rs_two_copies(unit))
        else:
            self.start(self.rs_three_copies(unit))

    def rs_three(self, unit):
        self.arrived(self.rs_two_copies(unit))

        @pl.loop(0, 4)
        def _(z):
            a, b = self.R2[self.term(unit, 0, z)], self.R2[self.term(unit, 1, z)]
            self.add_into(self.part(unit, 0, z, self.y, self.x, grad=True), a)
            self.add_into(self.part(unit, 1, z, self.y, self.x, grad=True), b)

        self.start(self.rs_three_copies(unit))

    def rs_total(self, unit):
        self.arrived(self.rs_three_copies(unit))
        y = slice(None) if unit == UP else self.y
        total = self.part(unit, None, self.z, y, self.x, grad=True)[...].astype(F32)
        for k in range(3):
            if unit < UP:
                more = self.R3[unit, k]
            else:
                more = self.RU3[k] if unit == UP else self.RH3[unit - DOWN, k]
            total = total + more.astype(F32)
        return total

    def rs_four(self, unit):
        even = self.c == 0
        if unit < UP:
            total = self.rs_total(unit)
            low, high = total[:24], total[24:]
            self.block_grad[:, self.grad_columns(unit)] = jnp.where(even, low, high)
            self.SF[unit] = jnp.where(even, high, low)
            self.start(self.rs_four_copies(unit))
        if unit == UP:
            total = self.rs_total(unit)
            south = self.y == 0
            self.UPS[...] = jnp.where(south, total[1], total[0]).astype(LOW)
            self.start(self.up_back_copies())
            self.up_rows(0, jnp.where(south, total[0], total[1]))
        if unit == DOWN + 1:
            low, high = self.rs_total(DOWN), self.rs_total(DOWN + 1)
            self.down_out[:, self.half_columns(self.c)] = jnp.where(even, low, high)
            self.SFH[...] = jnp.where(even, high, low)
            self.start(self.rs_four_copies(DOWN + 1))

    def up_rows(self, i, total):
        even = self.c == 0
        low, high = total[:24], total[24:]
        own = jnp.where(even, low, high)
        for h in range(2):
            self.block_grad[:, self.up_columns(i, h)] = own[:, 384 * h : 384 * h + 384]
        self.SFU[i] = jnp.where(even, high, low)

    def rs_up(self):
        self.arrived(self.up_back_copies())
        self.up_rows(1, self.UPR[...].astype(F32))
        self.start(self.rs_four_copies(UP))

    def rs_done(self, unit):
        if unit != DOWN:
            self.arrived(self.rs_four_copies(unit))

    def sum_copies(self, which, stage):
        peers = [[self.sibling()], [self.x_peer()], [self.y_peer()]]
        peers += [[self.z_peer(k) for k in (1, 2, 3)]]
        return [
            self.copy(
                self.V.at[which, stage],
                self.VR.at[which, stage + i],
                self.s_vec,
                (which, stage + i),
                peer,
            )
            for i, peer in enumerate(peers[stage])
        ]

    def placement(self, dtype):
        own = self.width // NODES
        at = lax.broadcasted_iota(jnp.int32, (128, self.width), 0)
        feature = lax.broadcasted_iota(jnp.int32, (128, self.width), 1)
        return ((at < own) & (feature == at + own * self.node)).astype(F32).astype(dtype)

    def sum_start(self, which, stage, value):
        self.V[which, stage] = value
        self.start(self.sum_copies(which, stage))

    def sum_end(self, which, stage):
        now = self.sum_copies(which, stage)
        self.arrived(now)
        value = self.V[which, stage]
        for i in range(len(now)):
            value = value + self.VR[which, stage + i]
        return value

    def keep_left(self, place, value):
        self.LHS[place, self.c] = value
        here = self.LHS.at[place, self.c]
        self.start([self.copy(here, here, self.s_left, place, self.sibling())])

    def keep_right(self, place, value):
        self.RHS[place, self.c] = value
        here = self.RHS.at[place, self.c]
        self.start([self.copy(here, here, self.s_right, place, self.sibling())])

    def left_arrived(self, place):
        here = self.LHS.at[place, self.c]
        self.copy(here, here, self.s_left, place, self.sibling()).wait_recv()

    def right_arrived(self, place):
        here = self.RHS.at[place, self.c]
        self.copy(here, here, self.s_right, place, self.sibling()).wait_recv()

    def weight(self, block):
        return self.W[block].reshape(self.width, self.width)

    def weight_grad(self, unit):
        left, right = {QS: (0, 0), KS: (0, 1), VS: (0, 2), SO: (1, 3), CQ: (2, 4), CO: (3, 5)}[unit]
        columns = self.half_columns(self.c)
        right_all = self.RHS[right, :, :, columns].reshape(2 * self.tokens, 384)
        for t in range(2):
            left_all = self.LHS[left, :, :, pl.ds(384 * t, 384)].reshape(2 * self.tokens, 384)
            part = mm_at(left_all, right_all).astype(LOW)
            self.W[unit, pl.ds(2 * t, 2), :, :, :, columns] = part.reshape(2, 2, 2, 48, 384)

    def up_grad(self):
        c = self.c
        right_all = self.DH[c].reshape(4 * self.tokens, self.width)
        for t in range(2):
            left_all = self.A3[:, :, :, pl.ds(384 * t, 384)].reshape(4 * self.tokens, 384)
            part = mm_at(left_all, right_all).astype(LOW)
            self.W[UP + c, pl.ds(2 * t, 2)] = part.reshape(2, 2, 2, 48, self.width)

    def down_grad(self):
        right_all = self.G4[:, :, :, self.half_columns(self.c)].reshape(4 * self.tokens, 384)
        for z in range(4):
            j, t = z // 2, z % 2
            left_all = self.U[j, :, :, :, pl.ds(384 * t, 384)].reshape(4 * self.tokens, 384)
            part = mm_at(left_all, right_all).astype(LOW)
            self.HG[z] = part.reshape(2, 192, 384)

    def memory_copy(self, which):
        return self.copy(
            self.CS.at[which], self.CM.at[which], self.s_memory, which, self.sibling()
        )

    def memory_term(self, which, c, t):
        left = self.IMG[:, pl.ds(384 * t, 384)]
        part = mm_at(left, self.KV[which, :, self.half_columns(c)])
        return part.reshape(2, 2, 2, 48, 384)

    def memory_grad_other(self, which):
        for t in range(2):
            part = self.memory_term(which, 1 - self.c, t)
            self.CS[which, pl.ds(2 * t, 2)] = part.astype(LOW)
        self.start([self.memory_copy(which)])

    def memory_grad_own(self, which):
        self.memory_copy(which).wait_recv()
        for t in range(2):
            part = self.memory_term(which, self.c, t)
            part = part + self.CM[which, pl.ds(2 * t, 2)].astype(F32)
            self.CP[which, pl.ds(2 * t, 2)] = part.astype(LOW)

    def masked(self, value):
        return value * self.low_lanes, value * self.high_lanes

    def self_attention(self):
        rows = lax.broadcasted_iota(jnp.int32, (128, 128), 0)
        cols = lax.broadcasted_iota(jnp.int32, (128, 128), 1)
        length = jnp.where(cols < 64, self.lengths[0], self.lengths[1])
        allowed = (lax.div(rows, 64) == lax.div(cols, 64)) & (cols <= rows)
        allowed = allowed & (lax.rem(cols, 64) < length)
        parts = []
        for p in range(self.pairs):
            at = slice(128 * p, 128 * p + 128)
            q, k, v = self.QKV[0, :, at], self.QKV[1, :, at], self.QKV[2, :, at]
            total = None
            for h, (qm, vm) in enumerate(zip(self.masked(q), self.masked(v))):
                s = mm_bt(qm, k) * 0.125
                s = jnp.where(allowed, s, -1000000000.0)
                e = jnp.exp(s - jnp.max(s, axis=-1, keepdims=True))
                prob = e / jnp.sum(e, axis=-1, keepdims=True)
                self.PS[2 * p + h] = prob
                out = mm(prob.astype(LOW), vm)
                total = out if total is None else total + out
            parts.append(total.astype(LOW))
        return jnp.concatenate(parts, axis=1)

    def self_attention_back(self, grad):
        parts = ([], [], [])
        for p in range(self.pairs):
            at = slice(128 * p, 128 * p + 128)
            q, k, v = self.QKV[0, :, at], self.QKV[1, :, at], self.QKV[2, :, at]
            g = grad[:, at]
            dq = dk = dv = 0.0
            for h, (qm, km, gm) in enumerate(
                zip(self.masked(q), self.masked(k), self.masked(g))
            ):
                prob = self.PS[2 * p + h]
                dp = mm_bt(gm, v)
                ds = prob * (dp - jnp.sum(prob * dp, axis=-1, keepdims=True))
                ds = ds.astype(LOW)
                dq = dq + mm(ds, km)
                dk = dk + mm_at(ds, qm)
                dv = dv + mm_at(prob.astype(LOW), gm)
            for out, item in zip(parts, (dq * 0.125, dk * 0.125, dv)):
                out.append(item.astype(LOW))
        return [jnp.concatenate(item, axis=1) for item in parts]

    def stacked(self, value):
        a, b = self.masked(value)
        return jnp.concatenate([a, b], axis=0)

    def diagonal(self, value):
        return jnp.where(self.is_first, value[:64], value[64:])

    def memory_forward(self, which):
        w = self.weight(CK + which)

        @pl.loop(0, 3)
        def _(t):
            size = self.images.shape[0] // 3
            rows = pl.ds(pl.multiple_of(size * t, 16), size)
            self.KV[which, rows] = mm(self.IMG[rows], w).astype(LOW)

    def cross_forward(self, place):
        rows = pl.ds(pl.multiple_of(place * self.image_rows, 16), self.image_rows)
        for p in range(self.pairs):
            at = slice(128 * p, 128 * p + 128)
            k, v = self.KV[0, rows, at], self.KV[1, rows, at]
            q = self.stacked(self.QA[place, :, at])
            s = mm_bt(k, q) * 0.125
            top = jnp.max(s, axis=0, keepdims=True)
            e = jnp.exp(s - top)
            low = e.astype(LOW)
            self.E[place, p] = low
            self.ST[place, p : p + 1] = jnp.sum(e, axis=0, keepdims=True)
            self.ST[place, 8 + p : 9 + p] = top
            self.TOP[place, p : p + 1] = top
            num = mm_at(low, v)
            self.NUM[place, :, at] = self.diagonal(num).astype(LOW)
        self.ST[place, 6:8] = jnp.ones((2, 128), F32)
        self.ST[place, 14:16] = jnp.zeros((2, 128), F32)

    def cross_backward(self, place):
        rows = pl.ds(pl.multiple_of(place * self.image_rows, 16), self.image_rows)
        for p in range(self.pairs):
            at = slice(128 * p, 128 * p + 128)
            k, v = self.KV[0, rows, at], self.KV[1, rows, at]
            q = self.stacked(self.QA[place, :, at])
            g = self.stacked(self.GA[place, :, at])
            share = jnp.exp(self.TOP[place, p : p + 1] - self.DL[place, 8 + p : 9 + p])
            e = self.E[place, p].astype(F32) * share
            ds = e * (mm_bt(v, g) + self.DL[place, p : p + 1])
            ds = ds.astype(LOW)
            dq = mm_at(ds, k)
            self.NUM[place, :, at] = (self.diagonal(dq) * 0.125).astype(LOW)
            self.KV[0, rows, at] = (mm(ds, q) * 0.125).astype(LOW)
            self.KV[1, rows, at] = mm(e.astype(LOW), g).astype(LOW)

    def captions_of(self, owner):
        return pl.ds(owner * self.count, self.count)

    def partner(self, bit):
        return (self.wide, jnp.bitwise_xor(self.nar, bit))

    def owner(self, bits):
        return jnp.bitwise_xor(self.nar, bits)

    def share_copies(self, ref, sems, bit, bits):
        here = ref.at[self.captions_of(self.owner(bits))]
        return self.copy(here, here, sems, (self.N + bits) // (2 * bit) - 1, self.partner(bit))

    def share_steps(self):
        bit = self.N // 2
        while bit:
            yield bit, range(0, self.N, 2 * bit)
            bit //= 2

    def share_start(self, refs):
        for bit, held in self.share_steps():
            self.start([self.share_copies(ref, sems, bit, 0) for ref, sems in refs])

    def share_end(self, refs):
        for bit, held in self.share_steps():
            for bits in held:
                if bits:
                    self.start([self.share_copies(ref, sems, bit, bits) for ref, sems in refs])
            for bits in held:
                self.arrived([self.share_copies(ref, sems, bit, bits) for ref, sems in refs])

    def merge_slot(self, bit, bits):
        return self.N - self.N // bit + bits // (2 * bit)

    def merge_copies(self, refs, bit, bits):
        slot = self.merge_slot(bit, bits)
        owner = self.captions_of(self.owner(bits + bit))
        return [
            self.copy(ref.at[owner], there.at[slot], sems, slot, self.partner(bit))
            for ref, there, sems in refs
        ]

    def merge_steps(self):
        bit = 1
        while bit < self.N:
            yield bit, range(0, self.N, 2 * bit)
            bit *= 2

    def merge_start(self, refs):
        for bits in range(0, self.N, 2):
            self.start(self.merge_copies(refs, 1, bits))

    def merge_end(self, refs, join):
        for bit, kept in self.merge_steps():
            for bits in reversed(kept):
                self.arrived(self.merge_copies(refs, bit, bits))
                for j in range(self.count):
                    join(self.owner(bits) * self.count + j, self.merge_slot(bit, bits), j)
                if bits % (4 * bit):
                    self.start(self.merge_copies(refs, 2 * bit, bits - 2 * bit))

    def column(self, turned, p):
        return jnp.where(self.is_first, turned[:64, p : p + 1], turned[64:, p : p + 1])

    def turn(self, *rows):
        have = 8 * len(rows)
        return jnp.concatenate([*rows, jnp.zeros((128 - have, 128), F32)], axis=0).T

    def join_softmax(self, place, slot, j):
        total_a, top_a = self.ST[place, :8], self.ST[place, 8:]
        total_b, top_b = self.STR[slot, j, :8], self.STR[slot, j, 8:]
        top = jnp.maximum(top_a, top_b)
        share_a, share_b = jnp.exp(top_a - top), jnp.exp(top_b - top)
        self.ST[place, :8] = share_a * total_a + share_b * total_b
        self.ST[place, 8:] = top
        turned = self.turn(share_a, share_b)
        for p in range(self.pairs):
            at = slice(128 * p, 128 * p + 128)
            a = self.NUM[place, :, at].astype(F32) * self.column(turned, p)
            b = self.NUMR[slot, j, :, at].astype(F32) * self.column(turned, 8 + p)
            self.NUM[place, :, at] = (a + b).astype(LOW)

    def join_sum(self, place, slot, j):
        self.add_into(self.NUM.at[place], self.NUMR[slot, j])

    def attended(self):
        done = []
        for j in range(self.count):
            place = self.nar * self.count + j
            turned = self.turn(1.0 / self.ST[place, :8])
            self.SCT[j] = turned
            parts = []
            for p in range(self.pairs):
                at = slice(128 * p, 128 * p + 128)
                parts.append(self.NUM[place, :, at].astype(F32) * self.column(turned, p))
            done.append(jnp.concatenate(parts, axis=1))
        return jnp.concatenate(done, axis=0)

    def spread_grad(self, doc):
        lane = lax.broadcasted_iota(jnp.int32, (128, 128), 1)
        for j in range(self.count):
            place = self.nar * self.count + j
            rows = slice(64 * j, 64 * j + 64)
            turned = self.SCT[j]
            inner = jnp.zeros((128, 128), F32)
            for p in range(self.pairs):
                at = slice(128 * p, 128 * p + 128)
                part = doc[rows, at] * self.column(turned, p)
                self.GA[place, :, at] = part.astype(LOW)
                prod = part * self.OCF[rows, at]
                a = jnp.sum(jnp.where(self.is_first, prod, 0.0), axis=1, keepdims=True)
                b = jnp.sum(jnp.where(self.is_first, 0.0, prod), axis=1, keepdims=True)
                inner = jnp.where(lane == p, jnp.concatenate([a, b], axis=0), inner)
            self.DL[place, :8] = -inner.T[:8]
            self.DL[place, 8:] = self.ST[place, 8:]

    def weight_images(self):
        return pltpu.make_async_copy(self.images, self.IMG, self.s_image[0].at[0])

    def keep_wide(self, ref, value, sems):
        ref[self.c, self.y] = value
        here = ref.at[self.c, self.y]
        self.start([self.copy(here, here, sems, 0, self.y_peer())])
        self.start([self.copy(here, here, sems, 1, self.sibling())])

    def wide_across(self, ref, sems):
        here = ref.at[self.c, self.y]
        self.copy(here, here, sems, 0, self.y_peer()).wait_recv()
        here = ref.at[self.c, 1 - self.y]
        self.start([self.copy(here, here, sems, 2, self.sibling())])

    def wide_arrived(self, ref, sems):
        for i in (1, 2):
            here = ref.at[self.c, self.y]
            self.copy(here, here, sems, i, self.sibling()).wait_recv()

    def hidden_copy(self, ref, j, sems):
        here = ref.at[j, self.c]
        return self.copy(here, here, sems, j, self.sibling())

    def fold_copy(self, which):
        return self.copy(self.FS.at[which], self.FR.at[which], self.s_fold, which, self.y_peer())

    def run(self):
        tokens, width, count = self.tokens, self.width, self.count
        image_copy = pltpu.make_async_copy(self.images, self.IMG, self.s_image[0].at[0])
        image_copy.start()
        self.pair_pack()
        self.enter()
        self.start(self.pair_copies())
        self.sum_start(0, 0, mm(self.vec[...], self.placement(LOW)))
        self.pair_merge()
        self.first(CK)
        self.start(self.up_copies())
        self.sum_start(0, 1, self.sum_end(0, 0))
        inputs = self.captions[...].astype(F32)
        self.second(CK)
        self.first(CV)
        self.first(QS)
        self.sum_start(0, 2, self.sum_end(0, 1))
        self.third(CK)
        self.second(CV)
        self.first(KS)
        self.sum_start(0, 3, self.sum_end(0, 2))
        self.hand(CK)
        self.third(CV)
        self.second(QS)
        self.first(VS)
        image_copy.wait()
        self.hand(CV)
        self.third(QS)
        self.second(KS)
        self.first(SO)
        self.done(CK)
        self.memory_forward(0)
        self.hand(QS)
        self.third(KS)
        self.second(VS)
        self.first(CQ)
        self.first(DOWN)
        self.done(CV)
        self.memory_forward(1)
        vectors = self.sum_end(0, 3)
        gain1, shift1 = vectors[0:1], vectors[1:2]
        gain2, shift2 = vectors[2:3], vectors[3:4]
        gain3, shift3 = vectors[4:5], vectors[5:6]
        hat1, rstd1, a1 = norm(inputs, gain1, shift1)
        self.HAT[0] = hat1
        a1 = a1.astype(LOW)
        self.keep_left(0, a1)
        self.hand(KS)
        self.third(VS)
        self.second(SO)
        self.first(CO)
        self.done(QS)
        self.QKV[0] = mm(a1, self.weight(QS)).astype(LOW)
        self.hand(VS)
        self.third(SO)
        self.second(CQ)
        self.second(DOWN)
        self.third(DOWN)
        self.first(DOWN + 1)
        self.done(KS)
        self.QKV[1] = mm(a1, self.weight(KS)).astype(LOW)
        self.hand(SO)
        self.third(CQ)
        self.second(CO)
        self.arrived(self.up_copies())
        self.first(UP)
        self.keep_wide(self.G4, self.out_grad[...], self.s_g4)
        self.done(VS)
        self.QKV[2] = mm(a1, self.weight(VS)).astype(LOW)
        mixed = self.self_attention()
        self.keep_left(1, mixed)
        self.hand(CQ)
        self.third(CO)
        self.hand(DOWN)
        self.second(DOWN + 1)
        self.third(DOWN + 1)
        self.done(SO)
        r1 = inputs + mm(mixed, self.weight(SO))
        hat2, rstd2, a2 = norm(r1, gain2, shift2)
        self.HAT[1] = hat2
        a2 = a2.astype(LOW)
        self.keep_left(2, a2)
        self.done(CQ)
        self.QA[self.captions_of(self.nar)] = (
            mm(a2, self.weight(CQ)).astype(LOW).reshape(count, 64, width)
        )
        queries = [(self.QA, self.s_query)]
        self.share_start(queries)
        self.hand(CO)
        self.wide_across(self.G4, self.s_g4)
        self.second(UP)
        self.third(UP)
        self.share_end(queries)
        pl.loop(0, self.groups)(self.cross_forward)
        numbers = [(self.NUM, self.NUMR, self.s_num), (self.ST, self.STR, self.s_st)]
        self.merge_start(numbers)
        self.hand(DOWN + 1)
        self.done(CO)
        self.done(DOWN)
        self.merge_end(numbers, self.join_softmax)
        full = self.attended()
        self.OCF[...] = full
        oc = full.astype(LOW)
        self.keep_left(3, oc)
        r2 = r1 + mm(oc, self.weight(CO))
        hat3, rstd3, a3 = norm(r2, gain3, shift3)
        self.HAT[2] = hat3
        self.keep_wide(self.A3, a3.astype(LOW), self.s_a3)
        self.hand(UP)
        self.done(DOWN + 1)
        self.wide_arrived(self.G4, self.s_g4)
        grad = self.G4[self.c].reshape(2 * tokens, width)
        self.done(UP)
        self.wide_across(self.A3, self.s_a3)
        a3 = self.A3[self.c].reshape(2 * tokens, width)
        for j in range(2):
            hidden = mm(a3, self.weight(UP + j))
            square = hidden * hidden
            tanh = jnp.tanh(GELU_A * hidden * (1.0 + GELU_B * square))
            act = (0.5 * hidden * (1.0 + tanh)).astype(LOW)
            slope = 0.5 * (1.0 + tanh) + 0.5 * hidden * (1.0 - tanh * tanh) * (
                GELU_A * (1.0 + 3.0 * GELU_B * square)
            )
            self.SLOPE[j] = slope
            self.U[j, self.c] = act.reshape(2, tokens, width)
            self.start([self.hidden_copy(self.U, j, self.s_u)])
        self.wide_arrived(self.A3, self.s_a3)
        for j in range(2):
            self.hidden_copy(self.U, j, self.s_u).wait_recv()
        self.gathered = len(self.started)
        self.down_grad()
        self.rs_one(DOWN)
        self.rs_one(DOWN + 1)
        e3 = 0.0
        for j in range(2):
            down = [self.HD[i, 2 * j : 2 * j + 2].reshape(width, 384) for i in range(2)]
            back = mm_bt(grad[:, :384], down[0]) + mm_bt(grad[:, 384:], down[1])
            dhp = (back * self.SLOPE[j]).astype(LOW)
            self.DH[j, self.c] = dhp.reshape(2, tokens, width)
            self.start([self.hidden_copy(self.DH, j, self.s_dh)])
            e3 = e3 + mm_bt(dhp, self.weight(UP + j))
        south = self.y == 0
        self.FS[0] = jnp.where(south, e3[tokens:], e3[:tokens]).astype(LOW)
        self.start([self.fold_copy(0)])
        e3 = jnp.where(south, e3[:tokens], e3[tokens:])
        out = [0.0, 0.0]
        for j in range(2):
            act = self.U[j, self.c].reshape(2 * tokens, width)
            for i in range(2):
                out[i] = out[i] + mm(act, self.HD[i, 2 * j : 2 * j + 2].reshape(width, 384))
        out = jnp.concatenate(out, axis=1)
        self.FS[1] = jnp.where(south, out[tokens:], out[:tokens]).astype(LOW)
        self.start([self.fold_copy(1)])
        out = r2 + jnp.where(south, out[:tokens], out[tokens:])
        for j in range(2):
            self.hidden_copy(self.DH, j, self.s_dh).wait_recv()
        self.finish_early()
        self.up_grad()
        self.rs_one(UP)
        self.fold_copy(0).wait_recv()
        e3 = e3 + self.FR[0].astype(F32)
        back3, gain3_grad, shift3_grad = norm_pull(e3, self.HAT[2], rstd3, gain3)
        dr2 = self.out_grad[...].astype(F32) + back3
        dcat = dr2.astype(LOW)
        self.keep_right(5, dcat)
        self.spread_grad(mm_bt(dcat, self.weight(CO)))
        grads = [(self.GA, self.s_g), (self.DL, self.s_dl)]
        self.share_start(grads)
        self.left_arrived(3)
        self.right_arrived(5)
        self.weight_grad(CO)
        self.rs_one(CO)
        self.rs_two(DOWN)
        self.rs_two(DOWN + 1)
        self.fold_copy(1).wait_recv()
        self.layer_out[...] = (out + self.FR[1].astype(F32)).astype(LOW)
        self.share_end(grads)
        pl.loop(0, self.groups)(self.cross_backward)
        back = [(self.NUM, self.NUMR, self.s_dq)]
        self.merge_start(back)
        self.memory_grad_other(0)
        self.memory_grad_other(1)
        self.rs_two(UP)
        self.rs_two(CO)
        self.memory_grad_own(0)
        self.rs_one(CK)
        self.memory_grad_own(1)
        self.rs_one(CV)
        self.rs_four(DOWN + 1)
        self.merge_end(back, self.join_sum)
        dqc = self.NUM[self.captions_of(self.nar)].reshape(tokens, width)
        self.keep_right(4, dqc)
        back2, gain2_grad, shift2_grad = norm_pull(
            mm_bt(dqc, self.weight(CQ)), self.HAT[1], rstd2, gain2
        )
        dr1 = dr2 + back2
        dattn = dr1.astype(LOW)
        self.keep_right(3, dattn)
        dos = mm_bt(dattn, self.weight(SO)).astype(LOW)
        self.rs_three(CO)
        self.left_arrived(2)
        self.right_arrived(4)
        self.weight_grad(CQ)
        self.rs_one(CQ)
        self.left_arrived(1)
        self.right_arrived(3)
        self.weight_grad(SO)
        self.rs_one(SO)
        self.rs_two(CK)
        self.rs_two(CV)
        e1 = 0.0
        for j, item in enumerate(self.self_attention_back(dos)):
            self.keep_right(j, item)
            e1 = e1 + mm_bt(item, self.weight(j))
        back1, gain1_grad, shift1_grad = norm_pull(e1, self.HAT[0], rstd1, gain1)
        self.input_grad[...] = (dr1 + back1).astype(LOW)
        self.left_arrived(0)
        for place, unit in enumerate((QS, KS, VS)):
            self.right_arrived(place)
            self.weight_grad(unit)
            self.rs_one(unit)
        vec = [gain1_grad, shift1_grad, gain2_grad, shift2_grad, gain3_grad, shift3_grad]
        vec = jnp.concatenate(vec + [jnp.zeros((2, width), F32)], axis=0)
        self.sum_start(1, 0, vec)
        self.rs_four(UP)
        self.rs_two(CQ)
        self.rs_three(CK)
        self.rs_four(CO)
        self.sum_start(1, 1, self.sum_end(1, 0))
        self.rs_two(SO)
        self.rs_three(CV)
        self.rs_up()
        self.sum_start(1, 2, self.sum_end(1, 1))

        @pl.loop(0, 3)
        def _(t):
            size = self.images.shape[0] // 3
            rows = pl.ds(pl.multiple_of(size * t, 16), size)
            part = mm_bt(self.KV[0, rows], self.weight(CK))
            part = part + mm_bt(self.KV[1, rows], self.weight(CV))
            self.IMG[rows] = part.astype(LOW)

        image_copy = pltpu.make_async_copy(self.IMG, self.image_grad, self.s_image[0].at[0])
        image_copy.start()
        self.rs_two(QS)
        self.rs_three(CQ)
        self.rs_four(CK)
        self.sum_start(1, 3, self.sum_end(1, 2))
        self.rs_two(KS)
        self.rs_three(SO)
        self.rs_four(CV)
        self.rs_two(VS)
        self.rs_three(QS)
        self.rs_four(CQ)
        self.rs_three(KS)
        self.rs_four(SO)
        self.rs_three(VS)
        self.rs_four(QS)
        total = self.sum_end(1, 3)
        self.vec_grad[...] = lax.dot_general(
            total,
            self.placement(F32),
            (((1,), (1,)), ((), ())),
            precision=lax.Precision.HIGHEST,
            preferred_element_type=F32,
        )
        self.rs_four(KS)
        self.rs_four(VS)
        for unit in range(UNITS):
            self.rs_done(unit)
        image_copy.wait()
        self.finish_sends()


def layer_call(lanes, narrow, captions, images, lengths, out_grad, vec, *weights):
    tokens, width = captions.shape
    count = tokens // 64
    groups = narrow * count
    image_rows = images.shape[0]
    pairs = width // 128
    ins = ["captions", "images", "lengths", "out_grad", "vec", "self_proj", "self_output"]
    ins += ["cross_query", "cross_memory", "cross_output", "hidden_up", "hidden_down"]
    outs = {
        "layer_out": ((tokens, width), LOW),
        "input_grad": ((tokens, width), LOW),
        "image_grad": ((image_rows, width), LOW),
        "block_grad": ((24, 12 * width), F32),
        "down_out": ((96, width), F32),
        "vec_grad": ((8, 128), F32),
    }
    memory = {
        "W": ((10, 4, 2, 2, 48, width), LOW),
        "HD": ((2, 4, 2, 192, 384), LOW),
        "HG": ((4, 2, 192, 384), LOW),
        "UPS": ((48, width), LOW),
        "UPR": ((48, width), LOW),
        "PA": ((2, 24 * UP, 384), LOW),
        "PB": ((2, 48, width), LOW),
        "IMG": ((image_rows, width), LOW),
        "KV": ((2, image_rows, width), LOW),
        "E": ((groups, pairs, image_rows // groups, 128), LOW),
        "LHS": ((4, 2, tokens, width), LOW),
        "RHS": ((6, 2, tokens, width), LOW),
        "A3": ((2, 2, tokens, width), LOW),
        "G4": ((2, 2, tokens, width), LOW),
        "U": ((2, 2, 2, tokens, width), LOW),
        "DH": ((2, 2, 2, tokens, width), LOW),
        "FS": ((2, tokens, width), LOW),
        "FR": ((2, tokens, width), LOW),
        "R1": ((UP, 4, 2, 48, 384), LOW),
        "R2": ((UP, 4, 48, 384), LOW),
        "R3": ((UP, 3, 48, 384), LOW),
        "RU1": ((4, 2, 48, width), LOW),
        "RU3": ((3, 2, 48, width), LOW),
        "RH1": ((2, 4, 96, 384), LOW),
        "RH3": ((2, 3, 96, 384), LOW),
        "CM": ((2, 4, 2, 2, 48, 384), LOW),
        "CS": ((2, 4, 2, 2, 48, 384), LOW),
        "CP": ((2, 4, 2, 2, 48, 384), LOW),
        "SF": ((UP, 24, 384), F32),
        "SFU": ((2, 24, width), F32),
        "SFH": ((96, 384), F32),
        "V": ((2, 4, 8, width), F32),
        "VR": ((2, 6, 8, width), F32),
        "QKV": ((3, tokens, width), LOW),
        "PS": ((HEADS, 128, 128), F32),
        "HAT": ((3, tokens, width), F32),
        "SLOPE": ((2, 2 * tokens, width), F32),
        "OCF": ((tokens, width), F32),
        "QA": ((groups, 64, width), LOW),
        "NUM": ((groups, 64, width), LOW),
        "ST": ((groups, 16, 128), F32),
        "TOP": ((groups, 8, 128), F32),
        "NUMR": ((narrow - 1, count, 64, width), LOW),
        "STR": ((narrow - 1, count, 16, 128), F32),
        "SCT": ((count, 128, 128), F32),
        "GA": ((groups, 64, width), LOW),
        "DL": ((groups, 16, 128), F32),
    }
    signals = {
        "s_pair": (3,),
        "s_up": (2,),
        "s_z": (UNITS, 3),
        "s_two": (UP, 2),
        "s_three": (UNITS, 2),
        "s_hand": (UNITS,),
        "s_rs1": (UNITS, 2),
        "s_rs2": (UP, 2),
        "s_rs3": (UNITS, 3),
        "s_rs4": (UNITS,),
        "s_rs5": (2, 2),
        "s_vec": (2, 6),
        "s_left": (4,),
        "s_right": (6,),
        "s_a3": (3,),
        "s_g4": (3,),
        "s_u": (2,),
        "s_dh": (2,),
        "s_fold": (2,),
        "s_memory": (2,),
        "s_query": (narrow - 1,),
        "s_num": (narrow - 1,),
        "s_st": (narrow - 1,),
        "s_g": (narrow - 1,),
        "s_dl": (narrow - 1,),
        "s_dq": (narrow - 1,),
        "s_image": (1,),
    }
    scratch = [pltpu.VMEM(shape, kind) for shape, kind in memory.values()]
    for shape in signals.values():
        scratch += [pltpu.SemaphoreType.DMA(shape)] * 2

    def body(*refs):
        named = dict(zip(ins + list(outs) + list(memory), refs))
        rest = refs[len(named) :]
        for i, name in enumerate(signals):
            named[name] = (rest[2 * i], rest[2 * i + 1])
        Layer(named, lanes, narrow).run()

    vmem = pl.BlockSpec(memory_space=pltpu.VMEM)
    in_specs = [vmem] * len(ins)
    in_specs[1] = pl.BlockSpec(memory_space=pl.ANY)
    in_specs[2] = pl.BlockSpec(memory_space=pltpu.SMEM)
    out_specs = [vmem] * len(outs)
    out_specs[2] = pl.BlockSpec(memory_space=pl.ANY)
    return pl.pallas_call(
        body,
        out_shape=[jax.ShapeDtypeStruct(shape, kind) for shape, kind in outs.values()],
        in_specs=in_specs,
        out_specs=out_specs,
        scratch_shapes=scratch,
        compiler_params=pltpu.CompilerParams(
            collective_id=0, has_side_effects=True, vmem_limit_bytes=64 * 1024 * 1024 - 65536
        ),
        cost_estimate=pl.CostEstimate(
            flops=17 * 10**9, bytes_accessed=8 * 10**6, transcendentals=2 * 10**6
        ),
        name="layer",
    )(captions, images, lengths, out_grad, vec, *weights)


def lane_gather(value, lanes, narrow, axis):
    if lanes == 1:
        return value
    assert lanes % narrow == 0
    value = lax.all_gather(value, "narrow", axis=axis, tiled=True)
    step = 1
    wide_count = lax.axis_size("wide")
    while step * narrow < lanes:
        swap = [(i, i ^ step) for i in range(wide_count)]
        other = lax.ppermute(value, "wide", swap)
        low = (lax.axis_index("wide") // step) % 2 == 0
        first = jnp.where(low, value, other)
        second = jnp.where(low, other, value)
        value = jnp.concatenate([first, second], axis=axis)
        step *= 2
    return value


def lane_scatter(value, lanes, narrow, axis):
    if lanes == 1:
        return value
    wide_count = lax.axis_size("wide")
    step = lanes // narrow
    while step > 1:
        step //= 2
        swap = [(i, i ^ step) for i in range(wide_count)]
        first, second = jnp.split(value, 2, axis=axis)
        low = (lax.axis_index("wide") // step) % 2 == 0
        other = lax.ppermute(jnp.where(low, second, first), "wide", swap)
        value = jnp.where(low, first, second) + other
    return lax.psum_scatter(value, "narrow", scatter_dimension=axis, tiled=True)


def per_device(captions, images, lengths, out_grad, *params):
    narrow = lax.axis_size("narrow")
    devices = lax.axis_size("wide") * narrow
    lanes = devices // NODES
    count, seq_len, width = captions.shape
    tokens = count * seq_len
    params = [lane_gather(item, lanes, narrow, 0) for item in params]
    own = width // NODES
    vec = jnp.pad(jnp.stack(params[7:]), ((0, 2), (0, 128 - own)))
    out, input_grad, image_grad, block_grad, down_grad, vec_grad = layer_call(
        lanes,
        narrow,
        captions.reshape(tokens, width),
        images.reshape(-1, width),
        lengths,
        out_grad.reshape(tokens, width),
        vec,
        *params[:7],
    )
    vec_own = vec_grad[:6, :own]
    block_grad = lane_scatter(block_grad, lanes, narrow, 0)
    down_grad = lane_scatter(down_grad, lanes, narrow, 0)
    vec_own = lane_scatter(vec_own, lanes, narrow, 1)

    def columns(start, stop):
        return block_grad[:, start * width : stop * width]

    return (
        out.reshape(captions.shape),
        input_grad.reshape(captions.shape),
        image_grad.reshape(images.shape),
        columns(QS, SO),
        columns(SO, CK),
        columns(CQ, CO),
        columns(CK, CQ),
        columns(CO, UP),
        columns(UP, UP + 4),
        down_grad,
        *[vec_own[i] for i in range(6)],
    )


def solution(mesh):
    both = ("wide", "narrow")
    rows = P(both, None)
    text = P(both, None, None)
    vector = P(both)
    image = P("wide", "narrow", None)
    in_specs = (text, image, vector, text) + (rows,) * 7 + (vector,) * 6
    out_specs = (text, text, image) + (rows,) * 7 + (vector,) * 6
    return jax.shard_map(
        per_device, mesh=mesh, in_specs=in_specs, out_specs=out_specs, check_vma=False
    )
```

time: 315 us -> 235 us (0.75)
  Pallas kernels: 295 us -> 220 us
    pallas_call x1, Pallas kernels: 295 us -> 220 us  [layer_call(): pl.pallas_call(body, out_shape=[jax.ShapeDtypeStruct(shape, kind) for sha...]
    slice x0 -> x4, local copies, waits for them, and re-layouts: none -> 6.55 us  [columns(): return block_grad[:, start * width:stop * width]]
    unnamed x20 -> x10, local copies, waits for them, and re-layouts: 8.01 us -> 4.22 us
where the time goes in v2:
time: 235 us; the launch traced here: 234 us
  Pallas kernels  220 us (94%)
  local copies, waits for them, and re-layouts  13.6 us (6%)
    pallas_call x1, Pallas kernels, layer_call(): pl.pallas_call(body, out_shape=[jax.ShapeDtypeStruct(shape, kind) for sha...  220 us
    slice x4, local copies, waits for them, and re-layouts, columns(): return block_grad[:, start * width:stop * width]  6.55 us

profile of v2, /device:TPU:1, one launch (start us, length us, event | category | flops | bytes accessed | tf_op | source)
XLA Modules:
  0.0 234.3 jit_solution(6557488111656371536)
XLA Ops:
  0.6 0.8 stack.27
  1.4 0.6 pad.4.refs_4_
  2.0 220.0 %layer.1 = (bf16[128,768]{1,0:T(8,128)(2,1)}, bf16[128,768]{1,0:T(8,128)(2,1)}, bf16[1152,768]{1,0:T(8,128)(2,1)}, f32[24,9216]{1,0:T(8,128)}, f32[96,768]{1,0:T(8,128)}, /*index=5*/f32[8,128]{1,0:T(8,128)}) custom-call(bf16[128,768]{1,0:T(8,128)(2,1)} %bitcast.34, bf16[1152,768]{1,0:T(8,128)(2,1)} %bitcast.33, s32[2]{0:T(128)} %refs_2_.1, ...), custom_call_target="tpu_custom_call" | custom-call | flops 16999999488 | bytes 8000000 | tf_op jit(solution)/shard_map/layer/pallas_call | solution.py:1154
  222.0 0.0 copy-start.2
  222.0 0.0 copy-start
  222.0 1.4 slice_bitcast_fusion
  223.5 1.6 slice.46
  225.1 1.6 slice.43
  226.7 1.6 fusion
  228.3 1.7 slice.48
  230.0 1.6 copy.37
  231.7 0.0 copy-done.2
  231.7 0.7 copy.38
  232.3 0.0 copy-done
  232.3 0.0 copy-start.1
  232.3 1.2 copy.39
  233.6 0.0 copy-done.1
  233.6 0.7 copy.40
Async XLA Ops:
  222.0 9.6 %copy-start.2 = (bf16[128,768]{1,0:T(8,128)(2,1)S(1)}, bf16[128,768]{1,0:T(8,128)(2,1)}, u32[]{:S(2)}) copy-start(bf16[128,768]{1,0:T(8,128)(2,1)} %get-tuple-element.23) | copy-start | bytes 589828
  222.0 10.3 %copy-start = (bf16[1152,768]{1,0:T(8,128)(2,1)S(1)}, bf16[1152,768]{1,0:T(8,128)(2,1)}, u32[]{:S(2)}) copy-start(bf16[1152,768]{1,0:T(8,128)(2,1)} %get-tuple-element.24) | copy-start | bytes 5308420
  232.3 1.2 copy-start.1

commit v3 on v2

v3 whole, which is shorter than its diff:
```python
import functools

import jax
import jax.numpy as jnp
from jax import lax
from jax.experimental import pallas as pl
from jax.experimental.pallas import tpu as pltpu
from jax.sharding import PartitionSpec as P

HEADS = 12
NODES = 32
UNITS = 11
VMEM_LIMIT = 64 * 1024 * 1024 - 65536
MESH = pl.DeviceIdType.MESH
F32 = jnp.float32
LOW = jnp.bfloat16
EPSILON = 1e-05
GELU_A = 0.7978845608028654
GELU_B = 0.044715

QS, KS, VS, SO, CK, CV, CQ, CO, UP = 0, 1, 2, 3, 4, 5, 6, 7, 8
DOWN = UP + 1
LATE = DOWN + 1
GATHER = (128, 256) * 4
SCATTER = (256, 128) * 4


VECTORS = ["first_gain", "first_shift", "second_gain", "second_shift"]
VECTORS += ["third_gain", "third_shift"]


class Step:
    (
        begin,
        up0,
        vec,
        g0,
        g1,
        mem,
        a1,
        qkv,
        sa,
        r1,
        cq,
        q1,
        cf,
        m1,
        m2,
        a3,
        x1,
        hp,
        dg,
        e3,
        out,
        lo,
        ug,
        dr2,
        p1,
        cb,
        n1,
        n2,
        dq,
        mo,
        mw,
        wg,
        sb,
        sum,
        img,
        end,
        F,
        S,
        TA,
        TB,
        H,
        R1,
        RA,
        RB,
        R3,
        R4,
        RU,
    ) = range(47)


ORDER = [
    (Step.begin,), (Step.F, 0), (Step.g0,), (Step.vec, 1), (Step.F, 1), (Step.vec, 2), (Step.F, 3),
    (Step.up0,), (Step.S, 0), (Step.F, 2), (Step.F, 5), (Step.S, 1), (Step.TA, 0), (Step.S, 3),
    (Step.TA, 1), (Step.TB, 1), (Step.F, 6), (Step.TB, 0), (Step.TA, 3), (Step.TB, 3),
    (Step.vec, 3), (Step.g1,), (Step.S, 2), (Step.F, 4), (Step.H, 1), (Step.S, 6), (Step.S, 5),
    (Step.F, 7), (Step.a1,), (Step.TA, 2), (Step.TB, 2), (Step.qkv, 1), (Step.F, 8), (Step.S, 4),
    (Step.F, 10), (Step.TA, 6), (Step.TB, 6), (Step.H, 0), (Step.H, 2), (Step.S, 7), (Step.TB, 5),
    (Step.TA, 5), (Step.qkv, 0), (Step.TB, 4), (Step.qkv, 2), (Step.H, 3), (Step.sa,), (Step.F, 9),
    (Step.r1,), (Step.H, 6), (Step.TA, 4), (Step.H, 5), (Step.S, 10), (Step.S, 8), (Step.cq,),
    (Step.TA, 7), (Step.H, 4), (Step.mem, 1), (Step.TB, 7), (Step.mem, 0), (Step.q1,),
    (Step.cf, 1), (Step.m1,), (Step.S, 9), (Step.cf, 0), (Step.H, 7), (Step.m2,), (Step.a3,),
    (Step.H, 8), (Step.H, 9), (Step.H, 10), (Step.x1,), (Step.hp,), (Step.e3,), (Step.dg,),
    (Step.ug,), (Step.R1, 10), (Step.R1, 9), (Step.R1, 8), (Step.out,), (Step.dr2,), (Step.wg, 7),
    (Step.cb, 0), (Step.R1, 7), (Step.p1,), (Step.cb, 1), (Step.n1,), (Step.mo, 0), (Step.mo, 1),
    (Step.mw, 0), (Step.R1, 4), (Step.RA, 9), (Step.RA, 7), (Step.n2,), (Step.RA, 8), (Step.RB, 7),
    (Step.mw, 1), (Step.R1, 5), (Step.dq,), (Step.sb,), (Step.wg, 3), (Step.R1, 3), (Step.wg, 0),
    (Step.RA, 4), (Step.wg, 2), (Step.R1, 2), (Step.sum, 1), (Step.RA, 5), (Step.RB, 4),
    (Step.wg, 6), (Step.img,), (Step.wg, 1), (Step.RB, 5), (Step.R1, 0), (Step.RA, 2),
    (Step.R1, 1), (Step.R3, 7), (Step.R3, 4), (Step.RB, 3), (Step.sum, 2), (Step.RA, 3),
    (Step.RB, 2), (Step.R3, 5), (Step.RA, 10), (Step.sum, 3), (Step.R1, 6), (Step.R3, 2),
    (Step.RA, 0), (Step.RB, 0), (Step.R4, 9), (Step.R3, 3), (Step.R4, 8), (Step.RB, 1),
    (Step.RA, 1), (Step.R3, 0), (Step.RA, 6), (Step.RU, 8), (Step.RB, 6), (Step.R4, 2),
    (Step.R3, 1), (Step.R4, 4), (Step.R4, 7), (Step.R4, 5), (Step.lo,), (Step.R3, 6), (Step.R4, 3),
    (Step.R4, 0), (Step.R4, 1), (Step.R4, 6), (Step.end,),
]


def mm(left, right):
    return jnp.dot(left, right, preferred_element_type=F32)


def mm_bt(left, right):
    return lax.dot_general(left, right, (((1,), (1,)), ((), ())), preferred_element_type=F32)


def mm_at(left, right):
    return lax.dot_general(left, right, (((0,), (0,)), ((), ())), preferred_element_type=F32)


def norm(value, gain, shift):
    centred = value - jnp.mean(value, axis=-1, keepdims=True)
    rstd = lax.rsqrt(jnp.mean(centred * centred, axis=-1, keepdims=True) + EPSILON)
    hat = centred * rstd
    return hat, rstd, hat * gain + shift


def norm_pull(grad, hat, rstd, gain):
    scaled = grad * gain
    inner = jnp.mean(scaled * hat, axis=-1, keepdims=True)
    back = rstd * (scaled - jnp.mean(scaled, axis=-1, keepdims=True) - hat * inner)
    gain_grad = jnp.sum(grad * hat, axis=0, keepdims=True)
    shift_grad = jnp.sum(grad, axis=0, keepdims=True)
    return back, gain_grad, shift_grad


class Layer:
    def __init__(self, refs, lanes, narrow):
        self.__dict__.update(refs)
        self.N = narrow
        self.lanes = lanes
        wide, nar = lax.axis_index("wide"), lax.axis_index("narrow")
        flat = wide * narrow + nar
        self.wide, self.nar = wide, nar
        self.node = lax.div(flat, lanes)
        self.lane = lax.rem(flat, lanes)
        node = self.node
        self.c = lax.rem(node, 2)
        self.x = lax.rem(lax.div(node, 2), 2)
        self.y = lax.rem(lax.div(node, 4), 2)
        self.z = lax.div(node, 8)
        self.started = {}
        self.here = set()
        self.count, self.seq = self.captions.shape[0] // 64, 64
        self.tokens, self.width = self.captions.shape
        self.groups = self.QA.shape[0]
        self.image_rows = self.images.shape[0] // self.groups
        self.pairs = self.width // 128
        lane = lax.broadcasted_iota(jnp.int32, (1, 128), 1)
        self.low_lanes = (lane < 64).astype(F32).astype(LOW)
        self.high_lanes = (lane >= 64).astype(F32).astype(LOW)
        self.is_first = lane < 64

    def device(self, z, y, x, c):
        flat = (z * 8 + y * 4 + x * 2 + c) * self.lanes + self.lane
        return (lax.div(flat, self.N), lax.rem(flat, self.N))

    def sibling(self):
        return self.device(self.z, self.y, self.x, 1 - self.c)

    def x_peer(self):
        return self.device(self.z, self.y, 1 - self.x, self.c)

    def y_peer(self):
        return self.device(self.z, 1 - self.y, self.x, self.c)

    def z_index(self, k):
        return lax.rem(self.z + k, 4)

    def z_peer(self, k):
        return self.device(self.z_index(k), self.y, self.x, self.c)

    def n_index(self, k):
        return lax.rem(self.nar + k, self.N)

    def n_peer(self, k):
        return (self.wide, self.n_index(k))

    def enter(self):
        barrier = pltpu.get_barrier_semaphore()
        peers = [self.sibling(), self.x_peer(), self.y_peer()]
        peers += [self.z_peer(k) for k in (1, 2, 3)]
        peers += [self.n_peer(k) for k in range(1, self.N)]
        for peer in peers:
            pl.semaphore_signal(barrier, inc=1, device_id=peer, device_id_type=MESH)
        pl.semaphore_wait(barrier, len(peers))

    def copy(self, src, dst, sems, where, peer):
        send, recv = sems
        return pltpu.make_async_remote_copy(
            src_ref=src,
            dst_ref=dst,
            send_sem=send.at[where],
            recv_sem=recv.at[where],
            device_id=peer,
            device_id_type=MESH,
        )

    def start(self, copies, group=None):
        for item in copies:
            item.start()
        self.started.setdefault(group, []).extend(copies)

    def sent(self, group):
        for item in self.started.pop(group, []):
            item.wait_send()

    def part(self, unit, half, z, y, x, grad=False):
        every = slice(None)
        if unit < UP:
            first = (SCATTER if grad else GATHER)[unit]
            low, size = ((0, 384), (0, first), (first, 384 - first))[0 if half is None else half + 1]
            if grad and unit in (CK, CV):
                return self.CP.at[unit - CK, z, y, x, every, pl.ds(low, size)]
            columns = pl.ds(pl.multiple_of(384 * self.c + low, 128), size)
            return self.W.at[unit, z, y, x, every, columns]
        if unit == UP:
            return self.W.at[UP + self.c, z, y, x]
        ref = self.HG if grad else self.HD.at[self.c]
        return ref.at[z, y, pl.ds(96 * (unit - DOWN), 96)]

    def half_columns(self, c):
        return pl.ds(pl.multiple_of(384 * c, 128), 384)

    def shards(self):
        found = [(self.self_proj, self.width * j) for j in range(3)] + [(self.self_output, 0)]
        found += [(self.cross_memory, self.width * j) for j in range(2)]
        return found + [(self.cross_query, 0), (self.cross_output, 0)]

    def half_block(self, block, c):
        ref, start = self.shards()[block]
        return ref[:, pl.ds(pl.multiple_of(start + 384 * c, 128), 384)].astype(F32)

    def swapped(self, value):
        return pltpu.roll(value, 64, 1)

    def split_runs(self, whole):
        n = [whole[:, 128 * i : 128 * i + 128] for i in range(6)]
        r = [self.swapped(item) for item in n]
        low = self.is_first
        a = [n[0], jnp.where(low, n[1], r[3]), jnp.where(low, r[3], r[4])]
        b = [jnp.where(low, r[1], r[2]), jnp.where(low, r[2], n[4]), n[5]]
        return jnp.concatenate(a, axis=1), jnp.concatenate(b, axis=1)

    def join_runs(self, left, right):
        a = [left[:, 128 * i : 128 * i + 128] for i in range(3)]
        b = [right[:, 128 * i : 128 * i + 128] for i in range(3)]
        ra, rb = [self.swapped(item) for item in a], [self.swapped(item) for item in b]
        low = self.is_first
        out = [a[0], jnp.where(low, a[1], rb[0]), jnp.where(low, rb[0], rb[1])]
        out += [jnp.where(low, ra[1], ra[2]), jnp.where(low, ra[2], b[1]), b[2]]
        return jnp.concatenate(out, axis=1)

    def up_blocks(self, c):
        found = []
        for j in range(2):
            start = pl.multiple_of(self.width * (2 * c + j), 128)
            found.append(self.split_runs(self.hidden_up[:, pl.ds(start, self.width)].astype(F32)))
        return [jnp.concatenate(item, axis=1) for item in zip(*found)]

    def pair_copies(self):
        c = self.c
        rows = pl.ds(pl.multiple_of(96 * c, 32), 96)
        there = self.HD.at[1 - c, self.z, self.y, rows]
        down = self.hidden_down.at[:, self.half_columns(1 - c)]
        return [
            self.copy(self.PA.at[0], self.PA.at[1], self.s_pair, 0, self.sibling()),
            self.copy(self.PB.at[0], self.PB.at[1], self.s_pair, 1, self.sibling()),
            self.copy(down, there, self.s_pair, 2, self.sibling()),
        ]

    def pair_pack(self):
        c = 1 - self.c
        blocks = [self.half_block(block, c) for block in range(UP)]
        self.PA[0] = jnp.concatenate(blocks, axis=0).astype(LOW)
        self.PB[0] = jnp.concatenate(self.up_blocks(c), axis=0).astype(LOW)

    def in_order(self, mine, theirs):
        even = self.c == 0
        low, high = jnp.where(even, mine, theirs), jnp.where(even, theirs, mine)
        return jnp.concatenate([low, high], axis=0)

    def pair_merge(self):
        c = self.c
        copies = self.pair_copies()
        rows = pl.ds(pl.multiple_of(96 * c, 32), 96)
        self.HD[c, self.z, self.y, rows] = self.hidden_down[:, self.half_columns(c)]
        columns = pl.ds(pl.multiple_of(384 * c, 128), 384)
        copies[0].wait_recv()
        theirs = self.PA[1].astype(F32)
        for block in range(UP):
            both = self.in_order(self.half_block(block, c), theirs[24 * block : 24 * block + 24])
            self.W[block, self.z, self.y, self.x, :, columns] = both.astype(LOW)
        copies[1].wait_recv()
        theirs = self.PB[1].astype(F32)
        both = [
            self.in_order(mine, theirs[24 * i : 24 * i + 24])
            for i, mine in enumerate(self.up_blocks(c))
        ]
        west = self.x == 0
        self.W[UP + c, self.z, self.y, self.x] = jnp.where(west, both[0], both[1]).astype(LOW)
        self.UPS[...] = jnp.where(west, both[1], both[0]).astype(LOW)
        copies[2].wait_recv()

    def up_copies(self):
        there = self.W.at[UP + self.c, self.z, self.y, self.x]
        return [self.copy(self.UPS, there, self.s_up, 0, self.x_peer())]

    def z_copies(self, unit):
        x = slice(None) if unit == UP else self.x
        y = slice(None) if unit == LATE else self.y
        here = self.part(unit, None, self.z, y, x)
        return [
            self.copy(here, here, self.s_z, (unit, k - 1), self.z_peer(k)) for k in (1, 2, 3)
        ]

    def halves(self, unit, table):
        return range(1 if table[unit] == 384 else 2)

    def two_copy(self, unit, half):
        here = self.part(unit, half, slice(None), self.y, self.x)
        peer = (self.x_peer, self.y_peer)[half]()
        return self.copy(here, here, self.s_two, (unit, half), peer)

    def three_copy(self, unit, half):
        every = slice(None)
        if unit >= UP:
            z = self.z if unit == LATE else every
            here = self.part(unit, None, z, self.y, every)
            return self.copy(here, here, self.s_three, (unit, 0), self.y_peer())
        y, x = ((self.y, every), (every, self.x))[half]
        here = self.part(unit, half, every, y, x)
        peer = (self.y_peer, self.x_peer)[half]()
        return self.copy(here, here, self.s_three, (unit, half), peer)

    def three_copies(self, unit):
        halves = (0,) if unit >= UP else self.halves(unit, GATHER)
        return [self.three_copy(unit, half) for half in halves]

    def hand_copies(self, unit):
        every = slice(None)
        whole = self.part(unit, None, every, every, every)
        return [self.copy(whole, whole, self.s_hand, unit, self.sibling())]

    def arrived(self, copies):
        for item in copies:
            item.wait_recv()

    def first(self, unit):
        if unit == UP:
            self.arrived(self.up_copies())
        self.start(self.three_copies(unit) if unit == LATE else self.z_copies(unit), unit)

    def second(self, unit):
        if unit == LATE:
            self.arrived(self.three_copies(unit))
            self.start(self.z_copies(unit), unit)
            return
        self.arrived(self.z_copies(unit))
        if unit < UP:
            copies = [self.two_copy(unit, half) for half in self.halves(unit, GATHER)]
        else:
            copies = self.three_copies(unit)
        self.start(copies, unit)

    def third(self, unit, half):
        if half in self.halves(unit, GATHER):
            self.arrived([self.two_copy(unit, half)])
            self.start([self.three_copy(unit, half)], unit)

    def hand(self, unit):
        self.arrived(self.z_copies(unit) if unit == LATE else self.three_copies(unit))
        self.start(self.hand_copies(unit), unit)

    def done(self, unit):
        self.arrived(self.hand_copies(unit))

    def term(self, unit, half, z=slice(None)):
        first = SCATTER[unit]
        return (unit, z, ..., pl.ds(*((0, first), (first, 384 - first))[half]))

    def rs_one_copy(self, unit, half):
        every = slice(None)
        if unit == LATE:
            here = self.part(unit, None, self.z, 1 - self.y, every, grad=True)
            return self.copy(here, self.RL1, self.s_rs1, (unit, 0), self.y_peer())
        if unit >= UP:
            here = self.part(unit, None, every, 1 - self.y, every, grad=True)
            there = self.RU1 if unit == UP else self.RH1
            return self.copy(here, there, self.s_rs1, (unit, 0), self.y_peer())
        y, x = ((1 - self.y, every), (every, 1 - self.x))[half]
        here = self.part(unit, half, every, y, x, grad=True)
        there = self.R1.at[self.term(unit, half)]
        peer = (self.y_peer, self.x_peer)[half]()
        return self.copy(here, there, self.s_rs1, (unit, half), peer)

    def rs_two_copy(self, unit, half):
        y, x = ((self.y, 1 - self.x), (1 - self.y, self.x))[half]
        here = self.part(unit, half, slice(None), y, x, grad=True)
        there = self.R2.at[self.term(unit, half)]
        peer = (self.x_peer, self.y_peer)[half]()
        return self.copy(here, there, self.s_rs2, (unit, half), peer)

    def rs_three_copies(self, unit):
        out = []
        x = slice(None) if unit == UP else self.x
        y = slice(None) if unit == LATE else self.y
        for k in (1, 2, 3):
            here = self.part(unit, None, self.z_index(k), y, x, grad=True)
            if unit < UP:
                there = self.R3.at[unit, k - 1]
            elif unit == UP:
                there = self.RU3.at[k - 1]
            else:
                there = (self.RL3 if unit == LATE else self.RH3).at[k - 1]
            out.append(self.copy(here, there, self.s_rs3, (unit, k - 1), self.z_peer(k)))
        return out

    def up_back_copies(self):
        return [self.copy(self.UPS, self.UPR, self.s_up, 1, self.x_peer())]

    def grad_columns(self, block):
        return pl.ds(pl.multiple_of(self.width * block + 384 * self.c, 128), 384)

    def rs_four_copies(self, unit):
        c = self.c
        if unit < UP:
            there = self.block_grad.at[:, self.grad_columns(unit)]
            return [self.copy(self.SF.at[unit], there, self.s_rs4, unit, self.sibling())]
        if unit == UP:
            columns = self.half_columns_up()
            return [
                self.copy(
                    self.SFU.at[i],
                    self.UPG.at[self.up_side(i), :, columns],
                    self.s_rs5,
                    i,
                    self.sibling(),
                )
                for i in range(2)
            ]
        there = self.down_out.at[:, self.half_columns(c)]
        return [self.copy(self.SFH, there, self.s_rs4, unit, self.sibling())]

    def up_side(self, i):
        return self.x if i == 0 else 1 - self.x

    def half_columns_up(self):
        return pl.ds(pl.multiple_of(self.width * self.c, 128), self.width)

    def add_into(self, ref, term):
        ref[...] = (ref[...].astype(F32) + term.astype(F32)).astype(LOW)

    def rs_one(self, unit):
        halves = (0,) if unit >= UP else self.halves(unit, SCATTER)
        if unit == LATE:
            self.start(self.rs_three_copies(unit))
        else:
            self.start([self.rs_one_copy(unit, half) for half in halves])

    def rs_two(self, unit, half=0):
        every = slice(None)
        if unit < UP and half not in self.halves(unit, SCATTER):
            return
        if unit == LATE:
            self.arrived(self.rs_three_copies(unit))
            here = self.part(unit, None, self.z, every, self.x, grad=True)
            here[...] = self.sum_of(here[...], [self.RL3[k] for k in range(3)]).astype(LOW)
            self.start([self.rs_one_copy(unit, 0)])
            return
        self.arrived([self.rs_one_copy(unit, half)])

        @pl.loop(0, 4)
        def _(z):
            if unit < UP:
                y, x = ((self.y, every), (every, self.x))[half]
                more = self.R1[self.term(unit, half, z)]
                self.add_into(self.part(unit, half, z, y, x, grad=True), more)
            else:
                more = self.RU1[z] if unit == UP else self.RH1[z]
                self.add_into(self.part(unit, None, z, self.y, every, grad=True), more)

        if unit < UP:
            self.start([self.rs_two_copy(unit, half)])
        else:
            self.start(self.rs_three_copies(unit))

    def rs_three(self, unit):
        halves = self.halves(unit, SCATTER)
        self.arrived([self.rs_two_copy(unit, half) for half in halves])

        @pl.loop(0, 4)
        def _(z):
            for half in halves:
                more = self.R2[self.term(unit, half, z)]
                self.add_into(self.part(unit, half, z, self.y, self.x, grad=True), more)

        self.start(self.rs_three_copies(unit))

    def sum_of(self, value, terms):
        return sum((item.astype(F32) for item in terms), value.astype(F32))

    def rs_total(self, unit):
        x = slice(None) if unit == UP else self.x
        own = self.part(unit, None, self.z, self.y, x, grad=True)
        if unit == LATE:
            self.arrived([self.rs_one_copy(unit, 0)])
            return self.sum_of(own[...], [self.RL1[...]])
        self.arrived(self.rs_three_copies(unit))
        if unit < UP:
            return self.sum_of(own[...], [self.R3[unit, k] for k in range(3)])
        ref = self.RU3 if unit == UP else self.RH3
        return self.sum_of(own[...], [ref[k] for k in range(3)])

    def rs_four(self, unit):
        even = self.c == 0
        if unit < UP:
            total = self.rs_total(unit)
            low, high = total[:24], total[24:]
            self.block_grad[:, self.grad_columns(unit)] = jnp.where(even, low, high)
            self.SF[unit] = jnp.where(even, high, low)
            self.start(self.rs_four_copies(unit))
        if unit == UP:
            total = self.rs_total(unit)
            west = self.x == 0
            self.sent("up")
            self.UPS[...] = jnp.where(west, total[1], total[0]).astype(LOW)
            self.start(self.up_back_copies())
            self.up_rows(0, jnp.where(west, total[0], total[1]))
        if unit == DOWN:
            low, high = self.rs_total(DOWN), self.rs_total(DOWN + 1)
            self.down_out[:, self.half_columns(self.c)] = jnp.where(even, low, high)
            self.SFH[...] = jnp.where(even, high, low)
            self.start(self.rs_four_copies(DOWN))

    def up_rows(self, i, total):
        even = self.c == 0
        low, high = total[:24], total[24:]
        self.UPG[self.up_side(i), :, self.half_columns_up()] = jnp.where(even, low, high)
        self.SFU[i] = jnp.where(even, high, low)

    def rs_up(self):
        self.arrived(self.up_back_copies())
        self.up_rows(1, self.UPR[...].astype(F32))
        self.start(self.rs_four_copies(UP))

    def rs_done(self, unit):
        if unit != DOWN + 1:
            self.arrived(self.rs_four_copies(unit))
        if unit == UP:
            for z in range(4):
                at = slice(384 * z, 384 * z + 384)
                start = self.width * (UP + z)
                both = self.join_runs(self.UPG[0, :, at], self.UPG[1, :, at])
                self.block_grad[:, start : start + self.width] = both

    def sum_copies(self, which, stage):
        peers = [[self.sibling()], [self.x_peer()], [self.y_peer()]]
        peers += [[self.z_peer(k) for k in (1, 2, 3)]]
        return [
            self.copy(
                self.V.at[which, stage],
                self.VR.at[which, stage + i],
                self.s_vec,
                (which, stage + i),
                peer,
            )
            for i, peer in enumerate(peers[stage])
        ]

    def placement(self, dtype, rows):
        own = self.width // NODES
        at = lax.broadcasted_iota(jnp.int32, (rows, self.width), 0)
        feature = lax.broadcasted_iota(jnp.int32, (rows, self.width), 1)
        return ((at < own) & (feature == at + own * self.node)).astype(F32).astype(dtype)

    def sum_start(self, which, stage, value):
        self.V[which, stage] = value
        self.start(self.sum_copies(which, stage))

    def sum_end(self, which, stage):
        now = self.sum_copies(which, stage)
        self.arrived(now)
        value = self.V[which, stage]
        for i in range(len(now)):
            value = value + self.VR[which, stage + i]
        return value

    def keep_left(self, place, value):
        self.LHS[place, self.c] = value
        here = self.LHS.at[place, self.c]
        self.start([self.copy(here, here, self.s_left, place, self.sibling())])

    def keep_right(self, place, value):
        self.RHS[place, self.c] = value
        here = self.RHS.at[place, self.c]
        self.start([self.copy(here, here, self.s_right, place, self.sibling())])

    def left_arrived(self, place):
        if ("left", place) not in self.here:
            self.here.add(("left", place))
            here = self.LHS.at[place, self.c]
            self.copy(here, here, self.s_left, place, self.sibling()).wait_recv()

    def right_arrived(self, place):
        if ("right", place) not in self.here:
            self.here.add(("right", place))
            here = self.RHS.at[place, self.c]
            self.copy(here, here, self.s_right, place, self.sibling()).wait_recv()

    def weight(self, block):
        return self.W[block].reshape(self.width, self.width)

    def weight_grad(self, unit):
        left, right = {QS: (0, 0), KS: (0, 1), VS: (0, 2), SO: (1, 3), CQ: (2, 4), CO: (3, 5)}[unit]
        self.sent(unit)
        self.left_arrived(left)
        self.right_arrived(right)
        columns = self.half_columns(self.c)
        right_all = self.RHS[right, :, :, columns].reshape(2 * self.tokens, 384)
        for t in range(2):
            left_all = self.LHS[left, :, :, pl.ds(384 * t, 384)].reshape(2 * self.tokens, 384)
            part = mm_at(left_all, right_all).astype(LOW)
            self.W[unit, pl.ds(2 * t, 2), :, :, :, columns] = part.reshape(2, 2, 2, 48, 384)

    def up_grad(self):
        c = self.c
        self.sent(UP)
        right_all = self.DH[c].reshape(4 * self.tokens, self.width)
        for t in range(2):
            left_all = self.A3[:, :, :, pl.ds(384 * t, 384)].reshape(4 * self.tokens, 384)
            part = mm_at(left_all, right_all).astype(LOW)
            self.W[UP + c, pl.ds(2 * t, 2)] = part.reshape(2, 2, 2, 48, self.width)

    def down_grad(self):
        right_all = self.G4[:, :, :, self.half_columns(self.c)].reshape(4 * self.tokens, 384)
        for z in range(4):
            j, t = z // 2, z % 2
            left_all = self.U[j, :, :, :, pl.ds(384 * t, 384)].reshape(4 * self.tokens, 384)
            part = mm_at(left_all, right_all).astype(LOW)
            self.HG[z] = part.reshape(2, 192, 384)

    def memory_copy(self, which):
        return self.copy(
            self.CS.at[which], self.CM.at[which], self.s_memory, which, self.sibling()
        )

    def memory_term(self, which, c, t):
        left = self.IMG[:, pl.ds(384 * t, 384)]
        part = mm_at(left, self.KV[which, :, self.half_columns(c)])
        return part.reshape(2, 2, 2, 48, 384)

    def memory_grad_other(self, which):
        for t in range(2):
            part = self.memory_term(which, 1 - self.c, t)
            self.CS[which, pl.ds(2 * t, 2)] = part.astype(LOW)
        self.start([self.memory_copy(which)])

    def memory_grad_own(self, which):
        self.memory_copy(which).wait_recv()
        for t in range(2):
            part = self.memory_term(which, self.c, t)
            part = part + self.CM[which, pl.ds(2 * t, 2)].astype(F32)
            self.CP[which, pl.ds(2 * t, 2)] = part.astype(LOW)

    def masked(self, value):
        return value * self.low_lanes, value * self.high_lanes

    def self_attention(self):
        rows = lax.broadcasted_iota(jnp.int32, (128, 128), 0)
        cols = lax.broadcasted_iota(jnp.int32, (128, 128), 1)
        length = jnp.where(cols < 64, self.lengths[0], self.lengths[1])
        allowed = (lax.div(rows, 64) == lax.div(cols, 64)) & (cols <= rows)
        allowed = allowed & (lax.rem(cols, 64) < length)
        parts = []
        for p in range(self.pairs):
            at = slice(128 * p, 128 * p + 128)
            q, k, v = self.QKV[0, :, at], self.QKV[1, :, at], self.QKV[2, :, at]
            both = mm_bt(q, self.stacked(k)) * 0.125
            probs = []
            for h in range(2):
                s = jnp.where(allowed, both[:, 128 * h : 128 * h + 128], -1000000000.0)
                e = jnp.exp(s - jnp.max(s, axis=-1, keepdims=True))
                probs.append(e / jnp.sum(e, axis=-1, keepdims=True))
            prob = jnp.concatenate(probs, axis=1)
            self.PS[p] = prob
            parts.append(mm(prob.astype(LOW), self.stacked(v)).astype(LOW))
        return jnp.concatenate(parts, axis=1)

    def self_attention_back(self, grad):
        parts = ([], [], [])
        for p in range(self.pairs):
            at = slice(128 * p, 128 * p + 128)
            q, k, v = self.QKV[0, :, at], self.QKV[1, :, at], self.QKV[2, :, at]
            g = grad[:, at]
            prob = self.PS[p]
            dp = mm_bt(g, self.stacked(v))
            prod = prob * dp
            parts_ds = []
            for h in range(2):
                lanes = slice(128 * h, 128 * h + 128)
                inner = jnp.sum(prod[:, lanes], axis=-1, keepdims=True)
                parts_ds.append(prob[:, lanes] * (dp[:, lanes] - inner))
            ds = jnp.concatenate(parts_ds, axis=1).astype(LOW)
            dq = mm(ds, self.stacked(k))
            dk = self.diagonal(mm_at(ds, q), 128)
            dv = self.diagonal(mm_at(prob.astype(LOW), g), 128)
            for out, item in zip(parts, (dq * 0.125, dk * 0.125, dv)):
                out.append(item.astype(LOW))
        return [jnp.concatenate(item, axis=1) for item in parts]

    def stacked(self, value):
        a, b = self.masked(value)
        return jnp.concatenate([a, b], axis=0)

    def diagonal(self, value, rows):
        return jnp.where(self.is_first, value[:rows], value[rows:])

    def stacked_four(self, value):
        zero = jnp.zeros((value.shape[0], 128), LOW)
        left = [jnp.concatenate([item, zero], axis=1) for item in self.masked(value[:, :128])]
        right = [jnp.concatenate([zero, item], axis=1) for item in self.masked(value[:, 128:])]
        return jnp.concatenate(left + right, axis=0)

    def diagonal_four(self, value):
        left = jnp.where(self.is_first, value[:64, :128], value[64:128, :128])
        right = jnp.where(self.is_first, value[128:192, 128:], value[192:, 128:])
        return jnp.concatenate([left, right], axis=1)

    def row_pair(self, ref, place, row):
        return jnp.concatenate([ref[place, row : row + 1], ref[place, row + 1 : row + 2]], axis=1)

    def put_pair(self, ref, place, row, value):
        ref[place, row : row + 1] = value[:, :128]
        ref[place, row + 1 : row + 2] = value[:, 128:]

    def memory_forward(self, which):
        w = self.weight(CK + which)

        @pl.loop(0, 3)
        def _(t):
            size = self.images.shape[0] // 3
            rows = pl.ds(pl.multiple_of(size * t, 16), size)
            self.KV[which, rows] = mm(self.IMG[rows], w).astype(LOW)

    def cross_forward(self, place):
        rows = pl.ds(pl.multiple_of(place * self.image_rows, 16), self.image_rows)
        for f in range(self.pairs // 2):
            at = slice(256 * f, 256 * f + 256)
            k, v = self.KV[0, rows, at], self.KV[1, rows, at]
            q = self.stacked_four(self.QA[place, :, at])
            s = mm_bt(k, q) * 0.125
            top = jnp.max(s, axis=0, keepdims=True)
            e = jnp.exp(s - top)
            low = e.astype(LOW)
            self.E[place, f] = low
            self.put_pair(self.ST, place, 2 * f, jnp.sum(e, axis=0, keepdims=True))
            self.put_pair(self.ST, place, 8 + 2 * f, top)
            self.put_pair(self.TOP, place, 2 * f, top)
            num = mm_at(low, v)
            self.NUM[place, :, at] = self.diagonal_four(num).astype(LOW)
        self.ST[place, 6:8] = jnp.ones((2, 128), F32)
        self.ST[place, 14:16] = jnp.zeros((2, 128), F32)

    def cross_backward(self, place):
        rows = pl.ds(pl.multiple_of(place * self.image_rows, 16), self.image_rows)
        for f in range(self.pairs // 2):
            at = slice(256 * f, 256 * f + 256)
            k, v = self.KV[0, rows, at], self.KV[1, rows, at]
            q = self.stacked_four(self.QA[place, :, at])
            g = self.stacked_four(self.GA[place, :, at])
            top = self.row_pair(self.TOP, place, 2 * f)
            share = jnp.exp(top - self.row_pair(self.DL, place, 8 + 2 * f))
            e = self.E[place, f].astype(F32) * share
            ds = e * (mm_bt(v, g) + self.row_pair(self.DL, place, 2 * f))
            ds = ds.astype(LOW)
            dq = mm_at(ds, k)
            self.NUM[place, :, at] = (self.diagonal_four(dq) * 0.125).astype(LOW)
            self.KV[0, rows, at] = (mm(ds, q) * 0.125).astype(LOW)
            self.KV[1, rows, at] = mm(e.astype(LOW), g).astype(LOW)

    def captions_of(self, owner):
        return pl.ds(owner * self.count, self.count)

    def partner(self, bit):
        return (self.wide, jnp.bitwise_xor(self.nar, bit))

    def owner(self, bits):
        return jnp.bitwise_xor(self.nar, bits)

    def share_copies(self, ref, sems, bit, bits):
        here = ref.at[self.captions_of(self.owner(bits))]
        return self.copy(here, here, sems, (self.N + bits) // (2 * bit) - 1, self.partner(bit))

    def share_steps(self):
        bit = self.N // 2
        while bit:
            yield bit, range(0, self.N, 2 * bit)
            bit //= 2

    def share_start(self, refs):
        for bit, held in self.share_steps():
            self.start([self.share_copies(ref, sems, bit, 0) for ref, sems in refs])

    def share_pass(self, refs):
        for bit, held in self.share_steps():
            for bits in held:
                if bits:
                    self.start([self.share_copies(ref, sems, bit, bits) for ref, sems in refs])
            if bit > 1:
                for bits in held:
                    self.arrived([self.share_copies(ref, sems, bit, bits) for ref, sems in refs])

    def share_wait(self, refs, far):
        for bits in range(far, far + self.N // 2, 2):
            self.arrived([self.share_copies(ref, sems, 1, bits) for ref, sems in refs])

    def captions_loop(self, far, step):
        @pl.loop(0, self.groups // 2)
        def _(i):
            bits = far + lax.div(i, self.count)
            step(self.owner(bits) * self.count + lax.rem(i, self.count))

    def merge_slot(self, bit, bits):
        return self.N - self.N // bit + bits // (2 * bit)

    def merge_copies(self, refs, bit, bits):
        slot = self.merge_slot(bit, bits)
        owner = self.captions_of(self.owner(bits + bit))
        return [
            self.copy(ref.at[owner], there.at[slot], sems, slot, self.partner(bit))
            for ref, there, sems in refs
        ]

    def merge_steps(self):
        bit = 1
        while bit < self.N:
            yield bit, range(0, self.N, 2 * bit)
            bit *= 2

    def merge_start(self, refs, group, far):
        for bits in range(far, far + self.N // 2, 2):
            self.start(self.merge_copies(refs, 1, bits), group)

    def merge_part(self, refs, join, bit, bits, group):
        self.arrived(self.merge_copies(refs, bit, bits))
        for j in range(self.count):
            join(self.owner(bits) * self.count + j, self.merge_slot(bit, bits), j)
        if bits % (4 * bit):
            self.start(self.merge_copies(refs, 2 * bit, bits - 2 * bit), group)

    def merge_far(self, refs, join, group):
        for bit, kept in self.merge_steps():
            for bits in reversed(kept):
                if bits:
                    self.merge_part(refs, join, bit, bits, group)

    def merge_own(self, refs, join, group, steps):
        for bit, kept in self.merge_steps():
            if bit in steps:
                self.merge_part(refs, join, bit, 0, group)

    def column(self, turned, p):
        return jnp.where(self.is_first, turned[:64, p : p + 1], turned[64:, p : p + 1])

    def turn(self, *rows):
        have = 8 * len(rows)
        return jnp.concatenate([*rows, jnp.zeros((128 - have, 128), F32)], axis=0).T

    def join_softmax(self, place, slot, j):
        total_a, top_a = self.ST[place, :8], self.ST[place, 8:]
        total_b, top_b = self.STR[slot, j, :8], self.STR[slot, j, 8:]
        top = jnp.maximum(top_a, top_b)
        share_a, share_b = jnp.exp(top_a - top), jnp.exp(top_b - top)
        self.ST[place, :8] = share_a * total_a + share_b * total_b
        self.ST[place, 8:] = top
        turned = self.turn(share_a, share_b)
        for p in range(self.pairs):
            at = slice(128 * p, 128 * p + 128)
            a = self.NUM[place, :, at].astype(F32) * self.column(turned, p)
            b = self.NUMR[slot, j, :, at].astype(F32) * self.column(turned, 8 + p)
            self.NUM[place, :, at] = (a + b).astype(LOW)

    def join_sum(self, place, slot, j):
        self.add_into(self.NUM.at[place], self.NUMR[slot, j])

    def attended(self):
        done = []
        for j in range(self.count):
            place = self.nar * self.count + j
            turned = self.turn(1.0 / self.ST[place, :8])
            self.SCT[j] = turned
            parts = []
            for p in range(self.pairs):
                at = slice(128 * p, 128 * p + 128)
                parts.append(self.NUM[place, :, at].astype(F32) * self.column(turned, p))
            done.append(jnp.concatenate(parts, axis=1))
        return jnp.concatenate(done, axis=0)

    def spread_grad(self, doc):
        lane = lax.broadcasted_iota(jnp.int32, (128, 128), 1)
        for j in range(self.count):
            place = self.nar * self.count + j
            rows = slice(64 * j, 64 * j + 64)
            turned = self.SCT[j]
            inner = jnp.zeros((128, 128), F32)
            for p in range(self.pairs):
                at = slice(128 * p, 128 * p + 128)
                part = doc[rows, at] * self.column(turned, p)
                self.GA[place, :, at] = part.astype(LOW)
                prod = part * self.OCF[rows, at]
                a = jnp.sum(jnp.where(self.is_first, prod, 0.0), axis=1, keepdims=True)
                b = jnp.sum(jnp.where(self.is_first, 0.0, prod), axis=1, keepdims=True)
                inner = jnp.where(lane == p, jnp.concatenate([a, b], axis=0), inner)
            self.DL[place, :8] = -inner.T[:8]
            self.DL[place, 8:] = self.ST[place, 8:]

    def weight_images(self):
        return pltpu.make_async_copy(self.images, self.IMG, self.s_image[0].at[0])

    def keep_wide(self, ref, value, sems):
        ref[self.c, self.x] = value
        here = ref.at[self.c, self.x]
        self.start([self.copy(here, here, sems, 0, self.x_peer())])
        self.start([self.copy(here, here, sems, 1, self.sibling())])

    def wide_across(self, ref, sems):
        here = ref.at[self.c, self.x]
        self.copy(here, here, sems, 0, self.x_peer()).wait_recv()
        here = ref.at[self.c, 1 - self.x]
        self.start([self.copy(here, here, sems, 2, self.sibling())])

    def wide_arrived(self, ref, sems):
        for i in (1, 2):
            here = ref.at[self.c, self.x]
            self.copy(here, here, sems, i, self.sibling()).wait_recv()

    def hidden_copy(self, ref, j, sems):
        here = ref.at[j, self.c]
        return self.copy(here, here, sems, j, self.sibling())

    def fold_copy(self, which):
        return self.copy(self.FS.at[which], self.FR.at[which], self.s_fold, which, self.x_peer())

    def image_copy(self, back):
        src, dst = (self.IMG, self.image_grad) if back else (self.images, self.IMG)
        return pltpu.make_async_copy(src, dst, self.s_image[0].at[0])

    def both_halves(self, value):
        low, high = value[: self.tokens], value[self.tokens :]
        west = self.x == 0
        return jnp.where(west, low, high), jnp.where(west, high, low)

    def do_begin(self):
        self.image_copy(False).start()
        self.pair_pack()
        self.enter()
        self.start(self.pair_copies())
        rows = [getattr(self, name)[...].astype(F32) for name in VECTORS]
        rows = jnp.concatenate(rows + [jnp.zeros((2, rows[0].shape[1]), F32)], axis=0)
        self.sum_start(0, 0, mm(rows.astype(LOW), self.placement(LOW, rows.shape[1])))
        self.pair_merge()
        self.inputs = self.captions[...].astype(F32)
        self.queries = [(self.QA, self.s_query)]
        self.numbers = [(self.NUM, self.NUMR, self.s_num), (self.ST, self.STR, self.s_st)]
        self.grads = [(self.GA, self.s_g), (self.DL, self.s_dl)]
        self.back = [(self.NUM, self.NUMR, self.s_dq)]

    def do_up0(self):
        self.start(self.up_copies(), "up")

    def do_vec(self, stage):
        self.sum_start(0, stage, self.sum_end(0, stage - 1))

    def do_g0(self):
        self.keep_wide(self.G4, self.out_grad[...], self.s_g4)

    def do_g1(self):
        self.wide_across(self.G4, self.s_g4)

    def do_mem(self, which):
        if "images" not in self.here:
            self.here.add("images")
            self.image_copy(False).wait()
        self.done(CK + which)
        self.memory_forward(which)

    def do_a1(self):
        vectors = self.sum_end(0, 3)
        self.gains = [vectors[i : i + 1] for i in (0, 2, 4)]
        self.shifts = [vectors[i : i + 1] for i in (1, 3, 5)]
        self.rstds = [None] * 3
        self.a1 = self.normed(0, self.inputs)
        self.keep_left(0, self.a1)

    def normed(self, which, value):
        hat, self.rstds[which], out = norm(value, self.gains[which], self.shifts[which])
        self.HAT[which] = hat
        return out.astype(LOW)

    def pulled(self, which, grad):
        return norm_pull(grad, self.HAT[which], self.rstds[which], self.gains[which])

    def do_qkv(self, which):
        self.done(which)
        self.QKV[which] = mm(self.a1, self.weight(which)).astype(LOW)

    def do_sa(self):
        self.mixed = self.self_attention()
        self.keep_left(1, self.mixed)

    def do_r1(self):
        self.done(SO)
        self.r1 = self.inputs + mm(self.mixed, self.weight(SO))
        self.a2 = self.normed(1, self.r1)
        self.keep_left(2, self.a2)

    def do_cq(self):
        self.done(CQ)
        query = mm(self.a2, self.weight(CQ)).astype(LOW)
        self.QA[self.captions_of(self.nar)] = query.reshape(self.count, 64, self.width)
        self.share_start(self.queries)

    def do_q1(self):
        self.share_pass(self.queries)

    def do_cf(self, far):
        far = far * self.N // 2
        self.share_wait(self.queries, far)
        self.captions_loop(far, self.cross_forward)
        self.merge_start(self.numbers, "numbers", far)

    def do_m1(self):
        self.merge_far(self.numbers, self.join_softmax, "numbers")

    def do_m2(self):
        self.merge_own(self.numbers, self.join_softmax, "numbers", (1,))

    def do_a3(self):
        steps = [2**i for i in range(1, self.N.bit_length() - 1)]
        self.merge_own(self.numbers, self.join_softmax, "numbers", steps)
        full = self.attended()
        self.OCF[...] = full
        oc = full.astype(LOW)
        self.keep_left(3, oc)
        self.done(CO)
        self.r2 = self.r1 + mm(oc, self.weight(CO))
        self.keep_wide(self.A3, self.normed(2, self.r2), self.s_a3)

    def do_x1(self):
        self.wide_across(self.A3, self.s_a3)

    def do_hp(self):
        self.done(UP)
        a3 = self.A3[self.c].reshape(2 * self.tokens, self.width)
        for j in range(2):
            hidden = mm(a3, self.weight(UP + j))
            square = hidden * hidden
            tanh = jnp.tanh(GELU_A * hidden * (1.0 + GELU_B * square))
            act = (0.5 * hidden * (1.0 + tanh)).astype(LOW)
            self.SLOPE[j] = 0.5 * (1.0 + tanh) + 0.5 * hidden * (1.0 - tanh * tanh) * (
                GELU_A * (1.0 + 3.0 * GELU_B * square)
            )
            self.U[j, self.c] = act.reshape(2, self.tokens, self.width)
            self.start([self.hidden_copy(self.U, j, self.s_u)])

    def do_dg(self):
        self.wide_arrived(self.G4, self.s_g4)
        for j in range(2):
            self.hidden_copy(self.U, j, self.s_u).wait_recv()
        self.down_grad()

    def do_e3(self):
        self.done(DOWN)
        self.done(DOWN + 1)
        grad = self.G4[self.c].reshape(2 * self.tokens, self.width)
        e3 = 0.0
        for j in range(2):
            down = [self.HD[i, 2 * j : 2 * j + 2].reshape(self.width, 384) for i in range(2)]
            back = mm_bt(grad[:, :384], down[0]) + mm_bt(grad[:, 384:], down[1])
            dhp = (back * self.SLOPE[j]).astype(LOW)
            self.DH[j, self.c] = dhp.reshape(2, self.tokens, self.width)
            self.start([self.hidden_copy(self.DH, j, self.s_dh)])
            e3 = e3 + mm_bt(dhp, self.weight(UP + j))
        self.e3, other = self.both_halves(e3)
        self.FS[0] = other.astype(LOW)
        self.start([self.fold_copy(0)])

    def do_out(self):
        out = [0.0, 0.0]
        for j in range(2):
            act = self.U[j, self.c].reshape(2 * self.tokens, self.width)
            for i in range(2):
                down = self.HD[i, 2 * j : 2 * j + 2].reshape(self.width, 384)
                out[i] = out[i] + mm(act, down)
        own, other = self.both_halves(jnp.concatenate(out, axis=1))
        self.out = self.r2 + own
        self.FS[1] = other.astype(LOW)
        self.start([self.fold_copy(1)])

    def do_lo(self):
        self.fold_copy(1).wait_recv()
        self.layer_out[...] = (self.out + self.FR[1].astype(F32)).astype(LOW)

    def do_ug(self):
        self.wide_arrived(self.A3, self.s_a3)
        for j in range(2):
            self.hidden_copy(self.DH, j, self.s_dh).wait_recv()
        self.up_grad()

    def do_dr2(self):
        self.fold_copy(0).wait_recv()
        back, *self.vec3 = self.pulled(2, self.e3 + self.FR[0].astype(F32))
        self.dr2 = self.out_grad[...].astype(F32) + back
        dcat = self.dr2.astype(LOW)
        self.keep_right(5, dcat)
        self.spread_grad(mm_bt(dcat, self.weight(CO)))
        self.share_start(self.grads)

    def do_p1(self):
        self.share_pass(self.grads)

    def do_cb(self, far):
        far = far * self.N // 2
        self.share_wait(self.grads, far)
        self.sent("numbers")
        self.captions_loop(far, self.cross_backward)
        self.merge_start(self.back, "back", far)

    def do_n1(self):
        self.merge_far(self.back, self.join_sum, "back")

    def do_n2(self):
        self.merge_own(self.back, self.join_sum, "back", (1,))

    def do_dq(self):
        steps = [2**i for i in range(1, self.N.bit_length() - 1)]
        self.merge_own(self.back, self.join_sum, "back", steps)
        dqc = self.NUM[self.captions_of(self.nar)].reshape(self.tokens, self.width)
        self.keep_right(4, dqc)
        back, *self.vec2 = self.pulled(1, mm_bt(dqc, self.weight(CQ)))
        self.dr1 = self.dr2 + back
        dattn = self.dr1.astype(LOW)
        self.keep_right(3, dattn)
        self.dos = mm_bt(dattn, self.weight(SO)).astype(LOW)

    def do_mo(self, which):
        self.memory_grad_other(which)

    def do_mw(self, which):
        self.memory_grad_own(which)

    def do_wg(self, unit):
        self.weight_grad(unit)

    def do_sb(self):
        e1 = 0.0
        for j, item in enumerate(self.self_attention_back(self.dos)):
            self.keep_right(j, item)
            e1 = e1 + mm_bt(item, self.weight(j))
        back, *vec = self.pulled(0, e1)
        self.input_grad[...] = (self.dr1 + back).astype(LOW)
        vec = vec + self.vec2 + self.vec3 + [jnp.zeros((2, self.width), F32)]
        self.sum_start(1, 0, jnp.concatenate(vec, axis=0))

    def do_sum(self, stage):
        self.sum_start(1, stage, self.sum_end(1, stage - 1))

    def do_img(self):
        @pl.loop(0, 3)
        def _(t):
            size = self.images.shape[0] // 3
            rows = pl.ds(pl.multiple_of(size * t, 16), size)
            part = mm_bt(self.KV[0, rows], self.weight(CK))
            part = part + mm_bt(self.KV[1, rows], self.weight(CV))
            self.IMG[rows] = part.astype(LOW)

        self.image_copy(True).start()

    def do_end(self):
        self.vec_grad[...] = lax.dot_general(
            self.sum_end(1, 3),
            self.placement(F32, 128),
            (((1,), (1,)), ((), ())),
            precision=lax.Precision.HIGHEST,
            preferred_element_type=F32,
        )
        for unit in range(UNITS):
            self.rs_done(unit)
        self.image_copy(True).wait()
        for group in list(self.started):
            self.sent(group)

    def run(self):
        steps = {
            Step.begin: self.do_begin,
            Step.up0: self.do_up0,
            Step.vec: self.do_vec,
            Step.g0: self.do_g0,
            Step.g1: self.do_g1,
            Step.mem: self.do_mem,
            Step.a1: self.do_a1,
            Step.qkv: self.do_qkv,
            Step.sa: self.do_sa,
            Step.r1: self.do_r1,
            Step.cq: self.do_cq,
            Step.q1: self.do_q1,
            Step.cf: self.do_cf,
            Step.m1: self.do_m1,
            Step.m2: self.do_m2,
            Step.a3: self.do_a3,
            Step.x1: self.do_x1,
            Step.hp: self.do_hp,
            Step.dg: self.do_dg,
            Step.e3: self.do_e3,
            Step.out: self.do_out,
            Step.lo: self.do_lo,
            Step.ug: self.do_ug,
            Step.dr2: self.do_dr2,
            Step.p1: self.do_p1,
            Step.cb: self.do_cb,
            Step.n1: self.do_n1,
            Step.n2: self.do_n2,
            Step.dq: self.do_dq,
            Step.mo: self.do_mo,
            Step.mw: self.do_mw,
            Step.wg: self.do_wg,
            Step.sb: self.do_sb,
            Step.sum: self.do_sum,
            Step.img: self.do_img,
            Step.end: self.do_end,
            Step.F: self.first,
            Step.S: self.second,
            Step.TA: lambda unit: self.third(unit, 0),
            Step.TB: lambda unit: self.third(unit, 1),
            Step.H: self.hand,
            Step.R1: self.rs_one,
            Step.RA: self.rs_two,
            Step.RB: lambda unit: self.rs_two(unit, 1),
            Step.R3: self.rs_three,
            Step.R4: self.rs_four,
            Step.RU: lambda unit: self.rs_up(),
        }
        for step, *place in ORDER:
            steps[step](*place)


def layer_call(lanes, narrow, captions, images, lengths, out_grad, *params):
    tokens, width = captions.shape
    count = tokens // 64
    groups = narrow * count
    image_rows = images.shape[0]
    pairs = width // 128
    ins = ["captions", "images", "lengths", "out_grad", "self_proj", "self_output"]
    ins += ["cross_query", "cross_memory", "cross_output", "hidden_up", "hidden_down", *VECTORS]
    outs = {
        "layer_out": ((tokens, width), LOW),
        "input_grad": ((tokens, width), LOW),
        "image_grad": ((image_rows, width), LOW),
        "block_grad": ((24, 12 * width), F32),
        "down_out": ((96, width), F32),
        "vec_grad": ((8, 128), F32),
    }
    memory = {
        "W": ((10, 4, 2, 2, 48, width), LOW),
        "HD": ((2, 4, 2, 192, 384), LOW),
        "HG": ((4, 2, 192, 384), LOW),
        "UPS": ((48, width), LOW),
        "UPR": ((48, width), LOW),
        "PA": ((2, 24 * UP, 384), LOW),
        "PB": ((2, 48, width), LOW),
        "IMG": ((image_rows, width), LOW),
        "KV": ((2, image_rows, width), LOW),
        "E": ((groups, pairs // 2, image_rows // groups, 256), LOW),
        "LHS": ((4, 2, tokens, width), LOW),
        "RHS": ((6, 2, tokens, width), LOW),
        "A3": ((2, 2, tokens, width), LOW),
        "G4": ((2, 2, tokens, width), LOW),
        "U": ((2, 2, 2, tokens, width), LOW),
        "DH": ((2, 2, 2, tokens, width), LOW),
        "FS": ((2, tokens, width), LOW),
        "FR": ((2, tokens, width), LOW),
        "R1": ((UP, 4, 2, 48, 384), LOW),
        "R2": ((UP, 4, 48, 384), LOW),
        "R3": ((UP, 3, 48, 384), LOW),
        "RU1": ((4, 2, 48, width), LOW),
        "RU3": ((3, 2, 48, width), LOW),
        "RH1": ((4, 96, 384), LOW),
        "RH3": ((3, 96, 384), LOW),
        "RL1": ((96, 384), LOW),
        "RL3": ((3, 2, 96, 384), LOW),
        "CM": ((2, 4, 2, 2, 48, 384), LOW),
        "CS": ((2, 4, 2, 2, 48, 384), LOW),
        "CP": ((2, 4, 2, 2, 48, 384), LOW),
        "SF": ((UP, 24, 384), F32),
        "SFU": ((2, 24, width), F32),
        "UPG": ((2, 24, 2 * width), F32),
        "SFH": ((96, 384), F32),
        "V": ((2, 4, 8, width), F32),
        "VR": ((2, 6, 8, width), F32),
        "QKV": ((3, tokens, width), LOW),
        "PS": ((HEADS // 2, 128, 256), F32),
        "HAT": ((3, tokens, width), F32),
        "SLOPE": ((2, 2 * tokens, width), F32),
        "OCF": ((tokens, width), F32),
        "QA": ((groups, 64, width), LOW),
        "NUM": ((groups, 64, width), LOW),
        "ST": ((groups, 16, 128), F32),
        "TOP": ((groups, 8, 128), F32),
        "NUMR": ((narrow - 1, count, 64, width), LOW),
        "STR": ((narrow - 1, count, 16, 128), F32),
        "SCT": ((count, 128, 128), F32),
        "GA": ((groups, 64, width), LOW),
        "DL": ((groups, 16, 128), F32),
    }
    signals = {
        "s_pair": (3,),
        "s_up": (2,),
        "s_z": (UNITS, 3),
        "s_two": (UP, 2),
        "s_three": (UNITS, 2),
        "s_hand": (UNITS,),
        "s_rs1": (UNITS, 2),
        "s_rs2": (UP, 2),
        "s_rs3": (UNITS, 3),
        "s_rs4": (UNITS,),
        "s_rs5": (2,),
        "s_vec": (2, 6),
        "s_left": (4,),
        "s_right": (6,),
        "s_a3": (3,),
        "s_g4": (3,),
        "s_u": (2,),
        "s_dh": (2,),
        "s_fold": (2,),
        "s_memory": (2,),
        "s_query": (narrow - 1,),
        "s_num": (narrow - 1,),
        "s_st": (narrow - 1,),
        "s_g": (narrow - 1,),
        "s_dl": (narrow - 1,),
        "s_dq": (narrow - 1,),
        "s_image": (1,),
    }
    scratch = [pltpu.VMEM(shape, kind) for shape, kind in memory.values()]
    for shape in signals.values():
        scratch += [pltpu.SemaphoreType.DMA(shape)] * 2

    def body(*refs):
        named = dict(zip(ins + list(outs) + list(memory), refs))
        rest = refs[len(named) :]
        for i, name in enumerate(signals):
            named[name] = (rest[2 * i], rest[2 * i + 1])
        Layer(named, lanes, narrow).run()

    vmem = pl.BlockSpec(memory_space=pltpu.VMEM)
    in_specs = [vmem] * len(ins)
    in_specs[1] = pl.BlockSpec(memory_space=pl.ANY)
    in_specs[2] = pl.BlockSpec(memory_space=pltpu.SMEM)
    out_specs = [vmem] * len(outs)
    out_specs[2] = pl.BlockSpec(memory_space=pl.ANY)
    return pl.pallas_call(
        body,
        out_shape=[jax.ShapeDtypeStruct(shape, kind) for shape, kind in outs.values()],
        in_specs=in_specs,
        out_specs=out_specs,
        scratch_shapes=scratch,
        compiler_params=pltpu.CompilerParams(
            collective_id=0, has_side_effects=True, vmem_limit_bytes=VMEM_LIMIT
        ),
        cost_estimate=pl.CostEstimate(
            flops=17 * 10**9, bytes_accessed=8 * 10**6, transcendentals=2 * 10**6
        ),
        name="layer",
    )(captions, images, lengths, out_grad, *params)


def deliver(ranges, arrays, block_grad, vec_grad, own):
    count = len(arrays)
    outs = [jax.ShapeDtypeStruct(item.shape, item.dtype) for item in arrays]
    outs += [jax.ShapeDtypeStruct((block_grad.shape[0], b - a), F32) for a, b in ranges]
    rows = [jax.ShapeDtypeStruct((1, own), F32)] * len(VECTORS)

    def body(*refs):
        ins, vec, rest = refs[: count + 1], refs[count + 1], refs[count + 2 :]
        found, rest = rest[: len(outs)], rest[len(outs) :]
        vectors, held, sems = rest[: len(rows)], rest[len(rows) : -1], rest[-1]
        into = [pltpu.make_async_copy(a, b, sems.at[i]) for i, (a, b) in enumerate(zip(ins, held))]
        views = [*held[:count], *[held[count].at[:, pl.ds(a, b - a)] for a, b in ranges]]
        back = [
            pltpu.make_async_copy(a, b, sems.at[count + 1 + i])
            for i, (a, b) in enumerate(zip(views, found))
        ]
        for item in into:
            item.start()
        for i, ref in enumerate(vectors):
            ref[...] = vec[i : i + 1, :own]
        for i, item in enumerate(into):
            item.wait()
            for out in back[i : i + 1] if i < count else back[count:]:
                out.start()
        for out in back:
            out.wait()

    vmem = pl.BlockSpec(memory_space=pltpu.VMEM)
    hold = [pltpu.VMEM(item.shape, item.dtype) for item in (*arrays, block_grad)]
    return pl.pallas_call(
        body,
        out_shape=outs + rows,
        in_specs=[pl.BlockSpec(memory_space=pl.ANY)] * (count + 1) + [vmem],
        out_specs=[pl.BlockSpec(memory_space=pl.ANY)] * len(outs) + [vmem] * len(rows),
        scratch_shapes=hold + [pltpu.SemaphoreType.DMA((count + 1 + len(outs),))],
        compiler_params=pltpu.CompilerParams(vmem_limit_bytes=VMEM_LIMIT),
        name="deliver",
    )(*arrays, block_grad, vec_grad)


def lane_gather(value, lanes, narrow, axis):
    if lanes == 1:
        return value
    assert lanes % narrow == 0
    value = lax.all_gather(value, "narrow", axis=axis, tiled=True)
    step = 1
    wide_count = lax.axis_size("wide")
    while step * narrow < lanes:
        swap = [(i, i ^ step) for i in range(wide_count)]
        other = lax.ppermute(value, "wide", swap)
        low = (lax.axis_index("wide") // step) % 2 == 0
        first = jnp.where(low, value, other)
        second = jnp.where(low, other, value)
        value = jnp.concatenate([first, second], axis=axis)
        step *= 2
    return value


def lane_scatter(value, lanes, narrow, axis):
    if lanes == 1:
        return value
    wide_count = lax.axis_size("wide")
    step = lanes // narrow
    while step > 1:
        step //= 2
        swap = [(i, i ^ step) for i in range(wide_count)]
        first, second = jnp.split(value, 2, axis=axis)
        low = (lax.axis_index("wide") // step) % 2 == 0
        other = lax.ppermute(jnp.where(low, second, first), "wide", swap)
        value = jnp.where(low, first, second) + other
    return lax.psum_scatter(value, "narrow", scatter_dimension=axis, tiled=True)


def per_device(captions, images, lengths, out_grad, *params):
    narrow = lax.axis_size("narrow")
    devices = lax.axis_size("wide") * narrow
    lanes = devices // NODES
    count, seq_len, width = captions.shape
    tokens = count * seq_len
    params = [lane_gather(item, lanes, narrow, 0) for item in params]
    out, input_grad, image_grad, block_grad, down_grad, vec_grad = layer_call(
        lanes,
        narrow,
        captions.reshape(tokens, width),
        images.reshape(-1, width),
        lengths,
        out_grad.reshape(tokens, width),
        *params[:7],
        *[item.reshape(1, -1) for item in params[7:]],
    )
    block_grad = lane_scatter(block_grad, lanes, narrow, 0)
    down_grad = lane_scatter(down_grad, lanes, narrow, 0)
    if lanes > 1:
        vec_grad = lane_scatter(vec_grad[:, : width // NODES], lanes, narrow, 1)

    ends = (QS, SO, CK, CQ, CO, UP, UP + 4)
    ranges = [(width * a, width * b) for a, b in zip(ends, ends[1:])]
    arrays = [out, input_grad, image_grad, down_grad]
    own = width // devices
    found = deliver(ranges, arrays, block_grad, vec_grad, own)
    out, input_grad, image_grad, down_grad = found[:4]
    joint, self_out, memory, query, cross, up = found[4:10]
    return (
        out.reshape(captions.shape),
        input_grad.reshape(captions.shape),
        image_grad.reshape(images.shape),
        joint,
        self_out,
        query,
        memory,
        cross,
        up,
        down_grad,
        *[item.reshape(-1) for item in found[10:]],
    )


def solution(mesh):
    both = ("wide", "narrow")
    rows = P(both, None)
    text = P(both, None, None)
    vector = P(both)
    image = P("wide", "narrow", None)
    in_specs = (text, image, vector, text) + (rows,) * 7 + (vector,) * 6
    out_specs = (text, text, image) + (rows,) * 7 + (vector,) * 6
    return jax.shard_map(
        per_device, mesh=mesh, in_specs=in_specs, out_specs=out_specs, check_vma=False
    )
```

time: 235 us -> 172 us (0.73)
  Pallas kernels: 220 us -> 170 us
  local copies, waits for them, and re-layouts: 13.6 us -> 0 us
    pallas_call x1, Pallas kernels: 220 us -> 166 us  [layer_call(): pl.pallas_call(body, out_shape=[jax.ShapeDtypeStruct(shape, kind) for sha...]
    slice x4 -> x0, local copies, waits for them, and re-layouts: 6.55 us -> none  [columns(): return block_grad[:, start * width:stop * width]]
    pallas_call x0 -> x1, Pallas kernels: none -> 4.62 us  [deliver(): pl.pallas_call(body, out_shape=outs + rows, in_specs=[pl.BlockSpec(memory...]
    unnamed x10 -> x0, local copies, waits for them, and re-layouts: 4.22 us -> none
where the time goes in v3:
time: 172 us; the launch traced here: 171 us
  Pallas kernels  170 us (99%)
    pallas_call x1, Pallas kernels, layer_call(): pl.pallas_call(body, out_shape=[jax.ShapeDtypeStruct(shape, kind) for sha...  166 us
    pallas_call x1, Pallas kernels, deliver(): pl.pallas_call(body, out_shape=outs + rows, in_specs=[pl.BlockSpec(memory...  4.62 us

profile of v3, /device:TPU:1, one launch (start us, length us, event | category | flops | bytes accessed | tf_op | source)
XLA Modules:
  0.0 171.3 jit_solution(13587569510739394692)
XLA Ops:
  0.7 165.9 %layer.1 = (bf16[128,768]{1,0:T(8,128)(2,1)}, bf16[128,768]{1,0:T(8,128)(2,1)}, bf16[1152,768]{1,0:T(8,128)(2,1)}, f32[24,9216]{1,0:T(8,128)}, f32[96,768]{1,0:T(8,128)}, /*index=5*/f32[8,128]{1,0:T(8,128)}) custom-call(bf16[128,768]{1,0:T(8,128)(2,1)} %bitcast.20, bf16[1152,768]{1,0:T(8,128)(2,1)} %bitcast.18, s32[2]{0:T(128)} %refs_2_.1, ...), custom_call_target="tpu_custom_call" | custom-call | flops 16999999488 | bytes 8000000 | tf_op jit(solution)/shard_map/layer/pallas_call | solution.py:1374
  166.5 4.6 %deliver.1 = (bf16[128,768]{1,0:T(8,128)(2,1)}, bf16[128,768]{1,0:T(8,128)(2,1)}, bf16[1152,768]{1,0:T(8,128)(2,1)}, f32[96,768]{1,0:T(8,128)}, f32[24,2304]{1,0...) custom-call(bf16[128,768]{1,0:T(8,128)(2,1)} %get-tuple-element.38.r, ...), custom_call_target="tpu_custom_call" | custom-call | tf_op jit(solution)/shard_map/deliver/pallas_call | solution.py:1419

commit v4 on v3

--- a/solution.py
+++ b/solution.py
@@ -82,29 +82,33 @@
 
 
 ORDER = [
-    (Step.begin,), (Step.F, 0), (Step.g0,), (Step.vec, 1), (Step.F, 1), (Step.vec, 2), (Step.F, 3),
-    (Step.up0,), (Step.S, 0), (Step.F, 2), (Step.F, 5), (Step.S, 1), (Step.TA, 0), (Step.S, 3),
-    (Step.TA, 1), (Step.TB, 1), (Step.F, 6), (Step.TB, 0), (Step.TA, 3), (Step.TB, 3),
-    (Step.vec, 3), (Step.g1,), (Step.S, 2), (Step.F, 4), (Step.H, 1), (Step.S, 6), (Step.S, 5),
-    (Step.F, 7), (Step.a1,), (Step.TA, 2), (Step.TB, 2), (Step.qkv, 1), (Step.F, 8), (Step.S, 4),
-    (Step.F, 10), (Step.TA, 6), (Step.TB, 6), (Step.H, 0), (Step.H, 2), (Step.S, 7), (Step.TB, 5),
-    (Step.TA, 5), (Step.qkv, 0), (Step.TB, 4), (Step.qkv, 2), (Step.H, 3), (Step.sa,), (Step.F, 9),
-    (Step.r1,), (Step.H, 6), (Step.TA, 4), (Step.H, 5), (Step.S, 10), (Step.S, 8), (Step.cq,),
-    (Step.TA, 7), (Step.H, 4), (Step.mem, 1), (Step.TB, 7), (Step.mem, 0), (Step.q1,),
-    (Step.cf, 1), (Step.m1,), (Step.S, 9), (Step.cf, 0), (Step.H, 7), (Step.m2,), (Step.a3,),
-    (Step.H, 8), (Step.H, 9), (Step.H, 10), (Step.x1,), (Step.hp,), (Step.e3,), (Step.dg,),
-    (Step.ug,), (Step.R1, 10), (Step.R1, 9), (Step.R1, 8), (Step.out,), (Step.dr2,), (Step.wg, 7),
-    (Step.cb, 0), (Step.R1, 7), (Step.p1,), (Step.cb, 1), (Step.n1,), (Step.mo, 0), (Step.mo, 1),
-    (Step.mw, 0), (Step.R1, 4), (Step.RA, 9), (Step.RA, 7), (Step.n2,), (Step.RA, 8), (Step.RB, 7),
-    (Step.mw, 1), (Step.R1, 5), (Step.dq,), (Step.sb,), (Step.wg, 3), (Step.R1, 3), (Step.wg, 0),
-    (Step.RA, 4), (Step.wg, 2), (Step.R1, 2), (Step.sum, 1), (Step.RA, 5), (Step.RB, 4),
-    (Step.wg, 6), (Step.img,), (Step.wg, 1), (Step.RB, 5), (Step.R1, 0), (Step.RA, 2),
-    (Step.R1, 1), (Step.R3, 7), (Step.R3, 4), (Step.RB, 3), (Step.sum, 2), (Step.RA, 3),
-    (Step.RB, 2), (Step.R3, 5), (Step.RA, 10), (Step.sum, 3), (Step.R1, 6), (Step.R3, 2),
-    (Step.RA, 0), (Step.RB, 0), (Step.R4, 9), (Step.R3, 3), (Step.R4, 8), (Step.RB, 1),
-    (Step.RA, 1), (Step.R3, 0), (Step.RA, 6), (Step.RU, 8), (Step.RB, 6), (Step.R4, 2),
-    (Step.R3, 1), (Step.R4, 4), (Step.R4, 7), (Step.R4, 5), (Step.lo,), (Step.R3, 6), (Step.R4, 3),
-    (Step.R4, 0), (Step.R4, 1), (Step.R4, 6), (Step.end,),
+    (Step.begin,), (Step.F, 1), (Step.up0,), (Step.vec, 1), (Step.g0,), (Step.F, 0), (Step.vec, 2),
+    (Step.F, 3), (Step.S, 1), (Step.F, 2), (Step.S, 0), (Step.F, 5), (Step.TA, 1), (Step.vec, 3),
+    (Step.S, 3), (Step.TA, 0), (Step.F, 6), (Step.TB, 0), (Step.S, 2), (Step.F, 4), (Step.TA, 3),
+    (Step.S, 5), (Step.TB, 1), (Step.F, 7), (Step.F, 8), (Step.S, 6), (Step.TB, 2), (Step.TA, 2),
+    (Step.S, 4), (Step.TA, 6), (Step.TB, 3), (Step.H, 1), (Step.a1,), (Step.qkv, 1), (Step.H, 0),
+    (Step.TB, 5), (Step.TA, 5), (Step.TA, 4), (Step.qkv, 0), (Step.F, 10), (Step.H, 2),
+    (Step.TB, 6), (Step.qkv, 2), (Step.sa,), (Step.TB, 4), (Step.H, 3), (Step.r1,), (Step.F, 9),
+    (Step.H, 6), (Step.S, 8), (Step.g1,), (Step.S, 7), (Step.H, 5), (Step.S, 10), (Step.cq,),
+    (Step.H, 4), (Step.mem, 1), (Step.mem, 0), (Step.cf, 0), (Step.q1, 0), (Step.cf, 3),
+    (Step.cf, 6), (Step.q1, 1), (Step.TA, 7), (Step.TB, 7), (Step.cf, 4), (Step.cf, 2),
+    (Step.cf, 7), (Step.m1, 0), (Step.cf, 5), (Step.H, 8), (Step.m2, 0), (Step.m1, 1), (Step.H, 7),
+    (Step.S, 9), (Step.cf, 1), (Step.a3, 0), (Step.m2, 1), (Step.a3, 1), (Step.H, 10),
+    (Step.x1, 0), (Step.H, 9), (Step.x1, 1), (Step.hp,), (Step.e3,), (Step.dg,), (Step.R1, 10),
+    (Step.R1, 9), (Step.ug,), (Step.dr2, 0), (Step.R1, 8), (Step.dr2, 1), (Step.cb, 0),
+    (Step.RA, 9), (Step.out,), (Step.cb, 3), (Step.p1, 0), (Step.wg, 7), (Step.cb, 1),
+    (Step.cb, 2), (Step.p1, 1), (Step.R1, 7), (Step.cb, 6), (Step.cb, 5), (Step.cb, 7),
+    (Step.n1, 1), (Step.cb, 4), (Step.n2, 1), (Step.mo, 0), (Step.n2, 0), (Step.n1, 0),
+    (Step.RB, 7), (Step.mo, 1), (Step.mw, 0), (Step.R1, 4), (Step.RA, 7), (Step.mw, 1),
+    (Step.R1, 5), (Step.RA, 8), (Step.dq,), (Step.sb,), (Step.wg, 3), (Step.R1, 3), (Step.wg, 1),
+    (Step.RB, 4), (Step.R3, 7), (Step.wg, 2), (Step.R1, 2), (Step.sum, 1), (Step.RA, 3),
+    (Step.RB, 5), (Step.wg, 0), (Step.RA, 5), (Step.R1, 0), (Step.RA, 4), (Step.RB, 2),
+    (Step.RA, 2), (Step.sum, 2), (Step.R3, 5), (Step.R1, 1), (Step.R4, 8), (Step.R3, 4),
+    (Step.RB, 0), (Step.RA, 10), (Step.wg, 6), (Step.RB, 3), (Step.sum, 3), (Step.R1, 6),
+    (Step.R4, 5), (Step.R3, 2), (Step.RA, 1), (Step.RA, 0), (Step.R4, 9), (Step.RB, 1),
+    (Step.R3, 3), (Step.R4, 2), (Step.R3, 0), (Step.RA, 6), (Step.RB, 6), (Step.R3, 1),
+    (Step.R4, 4), (Step.img,), (Step.R3, 6), (Step.R4, 3), (Step.R4, 1), (Step.R4, 7),
+    (Step.R4, 0), (Step.lo,), (Step.RU, 8), (Step.R4, 6), (Step.end,),
 ]
 
 
@@ -156,7 +160,7 @@
         self.count, self.seq = self.captions.shape[0] // 64, 64
         self.tokens, self.width = self.captions.shape
         self.groups = self.QA.shape[0]
-        self.image_rows = self.images.shape[0] // self.groups
+        self.image_rows = self.IMG.shape[0] // self.groups
         self.pairs = self.width // 128
         lane = lax.broadcasted_iota(jnp.int32, (1, 128), 1)
         self.low_lanes = (lane < 64).astype(F32).astype(LOW)
@@ -600,11 +604,17 @@
 
     def keep_left(self, place, value):
         self.LHS[place, self.c] = value
+        self.send_left(place)
+
+    def send_left(self, place):
         here = self.LHS.at[place, self.c]
         self.start([self.copy(here, here, self.s_left, place, self.sibling())])
 
     def keep_right(self, place, value):
         self.RHS[place, self.c] = value
+        self.send_right(place)
+
+    def send_right(self, place):
         here = self.RHS.at[place, self.c]
         self.start([self.copy(here, here, self.s_right, place, self.sibling())])
 
@@ -751,7 +761,7 @@
 
         @pl.loop(0, 3)
         def _(t):
-            size = self.images.shape[0] // 3
+            size = self.IMG.shape[0] // 3
             rows = pl.ds(pl.multiple_of(size * t, 16), size)
             self.KV[which, rows] = mm(self.IMG[rows], w).astype(LOW)
 
@@ -794,83 +804,81 @@
     def captions_of(self, owner):
         return pl.ds(owner * self.count, self.count)
 
+    def caption(self, bits, j):
+        return self.owner(bits) * self.count + j
+
     def partner(self, bit):
         return (self.wide, jnp.bitwise_xor(self.nar, bit))
 
     def owner(self, bits):
         return jnp.bitwise_xor(self.nar, bits)
 
-    def share_copies(self, ref, sems, bit, bits):
-        here = ref.at[self.captions_of(self.owner(bits))]
-        return self.copy(here, here, sems, (self.N + bits) // (2 * bit) - 1, self.partner(bit))
-
-    def share_steps(self):
+    def once(self, key, copies):
+        if key not in self.here:
+            self.here.add(key)
+            self.arrived(copies())
+
+    def share_copies(self, refs, bit, bits, j):
+        where = ((self.N + bits) // (2 * bit) - 1) * self.count + j
+        place = self.caption(bits, j)
+        peer = self.partner(bit)
+        return [self.copy(ref.at[place], ref.at[place], sems, where, peer) for ref, sems in refs]
+
+    def share_start(self, refs, j):
         bit = self.N // 2
         while bit:
-            yield bit, range(0, self.N, 2 * bit)
+            self.start(self.share_copies(refs, bit, 0, j))
             bit //= 2
 
-    def share_start(self, refs):
-        for bit, held in self.share_steps():
-            self.start([self.share_copies(ref, sems, bit, 0) for ref, sems in refs])
-
-    def share_pass(self, refs):
-        for bit, held in self.share_steps():
-            for bits in held:
-                if bits:
-                    self.start([self.share_copies(ref, sems, bit, bits) for ref, sems in refs])
-            if bit > 1:
-                for bits in held:
-                    self.arrived([self.share_copies(ref, sems, bit, bits) for ref, sems in refs])
-
-    def share_wait(self, refs, far):
-        for bits in range(far, far + self.N // 2, 2):
-            self.arrived([self.share_copies(ref, sems, 1, bits) for ref, sems in refs])
-
-    def captions_loop(self, far, step):
-        @pl.loop(0, self.groups // 2)
-        def _(i):
-            bits = far + lax.div(i, self.count)
-            step(self.owner(bits) * self.count + lax.rem(i, self.count))
+    def share_wait(self, refs, bits, j):
+        if bits:
+            bit = bits & -bits
+            key = (refs is self.queries, bits, j)
+            self.once(key, lambda: self.share_copies(refs, bit, bits - bit, j))
+
+    def share_pass(self, refs, j):
+        bit = self.N // 2
+        while bit:
+            for bits in range(2 * bit, self.N, 2 * bit):
+                self.share_wait(refs, bits, j)
+                self.start(self.share_copies(refs, bit, bits, j))
+            bit //= 2
 
     def merge_slot(self, bit, bits):
         return self.N - self.N // bit + bits // (2 * bit)
 
-    def merge_copies(self, refs, bit, bits):
+    def merge_copies(self, refs, bit, bits, j):
         slot = self.merge_slot(bit, bits)
-        owner = self.captions_of(self.owner(bits + bit))
+        place = self.caption(bits + bit, j)
+        where = slot * self.count + j
+        peer = self.partner(bit)
         return [
-            self.copy(ref.at[owner], there.at[slot], sems, slot, self.partner(bit))
+            self.copy(ref.at[place], there.at[slot, j], sems, where, peer)
             for ref, there, sems in refs
         ]
 
-    def merge_steps(self):
+    def merge_start(self, refs, bits, j, group):
+        if bits % 2:
+            self.start(self.merge_copies(refs, 1, bits - 1, j), group)
+
+    def merge_part(self, refs, join, bit, bits, j, group):
+        self.arrived(self.merge_copies(refs, bit, bits, j))
+        join(self.caption(bits, j), self.merge_slot(bit, bits), j)
+        if bits % (4 * bit):
+            self.start(self.merge_copies(refs, 2 * bit, bits - 2 * bit, j), group)
+
+    def merge_far(self, refs, join, j, group):
         bit = 1
         while bit < self.N:
-            yield bit, range(0, self.N, 2 * bit)
+            for bits in reversed(range(2 * bit, self.N, 2 * bit)):
+                self.merge_part(refs, join, bit, bits, j, group)
             bit *= 2
 
-    def merge_start(self, refs, group, far):
-        for bits in range(far, far + self.N // 2, 2):
-            self.start(self.merge_copies(refs, 1, bits), group)
-
-    def merge_part(self, refs, join, bit, bits, group):
-        self.arrived(self.merge_copies(refs, bit, bits))
-        for j in range(self.count):
-            join(self.owner(bits) * self.count + j, self.merge_slot(bit, bits), j)
-        if bits % (4 * bit):
-            self.start(self.merge_copies(refs, 2 * bit, bits - 2 * bit), group)
-
-    def merge_far(self, refs, join, group):
-        for bit, kept in self.merge_steps():
-            for bits in reversed(kept):
-                if bits:
-                    self.merge_part(refs, join, bit, bits, group)
-
-    def merge_own(self, refs, join, group, steps):
-        for bit, kept in self.merge_steps():
-            if bit in steps:
-                self.merge_part(refs, join, bit, 0, group)
+    def merge_own(self, refs, join, j, group, low, high):
+        bit = low
+        while bit < high:
+            self.merge_part(refs, join, bit, 0, j, group)
+            bit *= 2
 
     def column(self, turned, p):
         return jnp.where(self.is_first, turned[:64, p : p + 1], turned[64:, p : p + 1])
@@ -896,66 +904,75 @@
     def join_sum(self, place, slot, j):
         self.add_into(self.NUM.at[place], self.NUMR[slot, j])
 
-    def attended(self):
-        done = []
+    def attended(self, j):
+        place = self.nar * self.count + j
+        turned = self.turn(1.0 / self.ST[place, :8])
+        self.SCT[j] = turned
+        parts = []
+        for p in range(self.pairs):
+            at = slice(128 * p, 128 * p + 128)
+            parts.append(self.NUM[place, :, at].astype(F32) * self.column(turned, p))
+        return jnp.concatenate(parts, axis=1)
+
+    def spread_grad(self, j, doc):
+        lane = lax.broadcasted_iota(jnp.int32, (128, 128), 1)
+        place = self.nar * self.count + j
+        rows = self.rows_of(j)
+        turned = self.SCT[j]
+        inner = jnp.zeros((128, 128), F32)
+        for p in range(self.pairs):
+            at = slice(128 * p, 128 * p + 128)
+            part = doc[:, at] * self.column(turned, p)
+            self.GA[place, :, at] = part.astype(LOW)
+            prod = part * self.OCF[rows, at]
+            a = jnp.sum(jnp.where(self.is_first, prod, 0.0), axis=1, keepdims=True)
+            b = jnp.sum(jnp.where(self.is_first, 0.0, prod), axis=1, keepdims=True)
+            inner = jnp.where(lane == p, jnp.concatenate([a, b], axis=0), inner)
+        self.DL[place, :8] = -inner.T[:8]
+        self.DL[place, 8:] = self.ST[place, 8:]
+
+    def rows_of(self, j):
+        return slice(self.seq * j, self.seq * j + self.seq)
+
+    def wide_copy(self, ref, sems, i, j):
+        here = ref.at[self.c, 1 - self.x if i == 2 else self.x, self.rows_of(j)]
+        peer = self.x_peer() if i == 0 else self.sibling()
+        return self.copy(here, here, sems, i * self.count + j, peer)
+
+    def keep_wide(self, ref, value, sems, j):
+        ref[self.c, self.x, self.rows_of(j)] = value
+        self.start([self.wide_copy(ref, sems, i, j) for i in range(2)])
+
+    def wide_across(self, ref, sems, j):
+        self.arrived([self.wide_copy(ref, sems, 0, j)])
+        self.start([self.wide_copy(ref, sems, 2, j)])
+
+    def wide_arrived(self, ref, sems):
         for j in range(self.count):
-            place = self.nar * self.count + j
-            turned = self.turn(1.0 / self.ST[place, :8])
-            self.SCT[j] = turned
-            parts = []
-            for p in range(self.pairs):
-                at = slice(128 * p, 128 * p + 128)
-                parts.append(self.NUM[place, :, at].astype(F32) * self.column(turned, p))
-            done.append(jnp.concatenate(parts, axis=1))
-        return jnp.concatenate(done, axis=0)
-
-    def spread_grad(self, doc):
-        lane = lax.broadcasted_iota(jnp.int32, (128, 128), 1)
-        for j in range(self.count):
-            place = self.nar * self.count + j
-            rows = slice(64 * j, 64 * j + 64)
-            turned = self.SCT[j]
-            inner = jnp.zeros((128, 128), F32)
-            for p in range(self.pairs):
-                at = slice(128 * p, 128 * p + 128)
-                part = doc[rows, at] * self.column(turned, p)
-                self.GA[place, :, at] = part.astype(LOW)
-                prod = part * self.OCF[rows, at]
-                a = jnp.sum(jnp.where(self.is_first, prod, 0.0), axis=1, keepdims=True)
-                b = jnp.sum(jnp.where(self.is_first, 0.0, prod), axis=1, keepdims=True)
-                inner = jnp.where(lane == p, jnp.concatenate([a, b], axis=0), inner)
-            self.DL[place, :8] = -inner.T[:8]
-            self.DL[place, 8:] = self.ST[place, 8:]
-
-    def weight_images(self):
-        return pltpu.make_async_copy(self.images, self.IMG, self.s_image[0].at[0])
-
-    def keep_wide(self, ref, value, sems):
-        ref[self.c, self.x] = value
-        here = ref.at[self.c, self.x]
-        self.start([self.copy(here, here, sems, 0, self.x_peer())])
-        self.start([self.copy(here, here, sems, 1, self.sibling())])
-
-    def wide_across(self, ref, sems):
-        here = ref.at[self.c, self.x]
-        self.copy(here, here, sems, 0, self.x_peer()).wait_recv()
-        here = ref.at[self.c, 1 - self.x]
-        self.start([self.copy(here, here, sems, 2, self.sibling())])
-
-    def wide_arrived(self, ref, sems):
-        for i in (1, 2):
-            here = ref.at[self.c, self.x]
-            self.copy(here, here, sems, i, self.sibling()).wait_recv()
+            self.arrived([self.wide_copy(ref, sems, i, j) for i in (1, 2)])
 
     def hidden_copy(self, ref, j, sems):
         here = ref.at[j, self.c]
         return self.copy(here, here, sems, j, self.sibling())
 
-    def fold_copy(self, which):
-        return self.copy(self.FS.at[which], self.FR.at[which], self.s_fold, which, self.x_peer())
+    def fold_copy(self, which, j):
+        at = (which, self.rows_of(j))
+        where = which * self.count + j
+        return self.copy(self.FS.at[at], self.FR.at[at], self.s_fold, where, self.x_peer())
+
+    def fold_start(self, which):
+        self.start([self.fold_copy(which, j) for j in range(self.count)])
+
+    def inward(self, name):
+        sem = self.s_in[0].at[self.ins.index(name)]
+        return pltpu.make_async_copy(self.outer[name], getattr(self, name), sem)
+
+    def outward(self, name):
+        sem = self.s_out[0].at[self.outs.index(name)]
+        return pltpu.make_async_copy(getattr(self, name), self.outer[name], sem)
 
     def image_copy(self, back):
-        src, dst = (self.IMG, self.image_grad) if back else (self.images, self.IMG)
+        src, dst = (self.IMG, self.outer["image_grad"]) if back else (self.outer["images"], self.IMG)
         return pltpu.make_async_copy(src, dst, self.s_image[0].at[0])
 
     def both_halves(self, value):
@@ -964,9 +981,14 @@
         return jnp.where(west, low, high), jnp.where(west, high, low)
 
     def do_begin(self):
+        ins = [self.inward(name) for name in self.ins]
+        for item in ins:
+            item.start()
         self.image_copy(False).start()
+        self.enter()
+        for item in ins:
+            item.wait()
         self.pair_pack()
-        self.enter()
         self.start(self.pair_copies())
         rows = [getattr(self, name)[...].astype(F32) for name in VECTORS]
         rows = jnp.concatenate(rows + [jnp.zeros((2, rows[0].shape[1]), F32)], axis=0)
@@ -985,10 +1007,12 @@
         self.sum_start(0, stage, self.sum_end(0, stage - 1))
 
     def do_g0(self):
-        self.keep_wide(self.G4, self.out_grad[...], self.s_g4)
+        for j in range(self.count):
+            self.keep_wide(self.G4, self.out_grad[self.rows_of(j)], self.s_g4, j)
 
     def do_g1(self):
-        self.wide_across(self.G4, self.s_g4)
+        for j in range(self.count):
+            self.wide_across(self.G4, self.s_g4, j)
 
     def do_mem(self, which):
         if "images" not in self.here:
@@ -1001,7 +1025,8 @@
         vectors = self.sum_end(0, 3)
         self.gains = [vectors[i : i + 1] for i in (0, 2, 4)]
         self.shifts = [vectors[i : i + 1] for i in (1, 3, 5)]
-        self.rstds = [None] * 3
+        self.rstds = [None, None, []]
+        self.r2 = []
         self.a1 = self.normed(0, self.inputs)
         self.keep_left(0, self.a1)
 
@@ -1031,36 +1056,43 @@
         self.done(CQ)
         query = mm(self.a2, self.weight(CQ)).astype(LOW)
         self.QA[self.captions_of(self.nar)] = query.reshape(self.count, 64, self.width)
-        self.share_start(self.queries)
-
-    def do_q1(self):
-        self.share_pass(self.queries)
-
-    def do_cf(self, far):
-        far = far * self.N // 2
-        self.share_wait(self.queries, far)
-        self.captions_loop(far, self.cross_forward)
-        self.merge_start(self.numbers, "numbers", far)
-
-    def do_m1(self):
-        self.merge_far(self.numbers, self.join_softmax, "numbers")
-
-    def do_m2(self):
-        self.merge_own(self.numbers, self.join_softmax, "numbers", (1,))
-
-    def do_a3(self):
-        steps = [2**i for i in range(1, self.N.bit_length() - 1)]
-        self.merge_own(self.numbers, self.join_softmax, "numbers", steps)
-        full = self.attended()
-        self.OCF[...] = full
+        for j in range(self.count):
+            self.share_start(self.queries, j)
+
+    def do_q1(self, j):
+        self.share_pass(self.queries, j)
+
+    def do_cf(self, item):
+        bits, j = divmod(item, self.count)
+        self.share_wait(self.queries, bits, j)
+        self.cross_forward(self.caption(bits, j))
+        self.merge_start(self.numbers, bits, j, "numbers")
+
+    def do_m1(self, j):
+        self.merge_far(self.numbers, self.join_softmax, j, "numbers")
+
+    def do_m2(self, j):
+        self.merge_own(self.numbers, self.join_softmax, j, "numbers", 1, 2)
+
+    def do_a3(self, j):
+        self.merge_own(self.numbers, self.join_softmax, j, "numbers", 2, self.N)
+        rows = self.rows_of(j)
+        full = self.attended(j)
+        self.OCF[rows] = full
         oc = full.astype(LOW)
-        self.keep_left(3, oc)
-        self.done(CO)
-        self.r2 = self.r1 + mm(oc, self.weight(CO))
-        self.keep_wide(self.A3, self.normed(2, self.r2), self.s_a3)
-
-    def do_x1(self):
-        self.wide_across(self.A3, self.s_a3)
+        self.LHS[3, self.c, rows] = oc
+        self.once("co", lambda: self.hand_copies(CO))
+        r2 = self.r1[rows] + mm(oc, self.weight(CO))
+        hat, rstd, out = norm(r2, self.gains[2], self.shifts[2])
+        self.HAT[2, rows] = hat
+        self.keep_wide(self.A3, out.astype(LOW), self.s_a3, j)
+        self.r2.append(r2)
+        self.rstds[2].append(rstd)
+        if j == self.count - 1:
+            self.send_left(3)
+
+    def do_x1(self, j):
+        self.wide_across(self.A3, self.s_a3, j)
 
     def do_hp(self):
         self.done(UP)
@@ -1094,9 +1126,10 @@
             self.DH[j, self.c] = dhp.reshape(2, self.tokens, self.width)
             self.start([self.hidden_copy(self.DH, j, self.s_dh)])
             e3 = e3 + mm_bt(dhp, self.weight(UP + j))
+        self.dr2 = []
         self.e3, other = self.both_halves(e3)
         self.FS[0] = other.astype(LOW)
-        self.start([self.fold_copy(0)])
+        self.fold_start(0)
 
     def do_out(self):
         out = [0.0, 0.0]
@@ -1106,13 +1139,14 @@
                 down = self.HD[i, 2 * j : 2 * j + 2].reshape(self.width, 384)
                 out[i] = out[i] + mm(act, down)
         own, other = self.both_halves(jnp.concatenate(out, axis=1))
-        self.out = self.r2 + own
+        self.out = jnp.concatenate(self.r2, axis=0) + own
         self.FS[1] = other.astype(LOW)
-        self.start([self.fold_copy(1)])
+        self.fold_start(1)
 
     def do_lo(self):
-        self.fold_copy(1).wait_recv()
+        self.arrived([self.fold_copy(1, j) for j in range(self.count)])
         self.layer_out[...] = (self.out + self.FR[1].astype(F32)).astype(LOW)
+        self.outward("layer_out").start()
 
     def do_ug(self):
         self.wide_arrived(self.A3, self.s_a3)
@@ -1120,38 +1154,44 @@
             self.hidden_copy(self.DH, j, self.s_dh).wait_recv()
         self.up_grad()
 
-    def do_dr2(self):
-        self.fold_copy(0).wait_recv()
-        back, *self.vec3 = self.pulled(2, self.e3 + self.FR[0].astype(F32))
-        self.dr2 = self.out_grad[...].astype(F32) + back
-        dcat = self.dr2.astype(LOW)
-        self.keep_right(5, dcat)
-        self.spread_grad(mm_bt(dcat, self.weight(CO)))
-        self.share_start(self.grads)
-
-    def do_p1(self):
-        self.share_pass(self.grads)
-
-    def do_cb(self, far):
-        far = far * self.N // 2
-        self.share_wait(self.grads, far)
+    def do_dr2(self, j):
+        self.arrived([self.fold_copy(0, j)])
+        rows = self.rows_of(j)
+        e3 = self.e3[rows] + self.FR[0, rows].astype(F32)
+        back, *vec = norm_pull(e3, self.HAT[2, rows], self.rstds[2][j], self.gains[2])
+        self.vec3 = [a + b for a, b in zip(self.vec3, vec)] if j else vec
+        dr2 = self.out_grad[rows].astype(F32) + back
+        self.dr2.append(dr2)
+        dcat = dr2.astype(LOW)
+        self.RHS[5, self.c, rows] = dcat
+        self.spread_grad(j, mm_bt(dcat, self.weight(CO)))
+        self.share_start(self.grads, j)
+        if j == self.count - 1:
+            self.send_right(5)
+
+    def do_p1(self, j):
+        self.share_pass(self.grads, j)
+
+    def do_cb(self, item):
+        bits, j = divmod(item, self.count)
+        self.share_wait(self.grads, bits, j)
         self.sent("numbers")
-        self.captions_loop(far, self.cross_backward)
-        self.merge_start(self.back, "back", far)
-
-    def do_n1(self):
-        self.merge_far(self.back, self.join_sum, "back")
-
-    def do_n2(self):
-        self.merge_own(self.back, self.join_sum, "back", (1,))
+        self.cross_backward(self.caption(bits, j))
+        self.merge_start(self.back, bits, j, "back")
+
+    def do_n1(self, j):
+        self.merge_far(self.back, self.join_sum, j, "back")
+
+    def do_n2(self, j):
+        self.merge_own(self.back, self.join_sum, j, "back", 1, 2)
 
     def do_dq(self):
-        steps = [2**i for i in range(1, self.N.bit_length() - 1)]
-        self.merge_own(self.back, self.join_sum, "back", steps)
+        for j in range(self.count):
+            self.merge_own(self.back, self.join_sum, j, "back", 2, self.N)
         dqc = self.NUM[self.captions_of(self.nar)].reshape(self.tokens, self.width)
         self.keep_right(4, dqc)
         back, *self.vec2 = self.pulled(1, mm_bt(dqc, self.weight(CQ)))
-        self.dr1 = self.dr2 + back
+        self.dr1 = jnp.concatenate(self.dr2, axis=0) + back
         dattn = self.dr1.astype(LOW)
         self.keep_right(3, dattn)
         self.dos = mm_bt(dattn, self.weight(SO)).astype(LOW)
@@ -1172,6 +1212,7 @@
             e1 = e1 + mm_bt(item, self.weight(j))
         back, *vec = self.pulled(0, e1)
         self.input_grad[...] = (self.dr1 + back).astype(LOW)
+        self.outward("input_grad").start()
         vec = vec + self.vec2 + self.vec3 + [jnp.zeros((2, self.width), F32)]
         self.sum_start(1, 0, jnp.concatenate(vec, axis=0))
 
@@ -1181,7 +1222,7 @@
     def do_img(self):
         @pl.loop(0, 3)
         def _(t):
-            size = self.images.shape[0] // 3
+            size = self.IMG.shape[0] // 3
             rows = pl.ds(pl.multiple_of(size * t, 16), size)
             part = mm_bt(self.KV[0, rows], self.weight(CK))
             part = part + mm_bt(self.KV[1, rows], self.weight(CV))
@@ -1197,9 +1238,14 @@
             precision=lax.Precision.HIGHEST,
             preferred_element_type=F32,
         )
+        self.outward("vec_grad").start()
         for unit in range(UNITS):
             self.rs_done(unit)
+        self.outward("block_grad").start()
+        self.outward("down_out").start()
         self.image_copy(True).wait()
+        for name in self.outs:
+            self.outward(name).wait()
         for group in list(self.started):
             self.sent(group)
 
@@ -1263,8 +1309,9 @@
     groups = narrow * count
     image_rows = images.shape[0]
     pairs = width // 128
-    ins = ["captions", "images", "lengths", "out_grad", "self_proj", "self_output"]
+    ins = ["captions", "out_grad", "self_proj", "self_output"]
     ins += ["cross_query", "cross_memory", "cross_output", "hidden_up", "hidden_down", *VECTORS]
+    given = dict(zip(ins, (captions, out_grad, *params)))
     outs = {
         "layer_out": ((tokens, width), LOW),
         "input_grad": ((tokens, width), LOW),
@@ -1273,7 +1320,10 @@
         "down_out": ((96, width), F32),
         "vec_grad": ((8, 128), F32),
     }
-    memory = {
+    results = [name for name in outs if name != "image_grad"]
+    memory = {name: (item.shape, item.dtype) for name, item in given.items()}
+    memory |= {name: outs[name] for name in results}
+    memory |= {
         "W": ((10, 4, 2, 2, 48, width), LOW),
         "HD": ((2, 4, 2, 192, 384), LOW),
         "HG": ((4, 2, 192, 384), LOW),
@@ -1340,42 +1390,42 @@
         "s_vec": (2, 6),
         "s_left": (4,),
         "s_right": (6,),
-        "s_a3": (3,),
-        "s_g4": (3,),
+        "s_a3": (3 * count,),
+        "s_g4": (3 * count,),
         "s_u": (2,),
         "s_dh": (2,),
-        "s_fold": (2,),
+        "s_fold": (2 * count,),
         "s_memory": (2,),
-        "s_query": (narrow - 1,),
-        "s_num": (narrow - 1,),
-        "s_st": (narrow - 1,),
-        "s_g": (narrow - 1,),
-        "s_dl": (narrow - 1,),
-        "s_dq": (narrow - 1,),
+        "s_query": ((narrow - 1) * count,),
+        "s_num": ((narrow - 1) * count,),
+        "s_st": ((narrow - 1) * count,),
+        "s_g": ((narrow - 1) * count,),
+        "s_dl": ((narrow - 1) * count,),
+        "s_dq": ((narrow - 1) * count,),
         "s_image": (1,),
+        "s_in": (len(ins),),
+        "s_out": (len(results),),
     }
     scratch = [pltpu.VMEM(shape, kind) for shape, kind in memory.values()]
     for shape in signals.values():
         scratch += [pltpu.SemaphoreType.DMA(shape)] * 2
 
     def body(*refs):
-        named = dict(zip(ins + list(outs) + list(memory), refs))
-        rest = refs[len(named) :]
+        names = ["lengths", "images", *ins, *outs]
+        outer = dict(zip(names, refs))
+        named = dict(zip(memory, refs[len(names) :]))
+        rest = refs[len(names) + len(memory) :]
         for i, name in enumerate(signals):
             named[name] = (rest[2 * i], rest[2 * i + 1])
+        named |= {"outer": outer, "lengths": outer["lengths"], "ins": ins, "outs": results}
         Layer(named, lanes, narrow).run()
 
-    vmem = pl.BlockSpec(memory_space=pltpu.VMEM)
-    in_specs = [vmem] * len(ins)
-    in_specs[1] = pl.BlockSpec(memory_space=pl.ANY)
-    in_specs[2] = pl.BlockSpec(memory_space=pltpu.SMEM)
-    out_specs = [vmem] * len(outs)
-    out_specs[2] = pl.BlockSpec(memory_space=pl.ANY)
+    anywhere = pl.BlockSpec(memory_space=pl.ANY)
     return pl.pallas_call(
         body,
         out_shape=[jax.ShapeDtypeStruct(shape, kind) for shape, kind in outs.values()],
-        in_specs=in_specs,
-        out_specs=out_specs,
+        in_specs=[pl.BlockSpec(memory_space=pltpu.SMEM)] + [anywhere] * (len(ins) + 1),
+        out_specs=[anywhere] * len(outs),
         scratch_shapes=scratch,
         compiler_params=pltpu.CompilerParams(
             collective_id=0, has_side_effects=True, vmem_limit_bytes=VMEM_LIMIT
@@ -1384,47 +1434,54 @@
             flops=17 * 10**9, bytes_accessed=8 * 10**6, transcendentals=2 * 10**6
         ),
         name="layer",
-    )(captions, images, lengths, out_grad, *params)
+    )(lengths, images, *given.values())
 
 
 def deliver(ranges, arrays, block_grad, vec_grad, own):
     count = len(arrays)
-    outs = [jax.ShapeDtypeStruct(item.shape, item.dtype) for item in arrays]
+    ins = [vec_grad, block_grad, *arrays]
+    outs = [jax.ShapeDtypeStruct((1, own), F32)] * len(VECTORS)
     outs += [jax.ShapeDtypeStruct((block_grad.shape[0], b - a), F32) for a, b in ranges]
-    rows = [jax.ShapeDtypeStruct((1, own), F32)] * len(VECTORS)
+    outs += [jax.ShapeDtypeStruct(item.shape, item.dtype) for item in arrays]
 
     def body(*refs):
-        ins, vec, rest = refs[: count + 1], refs[count + 1], refs[count + 2 :]
-        found, rest = rest[: len(outs)], rest[len(outs) :]
-        vectors, held, sems = rest[: len(rows)], rest[len(rows) : -1], rest[-1]
-        into = [pltpu.make_async_copy(a, b, sems.at[i]) for i, (a, b) in enumerate(zip(ins, held))]
-        views = [*held[:count], *[held[count].at[:, pl.ds(a, b - a)] for a, b in ranges]]
+        given, found = refs[: len(ins)], refs[len(ins) : len(ins) + len(outs)]
+        rest = refs[len(ins) + len(outs) :]
+        held, rows, sems = rest[: len(ins)], rest[len(ins) : -1], rest[-1]
+        copies = zip(given, held)
+        into = [pltpu.make_async_copy(a, b, sems.at[i]) for i, (a, b) in enumerate(copies)]
+        for item in into:
+            item.start()
+        views = [*rows, *[held[1].at[:, pl.ds(a, b - a)] for a, b in ranges], *held[2:]]
         back = [
-            pltpu.make_async_copy(a, b, sems.at[count + 1 + i])
+            pltpu.make_async_copy(a, b, sems.at[len(ins) + i])
             for i, (a, b) in enumerate(zip(views, found))
         ]
-        for item in into:
+        into[0].wait()
+        for i, ref in enumerate(rows):
+            ref[...] = held[0][i : i + 1, :own]
+            back[i].start()
+        into[1].wait()
+        for item in back[len(rows) : len(rows) + len(ranges)]:
             item.start()
-        for i, ref in enumerate(vectors):
-            ref[...] = vec[i : i + 1, :own]
-        for i, item in enumerate(into):
+        for item, last in zip(into[2:], back[len(rows) + len(ranges) :]):
             item.wait()
-            for out in back[i : i + 1] if i < count else back[count:]:
-                out.start()
-        for out in back:
-            out.wait()
-
-    vmem = pl.BlockSpec(memory_space=pltpu.VMEM)
-    hold = [pltpu.VMEM(item.shape, item.dtype) for item in (*arrays, block_grad)]
+            last.start()
+        for item in back:
+            item.wait()
+
+    hold = [pltpu.VMEM(item.shape, item.dtype) for item in ins]
+    hold += [pltpu.VMEM((1, own), F32)] * len(VECTORS)
+    anywhere = pl.BlockSpec(memory_space=pl.ANY)
     return pl.pallas_call(
         body,
-        out_shape=outs + rows,
-        in_specs=[pl.BlockSpec(memory_space=pl.ANY)] * (count + 1) + [vmem],
-        out_specs=[pl.BlockSpec(memory_space=pl.ANY)] * len(outs) + [vmem] * len(rows),
-        scratch_shapes=hold + [pltpu.SemaphoreType.DMA((count + 1 + len(outs),))],
+        out_shape=outs,
+        in_specs=[anywhere] * len(ins),
+        out_specs=[anywhere] * len(outs),
+        scratch_shapes=hold + [pltpu.SemaphoreType.DMA((len(ins) + len(outs),))],
         compiler_params=pltpu.CompilerParams(vmem_limit_bytes=VMEM_LIMIT),
         name="deliver",
-    )(*arrays, block_grad, vec_grad)
+    )(*ins)
 
 
 def lane_gather(value, lanes, narrow, axis):
@@ -1487,8 +1544,9 @@
     arrays = [out, input_grad, image_grad, down_grad]
     own = width // devices
     found = deliver(ranges, arrays, block_grad, vec_grad, own)
-    out, input_grad, image_grad, down_grad = found[:4]
-    joint, self_out, memory, query, cross, up = found[4:10]
+    vectors, found = found[: len(VECTORS)], found[len(VECTORS) :]
+    joint, self_out, memory, query, cross, up = found[:6]
+    out, input_grad, image_grad, down_grad = found[6:]
     return (
         out.reshape(captions.shape),
         input_grad.reshape(captions.shape),
@@ -1500,7 +1558,7 @@
         cross,
         up,
         down_grad,
-        *[item.reshape(-1) for item in found[10:]],
+        *[item.reshape(-1) for item in vectors],
     )
 
 

time: 172 us -> 167 us (0.971)
  Pallas kernels: 170 us -> 166 us
    pallas_call x1, Pallas kernels: 166 us -> 163 us  [layer_call(): pl.pallas_call(body, out_shape=[jax.ShapeDtypeStruct(shape, kind) for sha...]
where the time goes in v4:
time: 167 us
  Pallas kernels  166 us (99%)
    pallas_call x1, Pallas kernels, layer_call(): pl.pallas_call(body, out_shape=[jax.ShapeDtypeStruct(shape, kind) for sha...  163 us
    pallas_call x1, Pallas kernels, deliver(): pl.pallas_call(body, out_shape=outs, in_specs=[anywhere] * len(ins), out_...  3.38 us

profile of v4, /device:TPU:1, one launch (start us, length us, event | category | flops | bytes accessed | tf_op | source)
XLA Modules:
  0.0 166.8 jit_solution(9132694409313749837)
XLA Ops:
  0.7 162.6 %layer.1 = (bf16[128,768]{1,0:T(8,128)(2,1)}, bf16[128,768]{1,0:T(8,128)(2,1)}, bf16[1152,768]{1,0:T(8,128)(2,1)}, f32[24,9216]{1,0:T(8,128)}, f32[96,768]{1,0:T(8,128)}, /*index=5*/f32[8,128]{1,0:T(8,128)}) custom-call(s32[2]{0:T(128)} %refs_0_.1, bf16[1152,768]{1,0:T(8,128)(2,1)} %bitcast.18, bf16[128,768]{1,0:T(8,128)(2,1)} %bitcast.20, ...), custom_call_target="tpu_custom_call" | custom-call | flops 16999999488 | bytes 8000000 | tf_op jit(solution)/shard_map/layer/pallas_call | solution.py:1424
  163.3 3.4 %deliver.1 = (f32[1,24]{1,0:T(1,128)}, f32[1,24]{1,0:T(1,128)}, f32[1,24]{1,0:T(1,128)}, f32[1,24]{1,0:T(1,128)}, f32[1,24]{1,0:T(1,128)}, /*index=5*/f32[1,24]{...) custom-call(f32[8,128]{1,0:T(8,128)} %get-tuple-element.38.refs_0_, ...), custom_call_target="tpu_custom_call" | custom-call | tf_op jit(solution)/shard_map/deliver/pallas_call | solution.py:1476

commit v5 on v4

--- a/solution.py
+++ b/solution.py
@@ -963,10 +963,6 @@
     def fold_start(self, which):
         self.start([self.fold_copy(which, j) for j in range(self.count)])
 
-    def inward(self, name):
-        sem = self.s_in[0].at[self.ins.index(name)]
-        return pltpu.make_async_copy(self.outer[name], getattr(self, name), sem)
-
     def outward(self, name):
         sem = self.s_out[0].at[self.outs.index(name)]
         return pltpu.make_async_copy(getattr(self, name), self.outer[name], sem)
@@ -981,14 +977,9 @@
         return jnp.where(west, low, high), jnp.where(west, high, low)
 
     def do_begin(self):
-        ins = [self.inward(name) for name in self.ins]
-        for item in ins:
-            item.start()
         self.image_copy(False).start()
+        self.pair_pack()
         self.enter()
-        for item in ins:
-            item.wait()
-        self.pair_pack()
         self.start(self.pair_copies())
         rows = [getattr(self, name)[...].astype(F32) for name in VECTORS]
         rows = jnp.concatenate(rows + [jnp.zeros((2, rows[0].shape[1]), F32)], axis=0)
@@ -1321,8 +1312,7 @@
         "vec_grad": ((8, 128), F32),
     }
     results = [name for name in outs if name != "image_grad"]
-    memory = {name: (item.shape, item.dtype) for name, item in given.items()}
-    memory |= {name: outs[name] for name in results}
+    memory = {name: outs[name] for name in results}
     memory |= {
         "W": ((10, 4, 2, 2, 48, width), LOW),
         "HD": ((2, 4, 2, 192, 384), LOW),
@@ -1403,7 +1393,6 @@
         "s_dl": ((narrow - 1) * count,),
         "s_dq": ((narrow - 1) * count,),
         "s_image": (1,),
-        "s_in": (len(ins),),
         "s_out": (len(results),),
     }
     scratch = [pltpu.VMEM(shape, kind) for shape, kind in memory.values()]
@@ -1417,14 +1406,16 @@
         rest = refs[len(names) + len(memory) :]
         for i, name in enumerate(signals):
             named[name] = (rest[2 * i], rest[2 * i + 1])
-        named |= {"outer": outer, "lengths": outer["lengths"], "ins": ins, "outs": results}
+        named |= {name: outer[name] for name in ["lengths", *ins]}
+        named |= {"outer": outer, "outs": results}
         Layer(named, lanes, narrow).run()
 
     anywhere = pl.BlockSpec(memory_space=pl.ANY)
+    vmem = pl.BlockSpec(memory_space=pltpu.VMEM)
     return pl.pallas_call(
         body,
         out_shape=[jax.ShapeDtypeStruct(shape, kind) for shape, kind in outs.values()],
-        in_specs=[pl.BlockSpec(memory_space=pltpu.SMEM)] + [anywhere] * (len(ins) + 1),
+        in_specs=[pl.BlockSpec(memory_space=pltpu.SMEM), anywhere] + [vmem] * len(ins),
         out_specs=[anywhere] * len(outs),
         scratch_shapes=scratch,
         compiler_params=pltpu.CompilerParams(

time: 167 us -> 167 us (level)
  no operation moved by 1% of the time
where the time goes in v5:
time: 167 us
  Pallas kernels  166 us (99%)
    pallas_call x1, Pallas kernels, layer_call(): pl.pallas_call(body, out_shape=[jax.ShapeDtypeStruct(shape, kind) for sha...  163 us
    pallas_call x1, Pallas kernels, deliver(): pl.pallas_call(body, out_shape=outs, in_specs=[anywhere] * len(ins), out_...  3.38 us

profile of v5, /device:TPU:1, one launch (start us, length us, event | category | flops | bytes accessed | tf_op | source)
XLA Modules:
  0.0 167.3 jit_solution(6497758438069122728)
XLA Ops:
  0.7 163.0 %layer.1 = (bf16[128,768]{1,0:T(8,128)(2,1)}, bf16[128,768]{1,0:T(8,128)(2,1)}, bf16[1152,768]{1,0:T(8,128)(2,1)}, f32[24,9216]{1,0:T(8,128)}, f32[96,768]{1,0:T(8,128)}, /*index=5*/f32[8,128]{1,0:T(8,128)}) custom-call(s32[2]{0:T(128)} %refs_0_.1, bf16[1152,768]{1,0:T(8,128)(2,1)} %bitcast.18, bf16[128,768]{1,0:T(8,128)(2,1)} %bitcast.20, ...), custom_call_target="tpu_custom_call" | custom-call | flops 16999999488 | bytes 8000000 | tf_op jit(solution)/shard_map/layer/pallas_call | solution.py:1415
  163.7 3.4 %deliver.1 = (f32[1,24]{1,0:T(1,128)}, f32[1,24]{1,0:T(1,128)}, f32[1,24]{1,0:T(1,128)}, f32[1,24]{1,0:T(1,128)}, f32[1,24]{1,0:T(1,128)}, /*index=5*/f32[1,24]{...) custom-call(f32[8,128]{1,0:T(8,128)} %get-tuple-element.38.refs_0_, ...), custom_call_target="tpu_custom_call" | custom-call | tf_op jit(solution)/shard_map/deliver/pallas_call | solution.py:1467

commit v6 on v5

--- a/solution.py
+++ b/solution.py
@@ -106,8 +106,8 @@
     (Step.RA, 2), (Step.sum, 2), (Step.R3, 5), (Step.R1, 1), (Step.R4, 8), (Step.R3, 4),
     (Step.RB, 0), (Step.RA, 10), (Step.wg, 6), (Step.RB, 3), (Step.sum, 3), (Step.R1, 6),
     (Step.R4, 5), (Step.R3, 2), (Step.RA, 1), (Step.RA, 0), (Step.R4, 9), (Step.RB, 1),
-    (Step.R3, 3), (Step.R4, 2), (Step.R3, 0), (Step.RA, 6), (Step.RB, 6), (Step.R3, 1),
-    (Step.R4, 4), (Step.img,), (Step.R3, 6), (Step.R4, 3), (Step.R4, 1), (Step.R4, 7),
+    (Step.R3, 3), (Step.R4, 2), (Step.img,), (Step.R3, 0), (Step.RA, 6), (Step.RB, 6),
+    (Step.R3, 1), (Step.R4, 4), (Step.R3, 6), (Step.R4, 3), (Step.R4, 1), (Step.R4, 7),
     (Step.R4, 0), (Step.lo,), (Step.RU, 8), (Step.R4, 6), (Step.end,),
 ]
 
@@ -486,7 +486,7 @@
             return
         self.arrived([self.rs_one_copy(unit, half)])
 
-        @pl.loop(0, 4)
+        @pl.loop(0, 4, unroll=2)
         def _(z):
             if unit < UP:
                 y, x = ((self.y, every), (every, self.x))[half]
@@ -505,7 +505,7 @@
         halves = self.halves(unit, SCATTER)
         self.arrived([self.rs_two_copy(unit, half) for half in halves])
 
-        @pl.loop(0, 4)
+        @pl.loop(0, 4, unroll=2)
         def _(z):
             for half in halves:
                 more = self.R2[self.term(unit, half, z)]
@@ -1230,10 +1230,11 @@
             preferred_element_type=F32,
         )
         self.outward("vec_grad").start()
-        for unit in range(UNITS):
+        for unit in reversed(range(UNITS)):
             self.rs_done(unit)
+            if unit == DOWN:
+                self.outward("down_out").start()
         self.outward("block_grad").start()
-        self.outward("down_out").start()
         self.image_copy(True).wait()
         for name in self.outs:
             self.outward(name).wait()

time: 167 us -> 168 us (level)
  no operation moved by 1% of the time
where the time goes in v6:
time: 168 us
  Pallas kernels  167 us (99%)
    pallas_call x1, Pallas kernels, layer_call(): pl.pallas_call(body, out_shape=[jax.ShapeDtypeStruct(shape, kind) for sha...  164 us
    pallas_call x1, Pallas kernels, deliver(): pl.pallas_call(body, out_shape=outs, in_specs=[anywhere] * len(ins), out_...  3.38 us

profile of v6, /device:TPU:1, one launch (start us, length us, event | category | flops | bytes accessed | tf_op | source)
XLA Modules:
  0.0 167.9 jit_solution(15175264702226619934)
XLA Ops:
  0.7 163.7 %layer.1 = (bf16[128,768]{1,0:T(8,128)(2,1)}, bf16[128,768]{1,0:T(8,128)(2,1)}, bf16[1152,768]{1,0:T(8,128)(2,1)}, f32[24,9216]{1,0:T(8,128)}, f32[96,768]{1,0:T(8,128)}, /*index=5*/f32[8,128]{1,0:T(8,128)}) custom-call(s32[2]{0:T(128)} %refs_0_.1, bf16[1152,768]{1,0:T(8,128)(2,1)} %bitcast.18, bf16[128,768]{1,0:T(8,128)(2,1)} %bitcast.20, ...), custom_call_target="tpu_custom_call" | custom-call | flops 16999999488 | bytes 8000000 | tf_op jit(solution)/shard_map/layer/pallas_call | solution.py:1416
  164.3 3.4 %deliver.1 = (f32[1,24]{1,0:T(1,128)}, f32[1,24]{1,0:T(1,128)}, f32[1,24]{1,0:T(1,128)}, f32[1,24]{1,0:T(1,128)}, f32[1,24]{1,0:T(1,128)}, /*index=5*/f32[1,24]{...) custom-call(f32[8,128]{1,0:T(8,128)} %get-tuple-element.38.refs_0_, ...), custom_call_target="tpu_custom_call" | custom-call | tf_op jit(solution)/shard_map/deliver/pallas_call | solution.py:1468
